TPU v7x, 32 devices: a whole 2x2x4 slice. The times are simulated.
32 devices in a mesh: dom: 8 (over z, x), rep: 4 (over y, core).
Axes of the slice: x: 2, y: 2, z: 4, core: 2. Of those that a mesh axis runs over, the one named last changes fastest.
Arguments:
- features: bfloat16 [131072, 100], P(('dom', 'rep')), may hold values from -6 to 6
- labels: int32 [65536], P(('dom', 'rep')), may hold values from 0 to 46
- seed_rows: int32 [65536], P(('dom', 'rep')), may hold values from 0 to 4095
- seed_mask: int32 [65536], P(('dom', 'rep')), may hold values from 0 to 1
- send_rows: int32 [1024, 16], P(('dom', 'rep')), may hold values from 0 to 4095
- neighbors_one: int32 [131072, 15], P(('dom', 'rep')), may hold values from 0 to 4607, as said below
- neighbors_two: int32 [131072, 10], P(('dom', 'rep')), may hold values from 0 to 4607, as said below
- neighbors_three: int32 [131072, 5], P(('dom', 'rep')), may hold values from 0 to 4607, as said below
- weight_one: float32 [200, 256], replicated, may hold values from -0.625 to 0.625
- weight_two: float32 [512, 256], replicated, may hold values from -6 to 6
- weight_three: float32 [512, 47], replicated, may hold values from -12 to 12
- left_one: float32 [200, 200], replicated, as said below
- right_one: float32 [256, 256], replicated, as said below
- left_two: float32 [512, 512], replicated, as said below
- right_two: float32 [256, 256], replicated, as said below
- left_three: float32 [512, 512], replicated, as said below
- right_three: float32 [47, 47], replicated, as said below
- first_one: float32 [200, 256], replicated
- first_two: float32 [512, 256], replicated
- first_three: float32 [512, 47], replicated
- second_one: float32 [200, 256], replicated
- second_two: float32 [512, 256], replicated, may hold values from 1.5258789e-12 to 6.1035157e-12
- second_three: float32 [512, 47], replicated, may hold values from 1.5258789e-12 to 6.1035157e-12
- bias_all: float32 [559], replicated, may hold values from -0.6 to 0.6
- bias_first: float32 [559], replicated
- bias_second: float32 [559], replicated, may hold values from 1.5258789e-10 to 6.1035155e-10
Outputs:
- new_weight_one: float32 [200, 256], replicated
- new_first_one: float32 [200, 256], replicated
- new_second_one: float32 [200, 256], replicated
- new_weight_two: float32 [512, 256], replicated
- new_first_two: float32 [512, 256], replicated
- new_second_two: float32 [512, 256], replicated
- new_weight_three: float32 [512, 47], replicated
- new_first_three: float32 [512, 47], replicated
- new_second_three: float32 [512, 47], replicated
- new_bias: float32 [559], replicated
- new_bias_first: float32 [559], replicated
- new_bias_second: float32 [559], replicated
- loss_sum: float32 [], replicated
- seed_total: float32 [], replicated
Inputs may be any that keep to these rules, and one draw needn't show every extreme that they name: `neighbors_one`: entries below 4096 name the part's own nodes, the others its halo rows; column 0 of a part's lists names every halo row of that part at least once. `neighbors_two`: as for neighbors_one. `neighbors_three`: as for neighbors_one. `left_one`: Orthogonal. `right_one`: Orthogonal. `left_two`: Orthogonal. `right_two`: Orthogonal. `left_three`: Orthogonal. `right_three`: Orthogonal.
All inputs are finite; a program needn't handle non-finite values.
Results may differ from a plain program's by a relative error of at most 0.0085.
Values may be sent and summed in bfloat16 or wider, within the bound.
A program may use at most 256 MiB of HBM per device.

v0:
```python
import functools

import jax
import jax.numpy as jnp
from jax import lax
from jax.experimental import pallas as pl
from jax.experimental.pallas import tpu as pltpu
from jax.sharding import PartitionSpec as P

STEP = 10


beta_one = 0.9
beta_two = 0.999
epsilon = 1e-08
step_rates = (0.05, 0.5, 1.0)
bias_rate = 0.05
weight_decay = 0.01

axes = ("dom", "rep")
WORDS = 4
SLOTS = 8
GROUPS = WORDS * SLOTS
BLOCK = 512
VMEM_BYTES = 56 * 1024 * 1024
TRANS_LEFT = (((0,), (0,)), ((), ()))
TRANS_RIGHT = (((1,), (1,)), ((), ()))


def dot(left, right, dims=(((1,), (0,)), ((), ()))):
    return lax.dot_general(left, right, dims, preferred_element_type=jnp.float32)


def params(collective=None):
    remote = {} if collective is None else dict(collective_id=collective, has_side_effects=True)
    return pltpu.CompilerParams(
        dimension_semantics=("arbitrary",), vmem_limit_bytes=VMEM_BYTES, **remote
    )


def whole(shape):
    return pl.BlockSpec(shape, lambda i: (0,) * len(shape))


def lanes(rows, width):
    return pl.BlockSpec((rows, width), lambda i: (0, i))


def words_layer(near_ref, out_ref, place_ref, field_ref):
    fanout, block = near_ref.shape
    span = out_ref.shape[0] // WORDS
    near = near_ref[...]
    group = ((near.astype(jnp.float32) + 0.5) * (1.0 / span)).astype(jnp.int32)
    place = near - group * span
    word = group >> 3
    bit = jnp.left_shift(jnp.int32(1), (group & 7) * 4)
    parts = [jnp.where(word == k, bit, 0) for k in range(WORDS)]
    totals = [jnp.zeros_like(bit) for _ in range(WORDS)]
    for g in range(fanout):
        same = place == place[g : g + 1]
        for k in range(WORDS):
            totals[k] = totals[k] + jnp.where(same, parts[k][g : g + 1], 0)
    place_ref[:fanout, :] = place
    for k in range(WORDS):
        field_ref[k, :fanout, :] = totals[k]
    chunk = 48
    for tile in range(0, block, 128):
        cols = slice(tile, tile + 128)
        for start in range(0, span, chunk):
            rows = lax.broadcasted_iota(jnp.int32, (chunk, 128), 0) + start
            sums = [jnp.zeros((chunk, 128), jnp.int32) for _ in range(WORDS)]
            for g in range(fanout):
                hit = rows == place_ref[g : g + 1, cols]
                for k in range(WORDS):
                    sums[k] = jnp.where(hit, field_ref[k, g : g + 1, cols], sums[k])
            for k in range(WORDS):
                out_ref[k * span + start : k * span + start + chunk, cols] = sums[k]


def ring(mesh_sizes):
    across, along = mesh_sizes
    parts = across * along
    me = lax.axis_index(axes[0]) * along + lax.axis_index(axes[1])

    def peer(ahead):
        index = lax.rem(me + ahead, parts)
        return index, (index // along, lax.rem(index, along))

    return parts, me, peer


def greet(mesh_sizes):
    parts, _, peer = ring(mesh_sizes)
    barrier = pltpu.get_barrier_semaphore()

    def tell(ahead, carry):
        pl.semaphore_signal(
            barrier, inc=1, device_id=peer(ahead)[1], device_id_type=pl.DeviceIdType.MESH
        )
        return carry

    lax.fori_loop(1, parts, tell, 0)


def all_greeted(mesh_sizes):
    pl.semaphore_wait(pltpu.get_barrier_semaphore(), ring(mesh_sizes)[0] - 1)


def block_copy(mesh_sizes, out_ref, in_ref, send_sem, recv_sem, ahead):
    _, me, peer = ring(mesh_sizes)
    index, where = peer(ahead)
    return pltpu.make_async_remote_copy(
        src_ref=out_ref.at[index],
        dst_ref=in_ref.at[me],
        send_sem=send_sem.at[index],
        recv_sem=recv_sem.at[me],
        device_id=where,
        device_id_type=pl.DeviceIdType.MESH,
    )


def send_blocks(mesh_sizes, out_ref, in_ref, send_sem, recv_sem):
    parts = ring(mesh_sizes)[0]

    def send(ahead, carry):
        block_copy(mesh_sizes, out_ref, in_ref, send_sem, recv_sem, ahead).start()
        return carry

    lax.fori_loop(1, parts, send, 0)


def wait_blocks(mesh_sizes, out_ref, in_ref, send_sem, recv_sem):
    parts, me, peer = ring(mesh_sizes)

    def wait(ahead, carry):
        block_copy(mesh_sizes, out_ref, in_ref, send_sem, recv_sem, ahead).wait_send()
        index, where = peer(ahead)
        pltpu.make_async_remote_copy(
            src_ref=out_ref.at[index],
            dst_ref=in_ref.at[index],
            send_sem=send_sem.at[index],
            recv_sem=recv_sem.at[index],
            device_id=where,
            device_id_type=pl.DeviceIdType.MESH,
        ).wait_recv()
        return carry

    lax.fori_loop(1, parts, wait, 0)


def send_all(mesh_sizes, own_ref, in_ref, send_sem, recv_sem):
    parts, me, peer = ring(mesh_sizes)

    def send(ahead, carry):
        index, where = peer(ahead)
        pltpu.make_async_remote_copy(
            src_ref=own_ref,
            dst_ref=in_ref.at[me],
            send_sem=send_sem.at[index],
            recv_sem=recv_sem.at[me],
            device_id=where,
            device_id_type=pl.DeviceIdType.MESH,
        ).start()
        return carry

    lax.fori_loop(1, parts, send, 0)


def wait_all(mesh_sizes, own_ref, in_ref, send_sem, recv_sem):
    parts, _, peer = ring(mesh_sizes)

    def wait(ahead, carry):
        index, where = peer(ahead)
        copy = pltpu.make_async_remote_copy(
            src_ref=own_ref,
            dst_ref=in_ref.at[index],
            send_sem=send_sem.at[index],
            recv_sem=recv_sem.at[index],
            device_id=where,
            device_id_type=pl.DeviceIdType.MESH,
        )
        copy.wait_send()
        copy.wait_recv()
        return carry

    lax.fori_loop(1, parts, wait, 0)


def semaphores(parts):
    return [pltpu.SemaphoreType.DMA((parts,)), pltpu.SemaphoreType.DMA((parts,))]


def chosen_nodes(send_row, start, count):
    node = lax.broadcasted_iota(jnp.int32, (count, send_row.shape[1]), 0) + start
    return jnp.where(node == send_row, 1.0, 0.0).astype(jnp.bfloat16)


def words_kernel(mesh_sizes, kind, near_ref, *refs):
    refs = list(refs)
    if kind == "features":
        feats_ref, send_ref, out_ref, got_ref, sent_ref = refs[:5]
        refs = refs[5:]
    elif kind == "seeds":
        sent_ref, slots_ref, labels_ref, mask_ref, out_ref, got_ref, seeds_ref = refs[:7]
        refs = refs[7:]
    else:
        sent_ref, out_ref, got_ref = refs[:3]
        refs = refs[3:]
    place_ref, field_ref, land_ref, send_sem, recv_sem = refs
    step = pl.program_id(0)
    block = near_ref.shape[1]
    moves = (mesh_sizes, sent_ref, land_ref, send_sem, recv_sem)

    @pl.when(step == 0)
    def _():
        greet(mesh_sizes)

    if kind == "features":

        @pl.when(step == 0)
        def _():
            width, nodes = feats_ref.shape
            halo = send_ref.shape[1]
            total = jnp.zeros((width, halo), jnp.float32)
            for start in range(0, nodes, block):
                chosen = chosen_nodes(send_ref[...], start, block)
                total = total + dot(feats_ref[:, start : start + block], chosen)
            padded = sent_ref.shape[2]
            total = jnp.concatenate([total, jnp.zeros((padded - width, halo), jnp.float32)])
            sent_ref[...] = total.T.astype(jnp.bfloat16).reshape(sent_ref.shape)

    words_layer(near_ref, out_ref, place_ref, field_ref)

    @pl.when(step == 0)
    def _():
        all_greeted(mesh_sizes)
        send_blocks(*moves)

    if kind == "seeds":
        classes = seeds_ref.shape[0]
        slots = slots_ref.shape[1]
        label = lax.broadcasted_iota(jnp.int32, (classes, slots), 0)
        marked = jnp.where((label == labels_ref[...]) & (mask_ref[...] != 0), 1.0, 0.0)
        chosen = chosen_nodes(slots_ref[...], step * block, block)
        seeds_ref[...] = dot(marked.astype(jnp.bfloat16), chosen, TRANS_RIGHT)

    @pl.when(step == pl.num_programs(0) - 1)
    def _():
        me = ring(mesh_sizes)[1]
        wait_blocks(*moves)
        land_ref[me] = sent_ref[me]
        got_ref[...] = land_ref[...]


def count_words(near, mesh_sizes, collective, halo, sent=None, feats=None, send_row=None, seeds=None):
    fanout, nodes = near.shape
    parts = mesh_sizes[0] * mesh_sizes[1]
    height = (nodes + halo) // SLOTS
    in_specs = [lanes(fanout, BLOCK)]
    operands = [near]
    scratch = []
    if sent is None:
        kind = "features"
        blocks = (parts, halo // parts, -(-feats.shape[0] // 128) * 128)
        in_specs += [whole(feats.shape), whole(send_row.shape)]
        operands += [feats, send_row]
        scratch.append(pltpu.VMEM(blocks, jnp.bfloat16))
    else:
        kind = "plain"
        blocks = (parts, halo // parts, sent.shape[1])
        in_specs.append(whole(blocks))
        operands.append(sent.reshape(blocks))
    out_specs = [lanes(height, BLOCK), whole(blocks)]
    out_shape = [
        jax.ShapeDtypeStruct((height, nodes), jnp.int32),
        jax.ShapeDtypeStruct(blocks, jnp.bfloat16),
    ]
    if seeds is not None:
        kind = "seeds"
        classes, slots, labels, mask = seeds
        in_specs += [whole(slots.shape)] * 3
        operands += [slots, labels, mask]
        out_specs.append(lanes(classes, BLOCK))
        out_shape.append(jax.ShapeDtypeStruct((classes, nodes), jnp.float32))
    return pl.pallas_call(
        functools.partial(words_kernel, mesh_sizes, kind),
        grid=(nodes // BLOCK,),
        in_specs=in_specs,
        out_specs=out_specs,
        out_shape=out_shape,
        scratch_shapes=scratch
        + [
            pltpu.VMEM((16, BLOCK), jnp.int32),
            pltpu.VMEM((WORDS, 16, BLOCK), jnp.int32),
            pltpu.VMEM(blocks, jnp.bfloat16),
        ]
        + semaphores(parts),
        compiler_params=params(collective),
        name="count_words",
    )(*operands)


def field(words, slot):
    if slot == SLOTS - 1:
        picked = lax.shift_right_logical(words, 4 * slot)
    else:
        picked = words & (15 << (4 * slot))
    return picked.astype(jnp.float32).astype(jnp.bfloat16)


def slot_scale(slot):
    return 1.0 if slot == SLOTS - 1 else 2.0 ** (-4 * slot)


def spread_counts(words_ref, counts_ref, group, span):
    word, slot = divmod(group, SLOTS)
    width = words_ref.shape[1]
    for tile in range(0, width, 128):
        cols = slice(tile, tile + 128)
        for start in range(0, span, 48):
            counts_ref[group * span + start : group * span + start + 48, cols] = field(
                words_ref[word * span + start : word * span + start + 48, cols], slot
            )


def gather_product(table_ref, words_ref, counts_ref):
    table = table_ref.shape[1]
    span = table // GROUPS
    total = None
    done = 0
    step = 512
    for group in range(GROUPS):
        spread_counts(words_ref, counts_ref, group, span)
        ready = (group + 1) * span
        while ready - done >= step or (group == GROUPS - 1 and done < table):
            stop = min(done + step, table)
            term = dot(table_ref[:, done:stop], counts_ref[done:stop, :])
            total = term if total is None else total + term
            done = stop
    return total


def scale_row(table):
    column = lax.broadcasted_iota(jnp.int32, (1, table), 1)
    group = ((column.astype(jnp.float32) + 0.5) * (GROUPS / table)).astype(jnp.int32)
    slot = group & (SLOTS - 1)
    scale = jnp.ones((1, table), jnp.float32)
    for k in range(SLOTS - 1):
        scale = jnp.where(slot == k, slot_scale(k), scale)
    return scale


def column_of(row):
    return jnp.broadcast_to(row, (128, row.shape[1])).T


def late(rows, width):
    return pl.BlockSpec((rows, width), lambda i: (0, jnp.maximum(i - 1, 0)))


def now(rows, width, steps):
    return pl.BlockSpec((rows, width), lambda i: (0, jnp.minimum(i, steps - 1)))


def hidden_kernel(
    fanout,
    bias_start,
    words_ref,
    own_ref,
    own_block,
    got_ref,
    weight_ref,
    bias_ref,
    send_ref,
    state_ref,
    preact_ref,
    sent_ref,
    extra_ref,
    table_ref,
    counts_ref,
    picked_ref,
    mean_ref,
    self_ref,
    near_ref,
    bias_col,
):
    step = pl.program_id(0)
    last = pl.num_programs(0) - 1
    width, nodes = own_ref.shape
    units, block = state_ref.shape
    padded = mean_ref.shape[0]

    @pl.when(step == 0)
    def _():
        if table_ref.shape[0] > width:
            table_ref[...] = jnp.zeros_like(table_ref)
        got = got_ref[...].reshape(-1, got_ref.shape[2]).T[:width]
        scale = scale_row(table_ref.shape[1])
        own = own_ref[...].astype(jnp.float32) * scale[:, :nodes]
        table_ref[:width, :nodes] = own.astype(jnp.bfloat16)
        far = got.astype(jnp.float32) * scale[:, nodes:]
        table_ref[:width, nodes:] = far.astype(jnp.bfloat16)
        if width == units:
            extra_ref[:, :nodes] = own_ref[...]
            extra_ref[:, nodes:] = got
        mean_ref[...] = jnp.zeros_like(mean_ref)
        picked_ref[...] = jnp.zeros_like(picked_ref)
        self_ref[...] = weight_ref[:width, :].T.astype(jnp.bfloat16)
        if padded > width:
            near_ref[...] = jnp.zeros_like(near_ref)
        near_ref[:, :width] = weight_ref[width:, :].T.astype(jnp.bfloat16)
        bias_col[...] = column_of(bias_ref[:, bias_start : bias_start + units])

    def finish():
        mean = mean_ref[...]
        if width != units:
            extra_ref[...] = mean
        preact = dot(self_ref[...], own_block[...]) + dot(near_ref[...], mean) + bias_col[:, :1]
        preact_ref[...] = preact
        active = preact * jax.nn.sigmoid(preact)
        norm = lax.rsqrt(jnp.sum(active * active, axis=0, keepdims=True) + 1e-06)
        state = (active * norm).astype(jnp.bfloat16)
        state_ref[...] = state
        picked_ref[...] += dot(state, chosen_nodes(send_ref[...], (step - 1) * block, block))

    @pl.when(step < last)
    def _():
        finish()
        total = gather_product(table_ref, words_ref, counts_ref)
        mean_ref[...] = (total[:padded] / fanout).astype(jnp.bfloat16)

    @pl.when(step == last)
    def _():
        finish()
        sent_ref[...] = picked_ref[...].T.astype(jnp.bfloat16)


def hidden_layer(words, own, got, weight, bias_row, bias_start, send_row, fanout):
    width, nodes = own.shape
    halo = send_row.shape[1]
    table = nodes + halo
    units = weight.shape[1]
    padded = -(-width // 16) * 16
    tall = max(padded, 3 * units // 4)
    steps = nodes // BLOCK
    if width == units:
        extra_shape, extra_spec = (units, table), whole((units, table))
    else:
        extra_shape, extra_spec = (padded, nodes), late(padded, BLOCK)
    return pl.pallas_call(
        functools.partial(hidden_kernel, fanout, bias_start),
        grid=(steps + 1,),
        in_specs=[
            now(words.shape[0], BLOCK, steps),
            whole(own.shape),
            late(width, BLOCK),
            whole(got.shape),
            whole(weight.shape),
            whole(bias_row.shape),
            whole(send_row.shape),
        ],
        out_specs=[
            late(units, BLOCK),
            late(units, BLOCK),
            whole((halo, units)),
            extra_spec,
        ],
        out_shape=[
            jax.ShapeDtypeStruct((units, nodes), jnp.bfloat16),
            jax.ShapeDtypeStruct((units, nodes), jnp.float32),
            jax.ShapeDtypeStruct((halo, units), jnp.bfloat16),
            jax.ShapeDtypeStruct(extra_shape, jnp.bfloat16),
        ],
        scratch_shapes=[
            pltpu.VMEM((tall, table), jnp.bfloat16),
            pltpu.VMEM((table, BLOCK), jnp.bfloat16),
            pltpu.VMEM((units, halo), jnp.float32),
            pltpu.VMEM((padded, BLOCK), jnp.bfloat16),
            pltpu.VMEM((units, width), jnp.bfloat16),
            pltpu.VMEM((units, padded), jnp.bfloat16),
            pltpu.VMEM((units, 128), jnp.float32),
        ],
        compiler_params=params(),
        name="hidden_layer",
    )(words, own, own, got, weight, bias_row, send_row)


def far_groups(nodes, halo):
    span = (nodes + halo) // GROUPS
    first = nodes // span
    return span, first, nodes - first * span


def far_finish(fanout, nodes, far_sums, far_ref, halo_ref, near_right):
    halo = far_ref.shape[0]
    span, first, skip = far_groups(nodes, halo)
    pieces = []
    for group in range(first, GROUPS):
        row = (group - first) * span
        pieces.append(far_sums[row : row + span, :] * (slot_scale(group % SLOTS) / fanout))
    sums = jnp.concatenate(pieces).astype(jnp.bfloat16)[skip:]
    far_ref[...] = sums
    halo_ref[...] = dot(sums, near_right).astype(jnp.bfloat16)


def last_kernel(
    fanout,
    bias_start,
    words_ref,
    own_ref,
    own_block,
    got_ref,
    weight_ref,
    bias_ref,
    seeds_ref,
    grad_ref,
    rows_ref,
    sums_ref,
    notes_ref,
    table_out,
    far_ref,
    halo_ref,
    reduced_ref,
    counts_ref,
    both_ref,
    self_ref,
    near_ref,
    bias_col,
    far_sums,
):
    step = pl.program_id(0)
    last = pl.num_programs(0) - 1
    classes = self_ref.shape[0]
    width, nodes = own_ref.shape
    kinds = weight_ref.shape[0]
    halo = far_ref.shape[0]
    span, first, skip = far_groups(nodes, halo)

    @pl.when(step == 0)
    def _():
        table_out[:, :nodes] = own_ref[...]
        table_out[:, nodes:] = got_ref[...].reshape(halo, width).T
        more = jnp.zeros((classes - kinds, 2 * width), jnp.float32)
        weight = jnp.concatenate([weight_ref[...], more]).astype(jnp.bfloat16)
        self_ref[...] = weight[:, :width]
        near_ref[...] = weight[:, width:]
        rest = jnp.full((1, classes - kinds), -1e30, jnp.float32)
        bias_col[...] = column_of(
            jnp.concatenate([bias_ref[:, bias_start : bias_start + kinds], rest], axis=1)
        )
        reduced = dot(near_ref[...], table_out[...]) * scale_row(table_out.shape[1])
        high = reduced.astype(jnp.bfloat16)
        reduced_ref[:classes, :] = high
        reduced_ref[classes:, :] = (reduced - high.astype(jnp.float32)).astype(jnp.bfloat16)
        both_ref[...] = jnp.zeros_like(both_ref)
        counts_ref[first * span :, :] = jnp.zeros_like(counts_ref[first * span :, :])

    @pl.when(step <= 1)
    def _():
        sums_ref[...] = jnp.zeros_like(sums_ref)
        notes_ref[...] = jnp.zeros_like(notes_ref)
        far_sums[...] = jnp.zeros_like(far_sums)

    def finish():
        near_part = (both_ref[:classes, :] + both_ref[classes:, :]) / fanout
        logits = dot(self_ref[...], own_block[...]) + near_part + bias_col[:, :1]
        top = jnp.max(logits, axis=0, keepdims=True)
        powers = jnp.exp(logits - top)
        total = jnp.sum(powers, axis=0, keepdims=True)
        normer = jnp.log(total) + top
        seeds = seeds_ref[...]
        uses = jnp.sum(seeds, axis=0, keepdims=True)
        grad = (powers / total * uses - seeds).astype(jnp.bfloat16)
        grad_ref[...] = grad
        loss = uses * normer - jnp.sum(seeds * logits, axis=0, keepdims=True)
        sums_ref[...] += jnp.sum(grad.astype(jnp.float32), axis=1, keepdims=True)
        notes_ref[:8, :] += jnp.sum(loss)
        notes_ref[8:, :] += jnp.sum(uses)
        rows = grad.T
        rows_ref[...] = rows
        far_sums[...] += dot(counts_ref[first * span :, :], rows)

    @pl.when(step < last)
    def _():
        finish()
        both_ref[...] = gather_product(reduced_ref, words_ref, counts_ref)

    @pl.when(step == last)
    def _():
        finish()
        far_finish(fanout, nodes, far_sums, far_ref, halo_ref, near_ref[...])


def last_layer(words, own, got, weight, bias_row, bias_start, seeds, fanout):
    width, nodes = own.shape
    halo = got.shape[0] * got.shape[1]
    table = nodes + halo
    classes = seeds.shape[0]
    steps = nodes // BLOCK
    span, first, _ = far_groups(nodes, halo)
    far_height = (GROUPS - first) * span
    return pl.pallas_call(
        functools.partial(last_kernel, fanout, bias_start),
        grid=(steps + 1,),
        in_specs=[
            now(words.shape[0], BLOCK, steps),
            whole(own.shape),
            late(width, BLOCK),
            whole(got.shape),
            whole(weight.shape),
            whole(bias_row.shape),
            late(classes, BLOCK),
        ],
        out_specs=[
            late(classes, BLOCK),
            pl.BlockSpec((BLOCK, classes), lambda i: (jnp.maximum(i - 1, 0), 0)),
            whole((classes, 128)),
            whole((16, 128)),
            whole((width, table)),
            whole((halo, classes)),
            whole((halo, width)),
        ],
        out_shape=[
            jax.ShapeDtypeStruct((classes, nodes), jnp.bfloat16),
            jax.ShapeDtypeStruct((nodes, classes), jnp.bfloat16),
            jax.ShapeDtypeStruct((classes, 128), jnp.float32),
            jax.ShapeDtypeStruct((16, 128), jnp.float32),
            jax.ShapeDtypeStruct((width, table), jnp.bfloat16),
            jax.ShapeDtypeStruct((halo, classes), jnp.bfloat16),
            jax.ShapeDtypeStruct((halo, width), jnp.bfloat16),
        ],
        scratch_shapes=[
            pltpu.VMEM((2 * classes, table), jnp.bfloat16),
            pltpu.VMEM((table, BLOCK), jnp.bfloat16),
            pltpu.VMEM((2 * classes, BLOCK), jnp.float32),
            pltpu.VMEM((classes, width), jnp.bfloat16),
            pltpu.VMEM((classes, width), jnp.bfloat16),
            pltpu.VMEM((classes, 128), jnp.float32),
            pltpu.VMEM((far_height, classes), jnp.float32),
        ],
        compiler_params=params(),
        name="last_layer",
    )(words, own, own, got, weight, bias_row, seeds)


def spread_slot(words_ref, word_row, counts_ref, count_row, slot, span):
    for start in range(0, span, 48):
        for tile in range(0, words_ref.shape[1], 512):
            cols = slice(tile, tile + 512)
            counts_ref[count_row + start : count_row + start + 48, cols] = field(
                words_ref[word_row + start : word_row + start + 48, cols], slot
            )


def scatter_kernel(
    mesh_sizes,
    fanout,
    flipped,
    words_ref,
    grad_ref,
    rows_ref,
    far_ref,
    table_ref,
    far_table,
    weight_in,
    halo_ref,
    other_ref,
    state_ref,
    weight_ref,
    got_ref,
    *refs,
):
    if flipped:
        notes_ref, padded_ref, counts_ref, sums_ref, self_ref, near_ref, land_ref = refs[:7]
        send_sem, recv_sem, notes_land, notes_send, notes_recv = refs[7:]
        total_ref = weight_ref
    else:
        padded_ref, counts_ref, sums_ref, self_ref, near_ref, total_ref, land_ref = refs[:7]
        send_sem, recv_sem = refs[7:]
    step = pl.program_id(0)
    units, nodes = grad_ref.shape
    width = table_ref.shape[0]
    span = words_ref.shape[0]
    part = span * SLOTS
    steps = -(-nodes // part)
    moves = (mesh_sizes, halo_ref, land_ref, send_sem, recv_sem)

    @pl.when(step == 0)
    def _():
        greet(mesh_sizes)
        for k in range(steps):
            start = k * part
            stop = min(start + part, nodes)
            padded_ref[k, :, : stop - start] = grad_ref[:, start:stop]
            if stop < start + part:
                padded_ref[k, :, stop - start :] = jnp.zeros(
                    (units, start + part - stop), jnp.bfloat16
                )
        if flipped:
            weight = weight_in[...]
            more = jnp.zeros((units - weight.shape[0], 2 * width), jnp.float32)
            weight = jnp.concatenate([weight, more]).T
        else:
            weight = weight_in[...]
        self_ref[...] = weight[:width].astype(jnp.bfloat16)
        near_ref[...] = weight[width:].astype(jnp.bfloat16)
        total_ref[:width, :] = jnp.zeros((width, units), jnp.float32)
        total_ref[width:, :] = dot(far_table[...], far_ref[...])
        sums_ref[...] = jnp.zeros_like(sums_ref)

    pair = 2

    def add(slot):
        for one in range(slot, slot + pair):
            spread_slot(words_ref, 0, counts_ref, one * span, one, span)
        added = dot(counts_ref[slot * span : (slot + pair) * span, :], rows_ref[...])
        for one in range(slot, slot + pair):
            piece = added[(one - slot) * span : (one - slot + 1) * span, :]
            piece = (piece * (slot_scale(one) / fanout)).astype(jnp.bfloat16)
            sums_ref[one * span : (one + 1) * span, :] = piece

    beyond = nodes - (steps - 1) * part
    ending = -(-beyond // (pair * span)) * pair
    for slot in range(0, ending, pair):
        add(slot)
    if ending < SLOTS:

        @pl.when(step < steps - 1)
        def _():
            for slot in range(ending, SLOTS, pair):
                add(slot)

    if beyond < part:

        @pl.when(step == steps - 1)
        def _():
            sums_ref[beyond:, :] = jnp.zeros((part - beyond, units), jnp.bfloat16)

    sums = sums_ref[...]
    own_grad = padded_ref[step]
    state_ref[...] = dot(near_ref[...], sums, TRANS_RIGHT) + dot(self_ref[...], own_grad)
    total_ref[:width, :] += dot(table_ref[...], own_grad, TRANS_RIGHT)
    total_ref[width:, :] += dot(table_ref[...], sums)

    @pl.when(step == 0)
    def _():
        all_greeted(mesh_sizes)
        send_blocks(*moves)
        if flipped:
            send_all(mesh_sizes, other_ref, notes_land, notes_send, notes_recv)

    @pl.when(step == steps - 1)
    def _():
        me = ring(mesh_sizes)[1]
        wait_blocks(*moves)
        land_ref[me] = halo_ref[me]
        got_ref[...] = land_ref[...]
        if flipped:
            wait_all(mesh_sizes, other_ref, notes_land, notes_send, notes_recv)
            notes_land[me] = other_ref[...]
            notes_ref[...] = jnp.sum(notes_land[...], axis=0)
        else:
            weight_ref[:, :units] = total_ref[...].astype(jnp.bfloat16)
            weight_ref[:, units:] = jnp.zeros_like(weight_ref[:, units:])
            narrow = other_ref.shape[1]
            weight_ref[:, units : units + narrow] = other_ref[...].astype(jnp.bfloat16)


def scatter_layer(words, grad, rows, far, table, weight, halo_rows, other, mesh_sizes, collective, fanout):
    units, nodes = grad.shape
    width, total = table.shape
    parts = mesh_sizes[0] * mesh_sizes[1]
    flipped = weight.shape[1] == 2 * width
    span = total // GROUPS
    part = total // WORDS
    steps = -(-nodes // part)
    far_table = table[:, nodes:]
    blocks = (parts, halo_rows.shape[0] // parts, width)
    out_specs = [lanes(width, part)]
    out_shape = [jax.ShapeDtypeStruct((width, total), jnp.float32)]
    if flipped:
        sums_shape, sums_type = (2 * width, units), jnp.float32
    else:
        wide = units + -(-other.shape[1] // 128) * 128
        sums_shape, sums_type = (2 * width, wide), jnp.bfloat16
    out_specs += [whole(sums_shape), whole(blocks)]
    out_shape += [
        jax.ShapeDtypeStruct(sums_shape, sums_type),
        jax.ShapeDtypeStruct(blocks, jnp.bfloat16),
    ]
    scratch = [
        pltpu.VMEM((steps, units, part), jnp.bfloat16),
        pltpu.VMEM((part, nodes), jnp.bfloat16),
        pltpu.VMEM((part, units), jnp.bfloat16),
        pltpu.VMEM((width, units), jnp.bfloat16),
        pltpu.VMEM((width, units), jnp.bfloat16),
    ]
    if not flipped:
        scratch.append(pltpu.VMEM((2 * width, units), jnp.float32))
    scratch += [pltpu.VMEM(blocks, jnp.bfloat16)] + semaphores(parts)
    if flipped:
        out_specs.append(whole(other.shape))
        out_shape.append(jax.ShapeDtypeStruct(other.shape, other.dtype))
        scratch += [pltpu.VMEM((parts,) + other.shape, other.dtype)] + semaphores(parts)
    return pl.pallas_call(
        functools.partial(scatter_kernel, mesh_sizes, fanout, flipped),
        grid=(steps,),
        in_specs=[
            pl.BlockSpec((span, nodes), lambda i: (i, 0)),
            whole(grad.shape),
            whole(rows.shape),
            whole(far.shape),
            lanes(width, part),
            whole(far_table.shape),
            whole(weight.shape),
            whole(blocks),
            whole(other.shape),
        ],
        out_specs=out_specs,
        out_shape=out_shape,
        scratch_shapes=scratch,
        compiler_params=params(collective),
        name="scatter_layer",
    )(words, grad, rows, far, table, far_table, weight, halo_rows.reshape(blocks), other)


def active_grad(step, state_ref, preact_ref, back_ref, send_ref):
    block = state_ref.shape[1]
    chosen = chosen_nodes(send_ref[...], step * block, block)
    upper = state_ref[...] + dot(back_ref[...], chosen, TRANS_RIGHT)
    preact = preact_ref[...]
    gate = jax.nn.sigmoid(preact)
    active = preact * gate
    norm = lax.rsqrt(jnp.sum(active * active, axis=0, keepdims=True) + 1e-06)
    along = jnp.sum(active * upper, axis=0, keepdims=True)
    inner = norm * upper - active * (norm * norm * norm * along)
    return (inner * (gate * (1.0 + preact * (1.0 - gate)))).astype(jnp.bfloat16)


def middle_kernel(
    fanout,
    state_ref,
    preact_ref,
    returned_ref,
    send_ref,
    words_ref,
    weight_ref,
    grad_ref,
    rows_ref,
    sums_ref,
    far_ref,
    halo_ref,
    back_ref,
    counts_ref,
    far_sums,
):
    step = pl.program_id(0)
    units, block = state_ref.shape
    halo = far_ref.shape[0]
    nodes = block * pl.num_programs(0)
    span, first, skip = far_groups(nodes, halo)

    @pl.when(step == 0)
    def _():
        back_ref[...] = returned_ref[...].reshape(halo, units).T
        sums_ref[...] = jnp.zeros_like(sums_ref)
        far_sums[...] = jnp.zeros_like(far_sums)

    base = first // SLOTS * SLOTS
    for group in range(first, GROUPS):
        word = group // SLOTS - base // SLOTS
        spread_slot(
            words_ref, word * span, counts_ref, (group - first) * span, group % SLOTS, span
        )
    grad = active_grad(step, state_ref, preact_ref, back_ref, send_ref)
    grad_ref[...] = grad
    sums_ref[...] += jnp.sum(grad.astype(jnp.float32), axis=1, keepdims=True)
    rows = grad.T
    rows_ref[...] = rows
    far_sums[...] += dot(counts_ref[...], rows)

    @pl.when(step == pl.num_programs(0) - 1)
    def _():
        near = weight_ref[units:, :].T.astype(jnp.bfloat16)
        far_finish(fanout, nodes, far_sums, far_ref, halo_ref, near)


def middle_layer(state_grad, preact, returned, send_row, words, weight, fanout):
    units, nodes = preact.shape
    halo = send_row.shape[1]
    span, first, _ = far_groups(nodes, halo)
    far_words = WORDS - first // SLOTS
    far_height = (GROUPS - first) * span
    return pl.pallas_call(
        functools.partial(middle_kernel, fanout),
        grid=(nodes // BLOCK,),
        in_specs=[
            lanes(units, BLOCK),
            lanes(units, BLOCK),
            whole(returned.shape),
            whole(send_row.shape),
            pl.BlockSpec((far_words * span, BLOCK), lambda i: (WORDS // far_words - 1, i)),
            whole(weight.shape),
        ],
        out_specs=[
            lanes(units, BLOCK),
            pl.BlockSpec((BLOCK, units), lambda i: (i, 0)),
            whole((units, 128)),
            whole((halo, units)),
            whole((halo, units)),
        ],
        out_shape=[
            jax.ShapeDtypeStruct((units, nodes), jnp.bfloat16),
            jax.ShapeDtypeStruct((nodes, units), jnp.bfloat16),
            jax.ShapeDtypeStruct((units, 128), jnp.float32),
            jax.ShapeDtypeStruct((halo, units), jnp.bfloat16),
            jax.ShapeDtypeStruct((halo, units), jnp.bfloat16),
        ],
        scratch_shapes=[
            pltpu.VMEM((units, halo), jnp.bfloat16),
            pltpu.VMEM((far_height, BLOCK), jnp.bfloat16),
            pltpu.VMEM((far_height, units), jnp.float32),
        ],
        compiler_params=params(),
        name="middle_layer",
    )(state_grad, preact, returned, send_row, words, weight)


def bottom_kernel(
    mesh_sizes,
    state_ref,
    preact_ref,
    returned_ref,
    send_ref,
    own_block,
    mean_block,
    sums_two,
    sums_three,
    early_ref,
    late_ref,
    early_sum,
    back_ref,
    sums_ref,
    weight_ref,
    land_ref,
    send_sem,
    recv_sem,
):
    step = pl.program_id(0)
    units = state_ref.shape[0]
    halo = send_ref.shape[1]
    moves = (mesh_sizes, early_ref, land_ref, send_sem, recv_sem)

    @pl.when(step == 0)
    def _():
        greet(mesh_sizes)
        back_ref[...] = returned_ref[...].reshape(halo, units).T
        sums_ref[...] = jnp.zeros_like(sums_ref)
        weight_ref[...] = jnp.zeros_like(weight_ref)

    grad = active_grad(step, state_ref, preact_ref, back_ref, send_ref)
    sums_ref[...] += jnp.sum(grad.astype(jnp.float32), axis=1, keepdims=True)
    width = own_block.shape[0]
    weight_ref[0, :width, :] += dot(own_block[...], grad, TRANS_RIGHT)
    weight_ref[1] += dot(mean_block[...], grad, TRANS_RIGHT)

    @pl.when(step == 0)
    def _():
        all_greeted(mesh_sizes)
        send_blocks(*moves)

    @pl.when(step == pl.num_programs(0) - 1)
    def _():
        me = ring(mesh_sizes)[1]
        padded = weight_ref.shape[1]
        row = 0
        for start in range(0, units, 128):
            for half in range(2):
                late_ref[row : row + padded, :] = weight_ref[half, :, start : start + 128].astype(
                    jnp.bfloat16
                )
                row += padded
        pieces = []
        for sums in (sums_ref, sums_two, sums_three):
            flat = sums[...].T[:1]
            for start in range(0, flat.shape[1], 128):
                piece = flat[:, start : start + 128]
                pieces.append(piece)
        narrow = pieces[-1].shape[1]
        pieces[-1] = jnp.concatenate(
            [pieces[-1], jnp.zeros((1, 128 - narrow), jnp.float32)], axis=1
        )
        rest = late_ref.shape[0] - row
        pieces.append(jnp.zeros((rest - len(pieces), 128), jnp.float32))
        late_ref[row:, :] = jnp.concatenate(pieces).astype(jnp.bfloat16)
        wait_blocks(*moves)
        land_ref[me] = early_ref[me]
        early_sum[...] = jnp.sum(land_ref[...].astype(jnp.float32), axis=0).astype(jnp.bfloat16)


def bottom_layer(
    state_grad, preact, returned, send_row, own, mean, sums_two, sums_three, early, mesh_sizes, collective
):
    units, nodes = preact.shape
    width = own.shape[0]
    padded = mean.shape[0]
    halo = send_row.shape[1]
    parts = mesh_sizes[0] * mesh_sizes[1]
    rows = units // 128 * (2 * padded + 2) + -(-sums_three.shape[0] // 128)
    rows = -(-rows // 512) * 512
    rows = -(-rows // parts) * parts
    early_blocks = (parts, early.shape[0] // parts, early.shape[1])
    return pl.pallas_call(
        functools.partial(bottom_kernel, mesh_sizes),
        grid=(nodes // BLOCK,),
        in_specs=[
            lanes(units, BLOCK),
            lanes(units, BLOCK),
            whole(returned.shape),
            whole(send_row.shape),
            lanes(width, BLOCK),
            lanes(padded, BLOCK),
            whole(sums_two.shape),
            whole(sums_three.shape),
            whole(early_blocks),
        ],
        out_specs=[whole((rows, 128)), whole(early_blocks[1:])],
        out_shape=[
            jax.ShapeDtypeStruct((rows, 128), jnp.bfloat16),
            jax.ShapeDtypeStruct(early_blocks[1:], jnp.bfloat16),
        ],
        scratch_shapes=[
            pltpu.VMEM((units, halo), jnp.bfloat16),
            pltpu.VMEM((units, 128), jnp.float32),
            pltpu.VMEM((2, padded, units), jnp.float32),
            pltpu.VMEM(early_blocks, jnp.bfloat16),
        ]
        + semaphores(parts),
        compiler_params=params(collective),
        name="bottom_layer",
    )(
        state_grad,
        preact,
        returned,
        send_row,
        own,
        mean,
        sums_two,
        sums_three,
        early.reshape(early_blocks),
    )


def share_kernel(
    mesh_sizes,
    early_ref,
    late_ref,
    early_out,
    late_out,
    early_land,
    late_land,
    late_sum,
    late_all,
    early_send,
    early_recv,
    late_send,
    late_recv,
    last_send,
    last_recv,
):
    me = ring(mesh_sizes)[1]
    first = (mesh_sizes, late_ref, late_land, late_send, late_recv)
    second = (mesh_sizes, early_ref, early_land, early_send, early_recv)
    third = (mesh_sizes, late_sum, late_all, last_send, last_recv)
    greet(mesh_sizes)
    all_greeted(mesh_sizes)
    send_blocks(*first)
    send_all(*second)
    wait_blocks(*first)
    late_land[me] = late_ref[me]
    late_sum[...] = jnp.sum(late_land[...].astype(jnp.float32), axis=0).astype(jnp.bfloat16)
    send_all(*third)
    wait_all(*second)
    early_land[me] = early_ref[...]
    early_out[...] = early_land[...]
    wait_all(*third)
    late_all[me] = late_sum[...]
    late_out[...] = late_all[...]


def share_sums(early_sum, late_rows, mesh_sizes, collective):
    parts = mesh_sizes[0] * mesh_sizes[1]
    early = (parts,) + early_sum.shape
    late_shape = (parts, late_rows.shape[0] // parts, 128)
    vmem = pl.BlockSpec(memory_space=pltpu.VMEM)
    return pl.pallas_call(
        functools.partial(share_kernel, mesh_sizes),
        in_specs=[vmem, vmem],
        out_specs=[vmem, vmem],
        out_shape=[
            jax.ShapeDtypeStruct(early, jnp.bfloat16),
            jax.ShapeDtypeStruct(late_shape, jnp.bfloat16),
        ],
        scratch_shapes=[
            pltpu.VMEM(early, jnp.bfloat16),
            pltpu.VMEM(late_shape, jnp.bfloat16),
            pltpu.VMEM(late_shape[1:], jnp.bfloat16),
            pltpu.VMEM(late_shape, jnp.bfloat16),
        ]
        + semaphores(parts)
        + semaphores(parts)
        + semaphores(parts),
        compiler_params=pltpu.CompilerParams(
            vmem_limit_bytes=VMEM_BYTES, collective_id=collective, has_side_effects=True
        ),
        name="share_sums",
    )(early_sum, late_rows.reshape(late_shape))


def in_two(value):
    high = value.astype(jnp.bfloat16)
    return high, (value - high.astype(jnp.float32)).astype(jnp.bfloat16)


def product(left, right, dims=(((1,), (0,)), ((), ()))):
    if left.dtype == jnp.bfloat16:
        high, low = in_two(right)
        return dot(left, high, dims) + dot(left, low, dims)
    high, low = in_two(left)
    if right.dtype == jnp.bfloat16:
        return dot(high, right, dims) + dot(low, right, dims)
    right_high, right_low = in_two(right)
    return dot(high, right_high, dims) + (
        dot(high, right_low, dims) + dot(low, right_high, dims)
    )


def moments(turned, first, second):
    first = beta_one * first + (1.0 - beta_one) * turned
    second = beta_two * second + (1.0 - beta_two) * turned * turned
    update = first / (1.0 - beta_one**STEP) / (jnp.sqrt(second / (1.0 - beta_two**STEP)) + epsilon)
    return first, second, update


def adam_kernel(
    padded,
    early_ref,
    late_ref,
    notes_ref,
    weight_one,
    weight_two,
    weight_three,
    left_one,
    right_one,
    left_two,
    right_two,
    left_three,
    right_three,
    first_one,
    first_two,
    first_three,
    second_one,
    second_two,
    second_three,
    bias_ref,
    bias_first,
    bias_second,
    *outs,
):
    share = 1.0 / notes_ref[8:9, 0:1]
    units = weight_two.shape[1]
    width = weight_one.shape[0] // 2
    kinds = weight_three.shape[0]

    def step(grad, weight, first, second, left, right, rate, out):
        turned = product(product(left[...], grad, TRANS_LEFT), right[...]) * share
        new_first, new_second, update = moments(turned, first[...], second[...])
        out[1][...] = new_first
        out[2][...] = new_second
        moved = product(product(left[...], update), right[...], TRANS_RIGHT)
        out[0][...] = weight[...] - rate * moved

    step(
        early_ref[:, :units],
        weight_two,
        first_two,
        second_two,
        left_two,
        right_two,
        step_rates[1],
        outs[3:6],
    )
    grad = early_ref[:, units:].astype(jnp.float32).T[:kinds].astype(jnp.bfloat16)
    turned = product(right_three[...], product(grad, left_three[...])) * share
    new_first, new_second, update = moments(turned, first_three[...], second_three[...])
    outs[7][...] = new_first
    outs[8][...] = new_second
    moved = product(update, left_three[...], TRANS_RIGHT)
    moved = product(right_three[...], moved, TRANS_LEFT)
    outs[6][...] = weight_three[...] - step_rates[2] * moved

    late_rows = late_ref[...].astype(jnp.float32)
    columns = []
    for start in range(0, units, 128):
        row = start // 128 * 2 * padded
        columns.append(
            jnp.concatenate(
                [late_rows[row : row + width], late_rows[row + padded : row + padded + width]]
            )
        )
    step(
        jnp.concatenate(columns, axis=1).astype(jnp.bfloat16),
        weight_one,
        first_one,
        second_one,
        left_one,
        right_one,
        step_rates[0],
        outs[0:3],
    )
    row = units // 128 * 2 * padded
    pieces = []
    while len(pieces) * 128 < 2 * units + kinds:
        pieces.append(late_rows[row : row + 1])
        row += 1
    grad = jnp.concatenate(pieces, axis=1)[:, : 2 * units + kinds] * share
    new_first, new_second, update = moments(grad, bias_first[...], bias_second[...])
    bias = bias_ref[...]
    outs[9][...] = bias - bias_rate * (update + weight_decay * bias)
    outs[10][...] = new_first
    outs[11][...] = new_second


def adam(padded, early_all, late_all, notes, *state):
    vmem = pl.BlockSpec(memory_space=pltpu.VMEM)
    order = (0, 9, 12, 1, 10, 13, 2, 11, 14, 15, 16, 17)
    outs = [jax.ShapeDtypeStruct(state[at].shape, jnp.float32) for at in order]
    return pl.pallas_call(
        functools.partial(adam_kernel, padded),
        in_specs=[vmem] * (3 + len(state)),
        out_specs=[vmem] * len(outs),
        out_shape=outs,
        compiler_params=pltpu.CompilerParams(vmem_limit_bytes=VMEM_BYTES),
        name="adam",
    )(early_all, late_all, notes, *state)


def on_device(
    mesh_sizes,
    features,
    labels,
    seed_rows,
    seed_mask,
    send_rows,
    neighbors_one,
    neighbors_two,
    neighbors_three,
    weight_one,
    weight_two,
    weight_three,
    left_one,
    right_one,
    left_two,
    right_two,
    left_three,
    right_three,
    first_one,
    first_two,
    first_three,
    second_one,
    second_two,
    second_three,
    bias_all,
    bias_first,
    bias_second,
):
    units = weight_one.shape[1]
    classes = weight_three.shape[1]
    halo = send_rows.size
    fans = (neighbors_one.shape[1], neighbors_two.shape[1], neighbors_three.shape[1])
    feats = features.T
    send_row = send_rows.reshape(1, halo)
    bias_row = bias_all.reshape(1, -1)
    weight_three = weight_three.T
    padded_classes = -(-classes // 16) * 16
    seed_slots = (
        padded_classes,
        seed_rows.reshape(1, -1),
        labels.reshape(1, -1),
        seed_mask.reshape(1, -1),
    )

    words_one, got = count_words(
        neighbors_one.T, mesh_sizes, 0, halo, feats=feats, send_row=send_row
    )
    state_one, preact_one, sent, mean_one = hidden_layer(
        words_one, feats, got, weight_one, bias_row, 0, send_row, fans[0]
    )
    words_two, got = count_words(neighbors_two.T, mesh_sizes, 1, halo, sent=sent)
    state_two, preact_two, sent, table_two = hidden_layer(
        words_two, state_one, got, weight_two, bias_row, units, send_row, fans[1]
    )
    words_three, got, seeds = count_words(
        neighbors_three.T, mesh_sizes, 2, halo, sent=sent, seeds=seed_slots
    )
    grad_three, rows_three, sums_three, notes, table_three, far, halo_grad = last_layer(
        words_three, state_two, got, weight_three, bias_row, 2 * units, seeds, fans[2]
    )
    state_grad, weight_grad, returned, notes = scatter_layer(
        words_three,
        grad_three,
        rows_three,
        far,
        table_three,
        weight_three,
        halo_grad,
        notes,
        mesh_sizes,
        3,
        fans[2],
    )
    grad_two, rows_two, sums_two, far, halo_grad = middle_layer(
        state_grad, preact_two, returned, send_row, words_two, weight_two, fans[1]
    )
    state_grad, early, returned = scatter_layer(
        words_two,
        grad_two,
        rows_two,
        far,
        table_two,
        weight_two,
        halo_grad,
        weight_grad,
        mesh_sizes,
        4,
        fans[1],
    )
    late_rows, early_sum = bottom_layer(
        state_grad,
        preact_one,
        returned,
        send_row,
        feats,
        mean_one,
        sums_two,
        sums_three,
        early,
        mesh_sizes,
        5,
    )
    early_all, late_all = share_sums(early_sum, late_rows, mesh_sizes, 6)
    out = adam(
        mean_one.shape[0],
        early_all.reshape(early.shape),
        late_all.reshape(late_rows.shape),
        notes,
        weight_one,
        weight_two,
        weight_three,
        left_one,
        right_one,
        left_two,
        right_two,
        left_three,
        right_three.T,
        first_one,
        first_two,
        first_three.T,
        second_one,
        second_two,
        second_three.T,
        bias_row,
        bias_first.reshape(1, -1),
        bias_second.reshape(1, -1),
    )
    biases = [value.reshape(-1) for value in out[9:12]]
    third = [value.T for value in out[6:9]]
    return (*out[:6], *third, *biases, notes[0, 0], notes[8, 0])


def solution(mesh):
    split = P(axes)
    rows = P(axes, None)
    placed = (rows, split, split, split, rows, rows, rows, rows) + (P(),) * 18
    mesh_sizes = (mesh.shape[axes[0]], mesh.shape[axes[1]])
    return jax.shard_map(
        functools.partial(on_device, mesh_sizes),
        mesh=mesh,
        in_specs=placed,
        out_specs=(P(),) * 14,
        check_vma=False,
    )
```

profile of v0, /device:TPU:0, one launch (start us, length us, event | category | flops | bytes accessed | tf_op | source)
XLA Modules:
  0.0 228.4 jit_solution(4717580619250470955)
XLA Ops:
  0.6 0.8 copy.42
  1.4 0.7 reshape.82.refs_1_.send_ref
  2.1 17.8 %count_words.3 = (s32[576,4096]{1,0:T(8,128)}, bf16[32,16,128]{2,1,0:T(8,128)(2,1)}) custom-call(s32[15,4096]{1,0:T(8,128)} %bitcast.34, bf16[100,4096]{1,0:T(8,128)(2,1)} %bitcast.24, s32[1,512]{1,0:T(1,128)} %reshape.82.refs_1_.send_ref), custom_call_target="tpu_custom_call" | custom-call | tf_op jit(solution)/shard_map/count_words/pallas_call | solution.py:285
  19.8 1.3 reshape.83.bias_ref
  21.1 18.8 %hidden_layer.2 = (bf16[256,4096]{1,0:T(8,128)(2,1)}, f32[256,4096]{1,0:T(8,128)}, bf16[512,256]{1,0:T(8,128)(2,1)}, bf16[112,4096]{1,0:T(8,128)(2,1)}) custom-call(s32[576,4096]{1,0:T(8,128)} %get-tuple-element.64.words_ref, bf16[100,4096]{1,0:T(8,128)(2,1)} %bitcast.25, bf16[100,4096]{1,0:T(8,128)(2,1)} %bitcast.26, ...), custom_call_target="tpu_custom_call" | custom-call | tf_op jit(solution)/shard_map/hidden_layer/pallas_call | solution.py:450
  39.9 12.6 %count_words.4 = (s32[576,4096]{1,0:T(8,128)}, bf16[32,16,256]{2,1,0:T(8,128)(2,1)}) custom-call(s32[10,4096]{1,0:T(8,128)} %bitcast.36, bf16[32,16,256]{2,1,0:T(8,128)(2,1)} %bitcast.38), custom_call_target="tpu_custom_call" | custom-call | tf_op jit(solution)/shard_map/count_words/pallas_call | solution.py:285
  52.6 21.8 %hidden_layer.3 = (bf16[256,4096]{1,0:T(8,128)(2,1)}, f32[256,4096]{1,0:T(8,128)}, bf16[512,256]{1,0:T(8,128)(2,1)}, bf16[256,4608]{1,0:T(8,128)(2,1)}) custom-call(s32[576,4096]{1,0:T(8,128)} %get-tuple-element.67.words_ref, bf16[256,4096]{1,0:T(8,128)(2,1)} %get-tuple-element.68.own_ref.own_block, bf16[256,4096]{1,0:T(8,128)(2,1)} %get-tuple-element.68.own_ref.own_block, ...), custom_call_target="tpu_custom_call" | custom-call | tf_op jit(solution)/shard_map/hidden_layer/pallas_call | solution.py:450
  74.4 16.9 %count_words.5 = (s32[576,4096]{1,0:T(8,128)}, bf16[32,16,256]{2,1,0:T(8,128)(2,1)}, f32[48,4096]{1,0:T(8,128)}) custom-call(s32[5,4096]{1,0:T(8,128)} %bitcast.39, bf16[32,16,256]{2,1,0:T(8,128)(2,1)} %bitcast.37, s32[1,2048]{1,0:T(1,128)} %bitcast.45, s32[1,2048]{1,0:T(1,128)} %bitcast.46, s32[1,2048]{1,0:T(1,128)} %bitcast.47), custom_call_target="tpu_custom_call" | custom-call | tf_op jit(solution)/shard_map/count_words/pallas_call | solution.py:285
  91.3 21.8 %last_layer.1 = (bf16[48,4096]{1,0:T(8,128)(2,1)}, bf16[4096,48]{1,0:T(8,128)(2,1)}, f32[48,128]{1,0:T(8,128)}, f32[16,128]{1,0:T(8,128)}, bf16[256,4608]{1,0:T(...) custom-call(s32[576,4096]{1,0:T(8,128)} %get-tuple-element.71.words_ref, ...), custom_call_target="tpu_custom_call" | custom-call | tf_op jit(solution)/shard_map/last_layer/pallas_call | solution.py:602
  113.1 1.7 slice.12.far_table
  114.8 21.6 %scatter_layer.2 = (f32[256,4608]{1,0:T(8,128)}, f32[512,48]{1,0:T(8,128)}, bf16[32,16,256]{2,1,0:T(8,128)(2,1)}, f32[16,128]{1,0:T(8,128)}) custom-call(s32[576,4096]{1,0:T(8,128)} %get-tuple-element.71.words_ref, bf16[48,4096]{1,0:T(8,128)(2,1)} %get-tuple-element.75.grad_ref, bf16[4096,48]{1,0:T(8,128)(2,1)} %get-tuple-element.76.rows_ref, ...), custom_call_target="tpu_custom_call" | custom-call | tf_op jit(solution)/shard_map/scatter_layer/pallas_call | solution.py:805
  136.4 12.6 %middle_layer.1 = (bf16[256,4096]{1,0:T(8,128)(2,1)}, bf16[4096,256]{1,0:T(8,128)(2,1)}, f32[256,128]{1,0:T(8,128)}, bf16[512,256]{1,0:T(8,128)(2,1)}, bf16[512,256]{1,0:T(8,128)(2,1)}) custom-call(f32[256,4608]{1,0:T(8,128)} %get-tuple-element.81.state_ref, f32[256,4096]{1,0:T(8,128)} %get-tuple-element.82.preact_ref, ...), custom_call_target="tpu_custom_call" | custom-call | tf_op jit(solution)/shard_map/middle_layer/pallas_call | solution.py:894
  149.0 1.7 slice.13.far_table
  150.6 21.7 %scatter_layer.3 = (f32[256,4608]{1,0:T(8,128)}, bf16[512,384]{1,0:T(8,128)(2,1)}, bf16[32,16,256]{2,1,0:T(8,128)(2,1)}) custom-call(s32[576,4096]{1,0:T(8,128)} %get-tuple-element.67.words_ref, bf16[256,4096]{1,0:T(8,128)(2,1)} %get-tuple-element.84.grad_ref, bf16[4096,256]{1,0:T(8,128)(2,1)} %get-tuple-element.85.rows_ref, ...), custom_call_target="tpu_custom_call" | custom-call | tf_op jit(solution)/shard_map/scatter_layer/pallas_call | solution.py:805
  172.4 0.0 copy-start
  172.4 0.0 copy-start.1
  172.4 0.0 copy-start.2
  172.4 16.5 %bottom_layer.1 = (bf16[512,128]{1,0:T(8,128)(2,1)}, bf16[16,384]{1,0:T(8,128)(2,1)}) custom-call(f32[256,4608]{1,0:T(8,128)} %get-tuple-element.90.state_ref, f32[256,4096]{1,0:T(8,128)} %get-tuple-element.91.preact_ref, bf16[32,16,256]{2,1,0:T(8,128)(2,1)} %get-tuple-element.92.returned_ref, s32[1,512]{1,0:T(1,128)} %reshape.82.refs_1_.send_ref, ...), custom_call_target="tpu_custom_call" | custom-call | tf_op jit(solution)/shard_map/bottom_layer/pallas_call | solution.py:1013
  188.9 24.2 %share_sums.1 = (bf16[32,16,384]{2,1,0:T(8,128)(2,1)}, bf16[32,16,128]{2,1,0:T(8,128)(2,1)}) custom-call(bf16[16,384]{1,0:T(8,128)(2,1)} %get-tuple-element.97.early_ref, bf16[32,16,128]{2,1,0:T(8,128)(2,1)} %bitcast.41), custom_call_target="tpu_custom_call" | custom-call | tf_op jit(solution)/shard_map/share_sums/pallas_call | solution.py:1096
  213.1 0.0 copy-done
  213.1 0.7 copy.43
  213.8 0.0 copy-done.1
  213.8 0.6 reshape.95.bias_first
  214.4 0.0 copy-done.2
  214.4 0.6 reshape.96.bias_second
  215.0 8.4 %adam.1 = (f32[200,256]{1,0:T(8,128)}, f32[200,256]{1,0:T(8,128)}, f32[200,256]{1,0:T(8,128)}, f32[512,256]{1,0:T(8,128)}, f32[512,256]{1,0:T(8,128)}, /*index=5...) custom-call(bf16[512,384]{1,0:T(8,128)(2,1)} %bitcast.32, ...), custom_call_target="tpu_custom_call" | custom-call | tf_op jit(solution)/shard_map/adam/pallas_call | solution.py:1238
  223.4 1.3 reduce
  224.6 1.3 reduce.1
  225.9 1.3 reduce.2
  227.2 1.2 fusion
Async XLA Ops:
  172.4 40.7 %copy-start = (f32[47,47]{1,0:T(8,128)S(1)}, f32[47,47]{1,0:T(8,128)}, u32[]{:S(2)}) copy-start(f32[47,47]{1,0:T(8,128)} %param.42) | copy-start | bytes 26512
  172.4 41.4 %copy-start.1 = (f32[559]{0:T(1024)S(1)}, f32[559]{0:T(1024)}, u32[]{:S(2)}) copy-start(f32[559]{0:T(1024)} %param.50) | copy-start | bytes 6712
  172.4 42.0 %copy-start.2 = (f32[559]{0:T(1024)S(1)}, f32[559]{0:T(1024)}, u32[]{:S(2)}) copy-start(f32[559]{0:T(1024)} %param.51) | copy-start | bytes 6712
where the time goes:
time: 229 us; the launch traced here: 228 us
  Pallas kernels  215 us (94%)
  local copies, waits for them, and re-layouts  9.11 us (4%)
  other arithmetic  3.81 us (2%)
    pallas_call x3, Pallas kernels, count_words(): pl.pallas_call(functools.partial(words_kernel, mesh_sizes, kind), grid=(n...  47.3 us
    pallas_call x2, Pallas kernels, scatter_layer(): pl.pallas_call(functools.partial(scatter_kernel, mesh_sizes, fanout, flip...  43.4 us
    pallas_call x2, Pallas kernels, hidden_layer(): pl.pallas_call(functools.partial(hidden_kernel, fanout, bias_start), grid...  40.6 us
    pallas_call x1, Pallas kernels, share_sums(): pl.pallas_call(functools.partial(share_kernel, mesh_sizes), in_specs=[vme...  24.2 us
    pallas_call x1, Pallas kernels, last_layer(): pl.pallas_call(functools.partial(last_kernel, fanout, bias_start), grid=(...  21.8 us
    pallas_call x1, Pallas kernels, bottom_layer(): pl.pallas_call(functools.partial(bottom_kernel, mesh_sizes), grid=(nodes...  16.5 us
    pallas_call x1, Pallas kernels, middle_layer(): pl.pallas_call(functools.partial(middle_kernel, fanout), grid=(nodes // B...  12.6 us
    pallas_call x1, Pallas kernels, adam(): pl.pallas_call(functools.partial(adam_kernel, padded), in_specs=[vmem] *...  8.4 us

commit v1 on v0

v1 whole, which is shorter than its diff:
```python
import functools

import jax
import jax.numpy as jnp
from jax import lax
from jax.experimental import pallas as pl
from jax.experimental.pallas import tpu as pltpu
from jax.sharding import PartitionSpec as P

STEP = 10


beta_one = 0.9
beta_two = 0.999
epsilon = 1e-08
step_rates = (0.05, 0.5, 1.0)
bias_rate = 0.05
weight_decay = 0.01

axes = ("dom", "rep")
WORDS = 4
SLOTS = 8
RUN = 48
UNIT = SLOTS * RUN
BLOCK = 512
MIB = 1024 * 1024
TRANS_LEFT = (((0,), (0,)), ((), ()))
TRANS_RIGHT = (((1,), (1,)), ((), ()))


def dot(left, right, dims=(((1,), (0,)), ((), ()))):
    return lax.dot_general(left, right, dims, preferred_element_type=jnp.float32)


def params(limit, collective=None):
    remote = {} if collective is None else dict(collective_id=collective, has_side_effects=True)
    return pltpu.CompilerParams(
        dimension_semantics=("arbitrary",), vmem_limit_bytes=limit * MIB, **remote
    )


def in_hbm(*arrays):
    return [pltpu.with_memory_space_constraint(array, pltpu.HBM) for array in arrays]


def whole(shape):
    return pl.BlockSpec(shape, lambda i: (0,) * len(shape))


def lanes(rows, width):
    return pl.BlockSpec((rows, width), lambda i: (0, i))


def floor_over(value, size):
    return ((value.astype(jnp.float32) + 0.5) * (1.0 / size)).astype(jnp.int32)


def words_layer(near_ref, out_ref, place_ref, field_ref):
    fanout, block = near_ref.shape
    span = out_ref.shape[0] // WORDS
    near = near_ref[...]
    unit = floor_over(near, UNIT)
    rest = near - unit * UNIT
    slot = floor_over(rest, RUN)
    word = floor_over(unit, span // RUN)
    place = (unit - word * (span // RUN)) * RUN + rest - slot * RUN
    bit = jnp.left_shift(jnp.int32(1), slot * 4)
    parts = [jnp.where(word == k, bit, 0) for k in range(WORDS)]
    totals = [jnp.zeros_like(bit) for _ in range(WORDS)]
    for g in range(fanout):
        same = place == place[g : g + 1]
        for k in range(WORDS):
            totals[k] = totals[k] + jnp.where(same, parts[k][g : g + 1], 0)
    place_ref[:fanout, :] = place
    for k in range(WORDS):
        field_ref[k, :fanout, :] = totals[k]
    chunk = RUN
    for tile in range(0, block, 128):
        cols = slice(tile, tile + 128)
        for start in range(0, span, chunk):
            rows = lax.broadcasted_iota(jnp.int32, (chunk, 128), 0) + start
            sums = [jnp.zeros((chunk, 128), jnp.int32) for _ in range(WORDS)]
            for g in range(fanout):
                hit = rows == place_ref[g : g + 1, cols]
                for k in range(WORDS):
                    sums[k] = jnp.where(hit, field_ref[k, g : g + 1, cols], sums[k])
            for k in range(WORDS):
                out_ref[k * span + start : k * span + start + chunk, cols] = sums[k]


def my_index(mesh_sizes):
    return lax.axis_index(axes[0]) * mesh_sizes[1] + lax.axis_index(axes[1])


def each_peer(mesh_sizes, act):
    across, along = mesh_sizes
    row, column = lax.axis_index(axes[0]), lax.axis_index(axes[1])

    def wrapped(value, size):
        return jnp.where(value >= size, value - size, value)

    def line(down, carry):
        other = wrapped(row + down, across)
        for ahead in range(along):
            place = wrapped(column + ahead, along)
            act(other * along + place, (other, place))
        return carry

    for ahead in range(1, along):
        place = wrapped(column + ahead, along)
        act(row * along + place, (row, place))
    lax.fori_loop(1, across, line, 0)


def greet(mesh_sizes):
    barrier = pltpu.get_barrier_semaphore()

    def tell(index, where):
        pl.semaphore_signal(
            barrier, inc=1, device_id=where, device_id_type=pl.DeviceIdType.MESH
        )

    each_peer(mesh_sizes, tell)


def all_greeted(mesh_sizes):
    pl.semaphore_wait(pltpu.get_barrier_semaphore(), mesh_sizes[0] * mesh_sizes[1] - 1)


def send_blocks(mesh_sizes, out_ref, in_ref, send_sem, recv_sem):
    me = my_index(mesh_sizes)

    def send(index, where):
        pltpu.make_async_remote_copy(
            src_ref=out_ref.at[index],
            dst_ref=in_ref.at[me],
            send_sem=send_sem,
            recv_sem=recv_sem,
            device_id=where,
            device_id_type=pl.DeviceIdType.MESH,
        ).start()

    each_peer(mesh_sizes, send)


def send_all(mesh_sizes, own_ref, in_ref, send_sem, recv_sem):
    me = my_index(mesh_sizes)

    def send(index, where):
        pltpu.make_async_remote_copy(
            src_ref=own_ref,
            dst_ref=in_ref.at[me],
            send_sem=send_sem,
            recv_sem=recv_sem,
            device_id=where,
            device_id_type=pl.DeviceIdType.MESH,
        ).start()

    each_peer(mesh_sizes, send)


def wait_moves(mesh_sizes, out_ref, in_ref, send_sem, recv_sem):
    others = pl.ds(0, mesh_sizes[0] * mesh_sizes[1] - 1)
    copy = pltpu.make_async_remote_copy(
        src_ref=in_ref.at[others],
        dst_ref=in_ref.at[others],
        send_sem=send_sem,
        recv_sem=recv_sem,
        device_id=(lax.axis_index(axes[0]), lax.axis_index(axes[1])),
        device_id_type=pl.DeviceIdType.MESH,
    )
    copy.wait_send()
    copy.wait_recv()


def semaphores():
    return [pltpu.SemaphoreType.DMA, pltpu.SemaphoreType.DMA]


def chosen_nodes(send_row, start, count):
    node = lax.broadcasted_iota(jnp.int32, (count, send_row.shape[1]), 0) + start
    return jnp.where(node == send_row, 1.0, 0.0).astype(jnp.bfloat16)


def words_kernel(mesh_sizes, kind, near_ref, *refs):
    refs = list(refs)
    if kind == "features":
        feats_ref, send_ref, out_ref, got_ref, sent_ref = refs[:5]
        refs = refs[5:]
    elif kind == "seeds":
        sent_ref, slots_ref, labels_ref, mask_ref, out_ref, got_ref, seeds_ref = refs[:7]
        refs = refs[7:]
    else:
        sent_ref, out_ref, got_ref = refs[:3]
        refs = refs[3:]
    place_ref, field_ref, land_ref, send_sem, recv_sem = refs
    step = pl.program_id(0)
    block = near_ref.shape[1]
    moves = (mesh_sizes, sent_ref, land_ref, send_sem, recv_sem)

    @pl.when(step == 0)
    def _():
        greet(mesh_sizes)

    if kind == "features":

        @pl.when(step == 0)
        def _():
            width, nodes = feats_ref.shape
            halo = send_ref.shape[1]
            total = jnp.zeros((width, halo), jnp.float32)
            for start in range(0, nodes, block):
                chosen = chosen_nodes(send_ref[...], start, block)
                total = total + dot(feats_ref[:, start : start + block], chosen)
            padded = sent_ref.shape[2]
            total = jnp.concatenate([total, jnp.zeros((padded - width, halo), jnp.float32)])
            sent_ref[...] = total.T.astype(jnp.bfloat16).reshape(sent_ref.shape)

    if kind == "seeds":
        classes = seeds_ref.shape[0]
        slots = slots_ref.shape[1]
        label = lax.broadcasted_iota(jnp.int32, (classes, slots), 0)
        marked = jnp.where((label == labels_ref[...]) & (mask_ref[...] != 0), 1.0, 0.0)
        chosen = chosen_nodes(slots_ref[...], step * block, block)
        seeds_ref[...] = dot(marked.astype(jnp.bfloat16), chosen, TRANS_RIGHT)

    words_layer(near_ref, out_ref, place_ref, field_ref)

    @pl.when(step == 0)
    def _():
        all_greeted(mesh_sizes)
        send_blocks(*moves)

    @pl.when(step == pl.num_programs(0) - 1)
    def _():
        me = my_index(mesh_sizes)
        wait_moves(*moves)
        land_ref[me] = sent_ref[me]
        got_ref[...] = land_ref[...]


def count_words(near, mesh_sizes, collective, halo, sent=None, feats=None, send_row=None, seeds=None):
    fanout, nodes = near.shape
    parts = mesh_sizes[0] * mesh_sizes[1]
    height = (nodes + halo) // SLOTS
    in_specs = [lanes(fanout, BLOCK)]
    operands = [near]
    scratch = []
    if sent is None:
        kind = "features"
        blocks = (parts, halo // parts, -(-feats.shape[0] // 128) * 128)
        in_specs += [whole(feats.shape), whole(send_row.shape)]
        operands += [*in_hbm(feats), send_row]
        scratch.append(pltpu.VMEM(blocks, jnp.bfloat16))
    else:
        kind = "plain"
        blocks = (parts, halo // parts, sent.shape[1])
        in_specs.append(whole(blocks))
        operands.append(sent.reshape(blocks))
    out_specs = [lanes(height, BLOCK), whole(blocks)]
    out_shape = [
        pltpu.HBM((height, nodes), jnp.int32),
        jax.ShapeDtypeStruct(blocks, jnp.bfloat16),
    ]
    if seeds is not None:
        kind = "seeds"
        classes, slots, labels, mask = seeds
        in_specs += [whole(slots.shape)] * 3
        operands += [slots, labels, mask]
        out_specs.append(lanes(classes, BLOCK))
        out_shape.append(jax.ShapeDtypeStruct((classes, nodes), jnp.float32))
    return pl.pallas_call(
        functools.partial(words_kernel, mesh_sizes, kind),
        grid=(nodes // BLOCK,),
        in_specs=in_specs,
        out_specs=out_specs,
        out_shape=out_shape,
        scratch_shapes=scratch
        + [
            pltpu.VMEM((16, BLOCK), jnp.int32),
            pltpu.VMEM((WORDS, 16, BLOCK), jnp.int32),
            pltpu.VMEM(blocks, jnp.bfloat16),
        ]
        + semaphores(),
        compiler_params=params(20, collective),
        name="count_words",
    )(*in_hbm(*operands[:1]), *operands[1:])


def field(words, slot):
    if slot == SLOTS - 1:
        picked = lax.shift_right_logical(words, 4 * slot)
    else:
        picked = words & (15 << (4 * slot))
    return picked.astype(jnp.float32).astype(jnp.bfloat16)


def slot_scale(slot):
    return 1.0 if slot == SLOTS - 1 else 2.0 ** (-4 * slot)


def spread_unit(words_ref, word_row, counts_ref, count_row):
    for start in range(0, RUN, 16):
        for tile in range(0, words_ref.shape[1], 256):
            cols = slice(tile, tile + 256)
            words = words_ref[word_row + start : word_row + start + 16, cols]
            for slot in range(SLOTS):
                row = count_row + slot * RUN + start
                counts_ref[row : row + 16, cols] = field(words, slot)


def gather_product(table_ref, words_ref, counts_ref):
    table = table_ref.shape[1]
    total = None
    for start in range(0, table, 2 * UNIT):
        stop = start + 2 * UNIT
        for row in range(start, stop, UNIT):
            spread_unit(words_ref, row // SLOTS, counts_ref, row)
        term = dot(table_ref[:, start:stop], counts_ref[start:stop, :])
        total = term if total is None else total + term
    return total


def scale_row(table):
    column = lax.broadcasted_iota(jnp.int32, (1, table), 1)
    rest = column - floor_over(column, UNIT) * UNIT
    slot = floor_over(rest, RUN)
    scale = jnp.ones((1, table), jnp.float32)
    for k in range(SLOTS - 1):
        scale = jnp.where(slot == k, slot_scale(k), scale)
    return scale


def column_of(row):
    return jnp.broadcast_to(row, (128, row.shape[1])).T


def late(rows, width):
    return pl.BlockSpec((rows, width), lambda i: (0, jnp.maximum(i - 1, 0)))


def now(rows, width, steps):
    return pl.BlockSpec((rows, width), lambda i: (0, jnp.minimum(i, steps - 1)))


def hidden_kernel(
    fanout,
    bias_start,
    words_ref,
    own_ref,
    own_block,
    got_ref,
    weight_ref,
    bias_ref,
    send_ref,
    state_ref,
    preact_ref,
    sent_ref,
    extra_ref,
    table_ref,
    counts_ref,
    picked_ref,
    mean_ref,
    self_ref,
    near_ref,
    bias_col,
):
    step = pl.program_id(0)
    last = pl.num_programs(0) - 1
    width, nodes = own_ref.shape
    units, block = state_ref.shape
    padded = mean_ref.shape[0]

    @pl.when(step == 0)
    def _():
        if table_ref.shape[0] > width:
            table_ref[...] = jnp.zeros_like(table_ref)
        got = got_ref[...].reshape(-1, got_ref.shape[2]).T[:width]
        scale = scale_row(table_ref.shape[1])
        own = own_ref[...].astype(jnp.float32) * scale[:, :nodes]
        table_ref[:width, :nodes] = own.astype(jnp.bfloat16)
        far = got.astype(jnp.float32) * scale[:, nodes:]
        table_ref[:width, nodes:] = far.astype(jnp.bfloat16)
        mean_ref[...] = jnp.zeros_like(mean_ref)
        picked_ref[...] = jnp.zeros_like(picked_ref)
        self_ref[...] = weight_ref[:width, :].T.astype(jnp.bfloat16)
        if padded > width:
            near_ref[...] = jnp.zeros_like(near_ref)
        near_ref[:, :width] = weight_ref[width:, :].T.astype(jnp.bfloat16)
        bias = bias_ref[...].reshape(1, -1)
        bias_col[...] = column_of(bias[:, bias_start : bias_start + units])

    def finish():
        mean = mean_ref[...]
        extra_ref[...] = mean
        preact = dot(self_ref[...], own_block[...]) + dot(near_ref[...], mean) + bias_col[:, :1]
        preact_ref[...] = preact
        active = preact * jax.nn.sigmoid(preact)
        norm = lax.rsqrt(jnp.sum(active * active, axis=0, keepdims=True) + 1e-06)
        state = (active * norm).astype(jnp.bfloat16)
        state_ref[...] = state
        picked_ref[...] += dot(state, chosen_nodes(send_ref[...], (step - 1) * block, block))

    @pl.when(step < last)
    def _():
        finish()
        total = gather_product(table_ref, words_ref, counts_ref)
        mean_ref[...] = (total / fanout).astype(jnp.bfloat16)

    @pl.when(step == last)
    def _():
        finish()
        sent_ref[...] = picked_ref[...].T.astype(jnp.bfloat16)


def hidden_layer(words, own, got, weight, bias, bias_start, send_row, fanout):
    width, nodes = own.shape
    halo = send_row.shape[1]
    table = nodes + halo
    units = weight.shape[1]
    padded = -(-width // 16) * 16
    steps = nodes // BLOCK
    return pl.pallas_call(
        functools.partial(hidden_kernel, fanout, bias_start),
        grid=(steps + 1,),
        in_specs=[
            now(words.shape[0], BLOCK, steps),
            whole(own.shape),
            late(width, BLOCK),
            whole(got.shape),
            whole(weight.shape),
            whole(bias.shape),
            whole(send_row.shape),
        ],
        out_specs=[
            late(units, BLOCK),
            late(units, BLOCK),
            whole((halo, units)),
            late(padded, BLOCK),
        ],
        out_shape=[
            jax.ShapeDtypeStruct((units, nodes), jnp.bfloat16),
            pltpu.HBM((units, nodes), jnp.float32),
            jax.ShapeDtypeStruct((halo, units), jnp.bfloat16),
            pltpu.HBM((padded, nodes), jnp.bfloat16),
        ],
        scratch_shapes=[
            pltpu.VMEM((padded, table), jnp.bfloat16),
            pltpu.VMEM((table, BLOCK), jnp.bfloat16),
            pltpu.VMEM((units, halo), jnp.float32),
            pltpu.VMEM((padded, BLOCK), jnp.bfloat16),
            pltpu.VMEM((units, width), jnp.bfloat16),
            pltpu.VMEM((units, padded), jnp.bfloat16),
            pltpu.VMEM((units, 128), jnp.float32),
        ],
        compiler_params=params(28),
        name="hidden_layer",
    )(*in_hbm(words), own, own, got, *in_hbm(weight, bias), send_row)


def far_start(nodes):
    return nodes // UNIT * UNIT


def unscaled(sums, fanout):
    pieces = []
    for row in range(0, sums.shape[0], RUN):
        slot = row // RUN % SLOTS
        pieces.append((sums[row : row + RUN] * (slot_scale(slot) / fanout)).astype(jnp.bfloat16))
    return jnp.concatenate(pieces)


def last_kernel(
    fanout,
    bias_start,
    words_ref,
    own_ref,
    own_block,
    got_ref,
    weight_ref,
    bias_ref,
    seeds_ref,
    grad_ref,
    rows_ref,
    sums_ref,
    notes_ref,
    table_out,
    far_ref,
    halo_ref,
    reduced_ref,
    counts_ref,
    both_ref,
    self_ref,
    near_ref,
    bias_col,
    far_sums,
):
    step = pl.program_id(0)
    last = pl.num_programs(0) - 1
    classes = self_ref.shape[0]
    width, nodes = own_ref.shape
    kinds = weight_ref.shape[0]
    halo = far_ref.shape[0]
    first = far_start(nodes)

    @pl.when(step == 0)
    def _():
        table_out[:, :nodes] = own_ref[...]
        table_out[:, nodes:] = got_ref[...].reshape(halo, width).T
        more = jnp.zeros((classes - kinds, 2 * width), jnp.float32)
        weight = jnp.concatenate([weight_ref[...], more]).astype(jnp.bfloat16)
        self_ref[...] = weight[:, :width]
        near_ref[...] = weight[:, width:]
        rest = jnp.full((1, classes - kinds), -1e30, jnp.float32)
        bias = bias_ref[...].reshape(1, -1)
        bias_col[...] = column_of(
            jnp.concatenate([bias[:, bias_start : bias_start + kinds], rest], axis=1)
        )
        reduced = dot(near_ref[...], table_out[...]) * scale_row(table_out.shape[1])
        high = reduced.astype(jnp.bfloat16)
        reduced_ref[:classes, :] = high
        reduced_ref[classes:, :] = (reduced - high.astype(jnp.float32)).astype(jnp.bfloat16)
        both_ref[...] = jnp.zeros_like(both_ref)
        counts_ref[first:, :] = jnp.zeros_like(counts_ref[first:, :])

    @pl.when(step <= 1)
    def _():
        sums_ref[...] = jnp.zeros_like(sums_ref)
        notes_ref[...] = jnp.zeros_like(notes_ref)
        far_sums[...] = jnp.zeros_like(far_sums)

    def finish():
        near_part = (both_ref[:classes, :] + both_ref[classes:, :]) / fanout
        logits = dot(self_ref[...], own_block[...]) + near_part + bias_col[:, :1]
        top = jnp.max(logits, axis=0, keepdims=True)
        powers = jnp.exp(logits - top)
        total = jnp.sum(powers, axis=0, keepdims=True)
        normer = jnp.log(total) + top
        seeds = seeds_ref[...]
        uses = jnp.sum(seeds, axis=0, keepdims=True)
        grad = (powers / total * uses - seeds).astype(jnp.bfloat16)
        grad_ref[...] = grad
        loss = uses * normer - jnp.sum(seeds * logits, axis=0, keepdims=True)
        sums_ref[...] += jnp.sum(grad.astype(jnp.float32), axis=1, keepdims=True)
        notes_ref[:8, :] += jnp.sum(loss)
        notes_ref[8:, :] += jnp.sum(uses)
        rows = grad.T
        rows_ref[...] = rows
        far_sums[...] += dot(counts_ref[first:, :], rows)

    @pl.when(step < last)
    def _():
        finish()
        both_ref[...] = gather_product(reduced_ref, words_ref, counts_ref)

    @pl.when(step == last)
    def _():
        finish()
        sums = unscaled(far_sums[...], fanout)[nodes - first :]
        far_ref[...] = sums
        halo_ref[...] = dot(sums, near_ref[...]).astype(jnp.bfloat16)


def last_layer(words, own, got, weight, bias, bias_start, seeds, fanout):
    width, nodes = own.shape
    halo = got.shape[0] * got.shape[1]
    table = nodes + halo
    classes = seeds.shape[0]
    steps = nodes // BLOCK
    far_height = table - far_start(nodes)
    return pl.pallas_call(
        functools.partial(last_kernel, fanout, bias_start),
        grid=(steps + 1,),
        in_specs=[
            now(words.shape[0], BLOCK, steps),
            whole(own.shape),
            late(width, BLOCK),
            whole(got.shape),
            whole(weight.shape),
            whole(bias.shape),
            late(classes, BLOCK),
        ],
        out_specs=[
            late(classes, BLOCK),
            pl.BlockSpec((BLOCK, classes), lambda i: (jnp.maximum(i - 1, 0), 0)),
            whole((classes, 128)),
            whole((16, 128)),
            whole((width, table)),
            whole((halo, classes)),
            whole((halo, width)),
        ],
        out_shape=[
            jax.ShapeDtypeStruct((classes, nodes), jnp.bfloat16),
            jax.ShapeDtypeStruct((nodes, classes), jnp.bfloat16),
            jax.ShapeDtypeStruct((classes, 128), jnp.float32),
            jax.ShapeDtypeStruct((16, 128), jnp.float32),
            jax.ShapeDtypeStruct((width, table), jnp.bfloat16),
            jax.ShapeDtypeStruct((halo, classes), jnp.bfloat16),
            jax.ShapeDtypeStruct((halo, width), jnp.bfloat16),
        ],
        scratch_shapes=[
            pltpu.VMEM((2 * classes, table), jnp.bfloat16),
            pltpu.VMEM((table, BLOCK), jnp.bfloat16),
            pltpu.VMEM((2 * classes, BLOCK), jnp.float32),
            pltpu.VMEM((classes, width), jnp.bfloat16),
            pltpu.VMEM((classes, width), jnp.bfloat16),
            pltpu.VMEM((classes, 128), jnp.float32),
            pltpu.VMEM((far_height, classes), jnp.float32),
        ],
        compiler_params=params(28),
        name="last_layer",
    )(*in_hbm(words), own, own, got, *in_hbm(weight, bias), seeds)


def scatter_kernel(mesh_sizes, fanout, flipped, words_ref, grad_ref, rows_ref, *refs):
    refs = list(refs)
    if flipped:
        weight_in, halo_ref, far_ref, table_ref, far_table = refs[:5]
        state_ref, got_ref, weight_ref = refs[5:8]
        padded_ref, counts_ref, sums_ref, self_ref, near_ref, land_ref = refs[8:14]
        send_sem, recv_sem = refs[14:]
    else:
        weight_in, halo_ref, early_ref = refs[:3]
        state_ref, got_ref, early_sum, notes_ref = refs[3:7]
        padded_ref, counts_ref, sums_ref, self_ref, near_ref, land_ref = refs[7:13]
        early_land, send_sem, recv_sem, early_send, early_recv = refs[13:]
        early_moves = (mesh_sizes, early_ref, early_land, early_send, early_recv)
    step = pl.program_id(0)
    units, nodes = grad_ref.shape
    width = state_ref.shape[0]
    span = words_ref.shape[0]
    part = span * SLOTS
    steps = -(-nodes // part)
    moves = (mesh_sizes, halo_ref, land_ref, send_sem, recv_sem)

    @pl.when(step == 0)
    def _():
        greet(mesh_sizes)
        for k in range(steps):
            start = k * part
            stop = min(start + part, nodes)
            padded_ref[k, :, : stop - start] = grad_ref[:, start:stop]
            if stop < start + part:
                padded_ref[k, :, stop - start :] = jnp.zeros(
                    (units, start + part - stop), jnp.bfloat16
                )
        weight = weight_in[...]
        if flipped:
            more = jnp.zeros((units - weight.shape[0], 2 * width), jnp.float32)
            weight = jnp.concatenate([weight, more]).T
            weight_ref[:width, :] = jnp.zeros((width, units), jnp.float32)
            weight_ref[width:, :] = dot(far_table[...], far_ref[...])
        self_ref[...] = weight[:width].astype(jnp.bfloat16)
        near_ref[...] = weight[width:].astype(jnp.bfloat16)
        sums_ref[...] = jnp.zeros_like(sums_ref)
        all_greeted(mesh_sizes)
        send_blocks(*moves)
        if not flipped:
            send_blocks(*early_moves)

    def add(row):
        spread_unit(words_ref, row // SLOTS, counts_ref, row)
        added = dot(counts_ref[row : row + UNIT, :], rows_ref[...])
        sums_ref[row : row + UNIT, :] = unscaled(added, fanout)

    beyond = nodes - (steps - 1) * part
    ending = -(-beyond // UNIT) * UNIT
    for row in range(0, ending, UNIT):
        add(row)
    if ending < part:

        @pl.when(step < steps - 1)
        def _():
            for row in range(ending, part, UNIT):
                add(row)

    if flipped and beyond < part:

        @pl.when(step == steps - 1)
        def _():
            sums_ref[beyond:, :] = jnp.zeros((part - beyond, units), jnp.bfloat16)

    sums = sums_ref[...]
    own_grad = padded_ref[step]
    state_ref[...] = dot(near_ref[...], sums, TRANS_RIGHT) + dot(self_ref[...], own_grad)
    if flipped:
        weight_ref[:width, :] += dot(table_ref[...], own_grad, TRANS_RIGHT)
        weight_ref[width:, :] += dot(table_ref[...], sums)

    @pl.when(step == steps - 1)
    def _():
        me = my_index(mesh_sizes)
        wait_moves(*moves)
        land_ref[me] = halo_ref[me]
        got_ref[...] = land_ref[...]
        if not flipped:
            wait_moves(*early_moves)
            early_land[me] = early_ref[me]
            total = jnp.sum(early_land[...].astype(jnp.float32), axis=0)
            early_sum[...] = total.astype(jnp.bfloat16)
            lane = lax.broadcasted_iota(jnp.int32, (8, 128), 1)
            row = lax.broadcasted_iota(jnp.int32, (8, 128), 0)
            last = jnp.broadcast_to(total[:1, -128:], (8, 128))
            for index in range(2):
                mine = (lane >= 120 + 3 * index) & (lane < 123 + 3 * index)
                note = jnp.sum(jnp.where(mine & (row == 0), last, 0.0))
                notes_ref[index] = jnp.full((1, 1), note, jnp.float32)


def scatter_layer(
    words, grad, rows, weight, halo_rows, mesh_sizes, collective, fanout, tables=None, early=None
):
    units, nodes = grad.shape
    halo, width = halo_rows.shape
    parts = mesh_sizes[0] * mesh_sizes[1]
    flipped = tables is not None
    total = nodes + halo
    part = total // WORDS
    span = part // SLOTS
    steps = -(-nodes // part)
    blocks = (parts, halo // parts, width)
    in_specs = [
        pl.BlockSpec((span, nodes), lambda i: (i, 0)),
        whole(grad.shape),
        whole(rows.shape),
        whole(weight.shape),
        whole(blocks),
    ]
    operands = [words, grad, rows, weight, halo_rows.reshape(blocks)]
    out_specs = [lanes(width, part), whole(blocks)]
    out_shape = [
        jax.ShapeDtypeStruct((width, total), jnp.float32),
        jax.ShapeDtypeStruct(blocks, jnp.bfloat16),
    ]
    if flipped:
        far, table = tables
        in_specs += [
            whole(far.shape),
            lanes(width, part),
            pl.BlockSpec((width, halo), lambda i: (0, nodes // halo)),
        ]
        operands += [far, table, table]
        out_specs.append(whole((2 * width, units)))
        out_shape.append(jax.ShapeDtypeStruct((2 * width, units), jnp.float32))
        scratch = semaphores()
    else:
        early_blocks = (parts, early.shape[0] // parts, early.shape[1])
        in_specs.append(whole(early_blocks))
        operands.append(early.reshape(early_blocks))
        out_specs += [whole(early_blocks[1:]), whole((2, 1, 1))]
        out_shape += [
            jax.ShapeDtypeStruct(early_blocks[1:], jnp.bfloat16),
            jax.ShapeDtypeStruct((2, 1, 1), jnp.float32),
        ]
        scratch = [pltpu.VMEM(early_blocks, jnp.bfloat16)] + semaphores() + semaphores()
    return pl.pallas_call(
        functools.partial(scatter_kernel, mesh_sizes, fanout, flipped),
        grid=(steps,),
        in_specs=in_specs,
        out_specs=out_specs,
        out_shape=out_shape,
        scratch_shapes=[
            pltpu.VMEM((steps, units, part), jnp.bfloat16),
            pltpu.VMEM((part, nodes), jnp.bfloat16),
            pltpu.VMEM((part, units), jnp.bfloat16),
            pltpu.VMEM((width, units), jnp.bfloat16),
            pltpu.VMEM((width, units), jnp.bfloat16),
            pltpu.VMEM(blocks, jnp.bfloat16),
        ]
        + scratch,
        compiler_params=params(36, collective),
        name="scatter_layer",
    )(*in_hbm(words), *operands[1:3], *in_hbm(weight), *operands[4:])


def active_grad(step, state_ref, preact_ref, back_ref, send_ref):
    block = state_ref.shape[1]
    chosen = chosen_nodes(send_ref[...], step * block, block)
    upper = state_ref[...] + dot(back_ref[...], chosen, TRANS_RIGHT)
    preact = preact_ref[...]
    gate = jax.nn.sigmoid(preact)
    active = preact * gate
    norm = lax.rsqrt(jnp.sum(active * active, axis=0, keepdims=True) + 1e-06)
    along = jnp.sum(active * upper, axis=0, keepdims=True)
    inner = norm * upper - active * (norm * norm * norm * along)
    return (inner * (gate * (1.0 + preact * (1.0 - gate)))).astype(jnp.bfloat16)


def middle_kernel(
    fanout,
    state_ref,
    preact_ref,
    returned_ref,
    send_ref,
    words_ref,
    weight_ref,
    own_block,
    mean_block,
    above_ref,
    notes_ref,
    grad_ref,
    rows_ref,
    sums_ref,
    halo_ref,
    early_ref,
    back_ref,
    counts_ref,
    far_sums,
    total_ref,
):
    step = pl.program_id(0)
    units, block = state_ref.shape
    halo = halo_ref.shape[0]
    nodes = block * pl.num_programs(0)
    first = far_start(nodes)
    part = (nodes + halo) // WORDS

    @pl.when(step == 0)
    def _():
        back_ref[...] = returned_ref[...].reshape(halo, units).T
        sums_ref[...] = jnp.zeros_like(sums_ref)
        far_sums[...] = jnp.zeros_like(far_sums)
        total_ref[...] = jnp.zeros_like(total_ref)

    base = first // part * part
    for row in range(first, nodes + halo, UNIT):
        spread_unit(words_ref, (row - base) // SLOTS, counts_ref, row - first)
    grad = active_grad(step, state_ref, preact_ref, back_ref, send_ref)
    grad_ref[...] = grad
    sums_ref[...] += jnp.sum(grad.astype(jnp.float32), axis=1, keepdims=True)
    rows = grad.T
    rows_ref[...] = rows
    far_sums[...] += dot(counts_ref[...], rows)
    width = own_block.shape[0]
    total_ref[:width, :] += dot(own_block[...], rows)
    total_ref[width:, :] += dot(mean_block[...], rows)

    @pl.when(step == pl.num_programs(0) - 1)
    def _():
        near = weight_ref[units:, :].T.astype(jnp.bfloat16)
        sums = unscaled(far_sums[...], fanout)[nodes - first :]
        halo_ref[...] = dot(sums, near).astype(jnp.bfloat16)
        early_ref[:, :units] = total_ref[...].astype(jnp.bfloat16)
        height, narrow = above_ref.shape
        above = jnp.concatenate(
            [above_ref[...], jnp.zeros((height, 128 - narrow), jnp.float32)], axis=1
        )
        lane = lax.broadcasted_iota(jnp.int32, above.shape, 1)
        for index in range(2):
            value = notes_ref[8 * index : 8 * index + 1, 0:1]
            for at in range(3):
                term = value.astype(jnp.bfloat16).astype(jnp.float32)
                above = jnp.where(lane == 120 + 3 * index + at, term, above)
                value = value - term
        early_ref[:, units:] = above.astype(jnp.bfloat16)


def middle_layer(
    state_grad, preact, returned, send_row, words, weight, own, mean, above, notes, fanout
):
    units, nodes = preact.shape
    width = own.shape[0]
    wide = units + 128
    halo = send_row.shape[1]
    part = (nodes + halo) // WORDS
    span = part // SLOTS
    far_words = WORDS - far_start(nodes) // part
    far_height = nodes + halo - far_start(nodes)
    return pl.pallas_call(
        functools.partial(middle_kernel, fanout),
        grid=(nodes // BLOCK,),
        in_specs=[
            lanes(units, BLOCK),
            lanes(units, BLOCK),
            whole(returned.shape),
            whole(send_row.shape),
            pl.BlockSpec((far_words * span, BLOCK), lambda i: (WORDS // far_words - 1, i)),
            whole(weight.shape),
            lanes(width, BLOCK),
            lanes(width, BLOCK),
            whole(above.shape),
            whole(notes.shape),
        ],
        out_specs=[
            lanes(units, BLOCK),
            pl.BlockSpec((BLOCK, units), lambda i: (i, 0)),
            whole((units, 128)),
            whole((halo, units)),
            whole((2 * width, wide)),
        ],
        out_shape=[
            jax.ShapeDtypeStruct((units, nodes), jnp.bfloat16),
            jax.ShapeDtypeStruct((nodes, units), jnp.bfloat16),
            jax.ShapeDtypeStruct((units, 128), jnp.float32),
            jax.ShapeDtypeStruct((halo, units), jnp.bfloat16),
            jax.ShapeDtypeStruct((2 * width, wide), jnp.bfloat16),
        ],
        scratch_shapes=[
            pltpu.VMEM((units, halo), jnp.bfloat16),
            pltpu.VMEM((far_height, BLOCK), jnp.bfloat16),
            pltpu.VMEM((far_height, units), jnp.float32),
            pltpu.VMEM((2 * width, units), jnp.float32),
        ],
        compiler_params=params(26),
        name="middle_layer",
    )(
        state_grad,
        *in_hbm(preact),
        returned,
        send_row,
        *in_hbm(words, weight),
        own,
        *in_hbm(mean),
        above,
        notes,
    )


def bottom_kernel(
    mesh_sizes,
    state_ref,
    preact_ref,
    returned_ref,
    send_ref,
    own_block,
    mean_block,
    sums_two,
    sums_three,
    early_ref,
    late_ref,
    early_all,
    back_ref,
    sums_ref,
    weight_ref,
    land_ref,
    send_sem,
    recv_sem,
):
    step = pl.program_id(0)
    units = state_ref.shape[0]
    halo = send_ref.shape[1]
    moves = (mesh_sizes, early_ref, land_ref, send_sem, recv_sem)

    @pl.when(step == 0)
    def _():
        greet(mesh_sizes)
        back_ref[...] = returned_ref[...].reshape(halo, units).T
        sums_ref[...] = jnp.zeros_like(sums_ref)
        weight_ref[...] = jnp.zeros_like(weight_ref)
        all_greeted(mesh_sizes)
        send_all(*moves)

    grad = active_grad(step, state_ref, preact_ref, back_ref, send_ref)
    sums_ref[...] += jnp.sum(grad.astype(jnp.float32), axis=1, keepdims=True)
    width = own_block.shape[0]
    weight_ref[0, :width, :] += dot(own_block[...], grad, TRANS_RIGHT)
    weight_ref[1] += dot(mean_block[...], grad, TRANS_RIGHT)

    @pl.when(step == pl.num_programs(0) - 1)
    def _():
        me = my_index(mesh_sizes)
        padded = weight_ref.shape[1]
        row = 0
        for start in range(0, units, 128):
            for half in range(2):
                late_ref[row : row + padded, :] = weight_ref[half, :, start : start + 128].astype(
                    jnp.bfloat16
                )
                row += padded
        pieces = []
        for sums in (sums_ref, sums_two, sums_three):
            flat = sums[...].T[:1]
            for start in range(0, flat.shape[1], 128):
                piece = flat[:, start : start + 128]
                pieces.append(piece)
        narrow = pieces[-1].shape[1]
        pieces[-1] = jnp.concatenate(
            [pieces[-1], jnp.zeros((1, 128 - narrow), jnp.float32)], axis=1
        )
        rest = late_ref.shape[0] - row
        pieces.append(jnp.zeros((rest - len(pieces), 128), jnp.float32))
        late_ref[row:, :] = jnp.concatenate(pieces).astype(jnp.bfloat16)
        wait_moves(*moves)
        land_ref[me] = early_ref[...]
        early_all[...] = land_ref[...]


def bottom_layer(
    state_grad, preact, returned, send_row, own, mean, sums_two, sums_three, early, mesh_sizes, collective
):
    units, nodes = preact.shape
    width = own.shape[0]
    padded = mean.shape[0]
    halo = send_row.shape[1]
    parts = mesh_sizes[0] * mesh_sizes[1]
    rows = units // 128 * (2 * padded + 2) + -(-sums_three.shape[0] // 128)
    rows = -(-rows // 512) * 512
    rows = -(-rows // parts) * parts
    early_blocks = (parts,) + early.shape
    return pl.pallas_call(
        functools.partial(bottom_kernel, mesh_sizes),
        grid=(nodes // BLOCK,),
        in_specs=[
            lanes(units, BLOCK),
            lanes(units, BLOCK),
            whole(returned.shape),
            whole(send_row.shape),
            lanes(width, BLOCK),
            lanes(padded, BLOCK),
            whole(sums_two.shape),
            whole(sums_three.shape),
            whole(early.shape),
        ],
        out_specs=[whole((rows, 128)), whole(early_blocks)],
        out_shape=[
            jax.ShapeDtypeStruct((rows, 128), jnp.bfloat16),
            jax.ShapeDtypeStruct(early_blocks, jnp.bfloat16),
        ],
        scratch_shapes=[
            pltpu.VMEM((units, halo), jnp.bfloat16),
            pltpu.VMEM((units, 128), jnp.float32),
            pltpu.VMEM((2, padded, units), jnp.float32),
            pltpu.VMEM(early_blocks, jnp.bfloat16),
        ]
        + semaphores(),
        compiler_params=params(24, collective),
        name="bottom_layer",
    )(
        state_grad,
        *in_hbm(preact),
        returned,
        send_row,
        *in_hbm(own, mean),
        sums_two,
        sums_three,
        early,
    )


def in_two(value):
    high = value.astype(jnp.bfloat16)
    return high, (value - high.astype(jnp.float32)).astype(jnp.bfloat16)


def product(left, right, dims=(((1,), (0,)), ((), ()))):
    if left.dtype == jnp.bfloat16:
        high, low = in_two(right)
        return dot(left, high, dims) + dot(left, low, dims)
    high, low = in_two(left)
    if right.dtype == jnp.bfloat16:
        return dot(high, right, dims) + dot(low, right, dims)
    right_high, right_low = in_two(right)
    return dot(high, right_high, dims) + (
        dot(high, right_low, dims) + dot(low, right_high, dims)
    )


def moments(turned, first, second):
    first = beta_one * first + (1.0 - beta_one) * turned
    second = beta_two * second + (1.0 - beta_two) * turned * turned
    update = first / (1.0 - beta_one**STEP) / (jnp.sqrt(second / (1.0 - beta_two**STEP)) + epsilon)
    return first, second, update


def share_kernel(
    mesh_sizes, late_ref, late_out, late_land, late_sum, late_all, send_sem, recv_sem, last_send, last_recv
):
    me = my_index(mesh_sizes)
    inward = (mesh_sizes, late_ref, late_land, send_sem, recv_sem)
    outward = (mesh_sizes, late_sum, late_all, last_send, last_recv)
    greet(mesh_sizes)
    all_greeted(mesh_sizes)
    send_blocks(*inward)
    wait_moves(*inward)
    late_land[me] = late_ref[me]
    late_sum[...] = jnp.sum(late_land[...].astype(jnp.float32), axis=0).astype(jnp.bfloat16)
    send_all(*outward)
    wait_moves(*outward)
    late_all[me] = late_sum[...]
    late_out[...] = late_all[...]


def share_sums(late_rows, mesh_sizes, collective):
    parts = mesh_sizes[0] * mesh_sizes[1]
    late_shape = (parts, late_rows.shape[0] // parts, 128)
    vmem = pl.BlockSpec(memory_space=pltpu.VMEM)
    return pl.pallas_call(
        functools.partial(share_kernel, mesh_sizes),
        in_specs=[vmem],
        out_specs=vmem,
        out_shape=jax.ShapeDtypeStruct(late_shape, jnp.bfloat16),
        scratch_shapes=[
            pltpu.VMEM(late_shape, jnp.bfloat16),
            pltpu.VMEM(late_shape[1:], jnp.bfloat16),
            pltpu.VMEM(late_shape, jnp.bfloat16),
        ]
        + semaphores()
        + semaphores(),
        compiler_params=pltpu.CompilerParams(
            vmem_limit_bytes=8 * MIB, collective_id=collective, has_side_effects=True
        ),
        name="share_sums",
    )(late_rows.reshape(late_shape))


def adam_kernel(
    padded,
    late_ref,
    early_ref,
    notes_ref,
    weight_one,
    weight_two,
    weight_three,
    left_one,
    right_one,
    left_two,
    right_two,
    left_three,
    right_three,
    first_one,
    first_two,
    first_three,
    second_one,
    second_two,
    second_three,
    bias_ref,
    bias_first,
    bias_second,
    *outs,
):
    share = 1.0 / notes_ref[1]
    units = weight_two.shape[1]
    width = weight_one.shape[0] // 2
    kinds = weight_three.shape[0]

    def step(grad, weight, first, second, left, right, rate, out):
        turned = product(product(left[...], grad, TRANS_LEFT), right[...]) * share
        new_first, new_second, update = moments(turned, first[...], second[...])
        out[1][...] = new_first
        out[2][...] = new_second
        moved = product(product(left[...], update), right[...], TRANS_RIGHT)
        out[0][...] = weight[...] - rate * moved

    step(
        early_ref[:, :units],
        weight_two,
        first_two,
        second_two,
        left_two,
        right_two,
        step_rates[1],
        outs[3:6],
    )

    grad = early_ref[:, units:].astype(jnp.float32).T[:kinds].astype(jnp.bfloat16)
    turned = product(right_three[...], product(grad, left_three[...])) * share
    new_first, new_second, update = moments(turned, first_three[...], second_three[...])
    outs[7][...] = new_first
    outs[8][...] = new_second
    moved = product(update, left_three[...], TRANS_RIGHT)
    moved = product(right_three[...], moved, TRANS_LEFT)
    outs[6][...] = weight_three[...] - step_rates[2] * moved

    late_rows = late_ref[...].astype(jnp.float32)
    columns = []
    for start in range(0, units, 128):
        row = start // 128 * 2 * padded
        columns.append(
            jnp.concatenate(
                [late_rows[row : row + width], late_rows[row + padded : row + padded + width]]
            )
        )
    step(
        jnp.concatenate(columns, axis=1).astype(jnp.bfloat16),
        weight_one,
        first_one,
        second_one,
        left_one,
        right_one,
        step_rates[0],
        outs[0:3],
    )
    row = units // 128 * 2 * padded
    pieces = []
    while len(pieces) * 128 < 2 * units + kinds:
        pieces.append(late_rows[row : row + 1])
        row += 1
    grad = jnp.concatenate(pieces, axis=1)[:, : 2 * units + kinds] * share
    flat = bias_ref.shape
    bias, first, second = (ref[...].reshape(grad.shape) for ref in (bias_ref, bias_first, bias_second))
    new_first, new_second, update = moments(grad, first, second)
    outs[9][...] = (bias - bias_rate * (update + weight_decay * bias)).reshape(flat)
    outs[10][...] = new_first.reshape(flat)
    outs[11][...] = new_second.reshape(flat)


def adam(padded, late_all, early_all, notes, *state):
    vmem = pl.BlockSpec(memory_space=pltpu.VMEM)
    order = (0, 9, 12, 1, 10, 13, 2, 11, 14, 15, 16, 17)
    outs = [jax.ShapeDtypeStruct(state[at].shape, jnp.float32) for at in order]
    return pl.pallas_call(
        functools.partial(adam_kernel, padded),
        in_specs=[vmem] * (3 + len(state)),
        out_specs=[vmem] * len(outs),
        out_shape=outs,
        compiler_params=pltpu.CompilerParams(vmem_limit_bytes=32 * MIB),
        name="adam",
    )(late_all, early_all, notes, *in_hbm(*state))


def on_device(
    mesh_sizes,
    features,
    labels,
    seed_rows,
    seed_mask,
    send_rows,
    neighbors_one,
    neighbors_two,
    neighbors_three,
    weight_one,
    weight_two,
    weight_three,
    left_one,
    right_one,
    left_two,
    right_two,
    left_three,
    right_three,
    first_one,
    first_two,
    first_three,
    second_one,
    second_two,
    second_three,
    bias_all,
    bias_first,
    bias_second,
):
    units = weight_one.shape[1]
    classes = weight_three.shape[1]
    halo = send_rows.size
    fans = (neighbors_one.shape[1], neighbors_two.shape[1], neighbors_three.shape[1])
    feats = features.T
    send_row = send_rows.reshape(1, halo)
    weight_three = weight_three.T
    padded_classes = -(-classes // 16) * 16
    seed_slots = (
        padded_classes,
        seed_rows.reshape(1, -1),
        labels.reshape(1, -1),
        seed_mask.reshape(1, -1),
    )

    words_one, got = count_words(
        neighbors_one.T, mesh_sizes, 0, halo, feats=feats, send_row=send_row
    )
    state_one, preact_one, sent, mean_one = hidden_layer(
        words_one, feats, got, weight_one, bias_all, 0, send_row, fans[0]
    )
    words_two, got = count_words(neighbors_two.T, mesh_sizes, 1, halo, sent=sent)
    state_two, preact_two, sent, mean_two = hidden_layer(
        words_two, state_one, got, weight_two, bias_all, units, send_row, fans[1]
    )
    words_three, got, seeds = count_words(
        neighbors_three.T, mesh_sizes, 2, halo, sent=sent, seeds=seed_slots
    )
    grad_three, rows_three, sums_three, notes, table_three, far, halo_grad = last_layer(
        words_three, state_two, got, weight_three, bias_all, 2 * units, seeds, fans[2]
    )
    state_grad, returned, weight_grad = scatter_layer(
        words_three,
        grad_three,
        rows_three,
        weight_three,
        halo_grad,
        mesh_sizes,
        3,
        fans[2],
        tables=(far, table_three),
    )
    grad_two, rows_two, sums_two, halo_grad, early = middle_layer(
        state_grad,
        preact_two,
        returned,
        send_row,
        words_two,
        weight_two,
        state_one,
        mean_two,
        weight_grad,
        notes,
        fans[1],
    )
    state_grad, returned, early_sum, notes = scatter_layer(
        words_two, grad_two, rows_two, weight_two, halo_grad, mesh_sizes, 4, fans[1], early=early
    )
    late_rows, early_all = bottom_layer(
        state_grad,
        preact_one,
        returned,
        send_row,
        feats,
        mean_one,
        sums_two,
        sums_three,
        early_sum,
        mesh_sizes,
        5,
    )
    late_all = share_sums(late_rows, mesh_sizes, 6)
    out = adam(
        mean_one.shape[0],
        late_all.reshape(late_rows.shape),
        early_all.reshape(early.shape),
        notes,
        weight_one,
        weight_two,
        weight_three,
        left_one,
        right_one,
        left_two,
        right_two,
        left_three,
        right_three.T,
        first_one,
        first_two,
        first_three.T,
        second_one,
        second_two,
        second_three.T,
        bias_all,
        bias_first,
        bias_second,
    )
    third = [value.T for value in out[6:9]]
    return (*out[:6], *third, *out[9:12], notes[0, 0, 0], notes[1, 0, 0])


def solution(mesh):
    split = P(axes)
    rows = P(axes, None)
    placed = (rows, split, split, split, rows, rows, rows, rows) + (P(),) * 18
    mesh_sizes = (mesh.shape[axes[0]], mesh.shape[axes[1]])
    return jax.shard_map(
        functools.partial(on_device, mesh_sizes),
        mesh=mesh,
        in_specs=placed,
        out_specs=(P(),) * 14,
        check_vma=False,
    )
```

time: 229 us -> 188 us (0.82)
  Pallas kernels: 215 us -> 183 us
  local copies, waits for them, and re-layouts: 9.11 us -> 3.24 us
  other arithmetic: 3.81 us -> 0 us
    pallas_call x1, Pallas kernels: 24.2 us -> 16.6 us  [share_sums(): pl.pallas_call(functools.partial(share_kernel, mesh_sizes), in_specs=[vme...]
    pallas_call x1, Pallas kernels: 21.8 us -> 15.6 us  [last_layer(): pl.pallas_call(functools.partial(last_kernel, fanout, bias_start), grid=(...]
    pallas_call x2, Pallas kernels: 43.4 us -> 37.8 us  [scatter_layer(): pl.pallas_call(functools.partial(scatter_kernel, mesh_sizes, fanout, flip...]
    pallas_call x3, Pallas kernels: 47.3 us -> 42 us  [count_words(): pl.pallas_call(functools.partial(words_kernel, mesh_sizes, kind), grid=(n...]
    pallas_call x2, Pallas kernels: 40.6 us -> 36.5 us  [hidden_layer(): pl.pallas_call(functools.partial(hidden_kernel, fanout, bias_start), grid...]
    slice x3 -> x1, local copies, waits for them, and re-layouts: 4.54 us -> 0.52 us  [on_device(): return (*out[:6], *third, *out[9:12], notes[0, 0, 0], notes[1, 0, 0])]
    pallas_call x3 -> x0, other arithmetic: 3.81 us -> none  [adam(): pl.pallas_call(functools.partial(adam_kernel, padded), in_specs=[vmem] *...]
    reshape x3 -> x0, local copies, waits for them, and re-layouts: 2.43 us -> none  [the longest x1 1.27 us: on_device(): bias_row = bias_all.reshape(1, -1)]
where the time goes in v1:
time: 188 us; the launch traced here: 187 us
  Pallas kernels  183 us (97%)
  local copies, waits for them, and re-layouts  3.24 us (2%)
    pallas_call x3, Pallas kernels, count_words(): pl.pallas_call(functools.partial(words_kernel, mesh_sizes, kind), grid=(n...  42 us
    pallas_call x2, Pallas kernels, scatter_layer(): pl.pallas_call(functools.partial(scatter_kernel, mesh_sizes, fanout, flip...  37.8 us
    pallas_call x2, Pallas kernels, hidden_layer(): pl.pallas_call(functools.partial(hidden_kernel, fanout, bias_start), grid...  36.5 us
    pallas_call x1, Pallas kernels, share_sums(): pl.pallas_call(functools.partial(share_kernel, mesh_sizes), in_specs=[vme...  16.6 us
    pallas_call x1, Pallas kernels, last_layer(): pl.pallas_call(functools.partial(last_kernel, fanout, bias_start), grid=(...  15.6 us
    pallas_call x1, Pallas kernels, bottom_layer(): pl.pallas_call(functools.partial(bottom_kernel, mesh_sizes), grid=(nodes...  14.9 us
    pallas_call x1, Pallas kernels, middle_layer(): pl.pallas_call(functools.partial(middle_kernel, fanout), grid=(nodes // B...  11.2 us
    pallas_call x1, Pallas kernels, adam(): pl.pallas_call(functools.partial(adam_kernel, padded), in_specs=[vmem] *...  8.12 us

profile of v1, /device:TPU:0, one launch (start us, length us, event | category | flops | bytes accessed | tf_op | source)
XLA Modules:
  0.0 186.8 jit_solution(10074083498428923451)
XLA Ops:
  0.6 0.8 copy.42
  1.4 0.1 reshape.64.refs_1_.send_ref
  1.5 16.7 %count_words.3 = (s32[576,4096]{1,0:T(8,128)}, bf16[32,16,128]{2,1,0:T(8,128)(2,1)S(1)}) custom-call(s32[15,4096]{1,0:T(8,128)} %bitcast.42, bf16[100,4096]{1,0:T(8,128)(2,1)} %bitcast.24, s32[1,512]{1,0:T(1,128)S(1)} %reshape.64.refs_1_.send_ref), custom_call_target="tpu_custom_call" | custom-call | tf_op jit(solution)/shard_map/count_words/pallas_call | solution.py:272
  18.2 0.0 copy-start
  18.2 1.1 copy-done
  19.4 16.3 %hidden_layer.2 = (bf16[256,4096]{1,0:T(8,128)(2,1)S(1)}, f32[256,4096]{1,0:T(8,128)}, bf16[512,256]{1,0:T(8,128)(2,1)S(1)}, bf16[112,4096]{1,0:T(8,128)(2,1)}) custom-call(s32[576,4096]{1,0:T(8,128)} %get-tuple-element.62.words_ref, bf16[100,4096]{1,0:T(8,128)(2,1)S(1)} %bitcast.26, bf16[100,4096]{1,0:T(8,128)(2,1)S(1)} %bitcast.27, ...), custom_call_target="tpu_custom_call" | custom-call | tf_op jit(solution)/shard_map/hidden_layer/pallas_call | solution.py:423
  35.6 10.5 %count_words.4 = (s32[576,4096]{1,0:T(8,128)}, bf16[32,16,256]{2,1,0:T(8,128)(2,1)S(1)}) custom-call(s32[10,4096]{1,0:T(8,128)} %bitcast.43, bf16[32,16,256]{2,1,0:T(8,128)(2,1)S(1)} %bitcast.33), custom_call_target="tpu_custom_call" | custom-call | tf_op jit(solution)/shard_map/count_words/pallas_call | solution.py:272
  46.2 0.0 copy-start.1
  46.2 0.0 copy-start.2
  46.2 0.0 copy-start.3
  46.2 20.2 %hidden_layer.3 = (bf16[256,4096]{1,0:T(8,128)(2,1)S(1)}, f32[256,4096]{1,0:T(8,128)}, bf16[512,256]{1,0:T(8,128)(2,1)S(1)}, bf16[256,4096]{1,0:T(8,128)(2,1)}) custom-call(s32[576,4096]{1,0:T(8,128)} %get-tuple-element.65.words_ref, bf16[256,4096]{1,0:T(8,128)(2,1)S(1)} %get-tuple-element.66.own_ref.own_block, ...), custom_call_target="tpu_custom_call" | custom-call | tf_op jit(solution)/shard_map/hidden_layer/pallas_call | solution.py:423
  66.5 0.0 copy-done.1
  66.5 0.0 copy-done.2
  66.5 0.0 copy-done.3
  66.5 14.8 %count_words.5 = (s32[576,4096]{1,0:T(8,128)}, bf16[32,16,256]{2,1,0:T(8,128)(2,1)S(1)}, f32[48,4096]{1,0:T(8,128)S(1)}) custom-call(s32[5,4096]{1,0:T(8,128)} %bitcast.44, bf16[32,16,256]{2,1,0:T(8,128)(2,1)S(1)} %bitcast.34, s32[1,2048]{1,0:T(1,128)S(1)} %bitcast.36, s32[1,2048]{1,0:T(1,128)S(1)} %bitcast.37, s32[1,2048]{1,0:T(1,128)S(1)} %bitcast.38), custom_call_target="tpu_custom_call" | custom-call | tf_op jit(solution)/shard_map/count_words/pallas_call | solution.py:272
  81.3 15.6 %last_layer.1 = (bf16[48,4096]{1,0:T(8,128)(2,1)S(1)}, bf16[4096,48]{1,0:T(8,128)(2,1)S(1)}, f32[48,128]{1,0:T(8,128)S(1)}, f32[16,128]{1,0:T(8,128)S(1)}, bf16[...) custom-call(s32[576,4096]{1,0:T(8,128)} %get-tuple-element.69.words_ref, ...), custom_call_target="tpu_custom_call" | custom-call | tf_op jit(solution)/shard_map/last_layer/pallas_call | solution.py:571
  96.9 18.8 %scatter_layer.2 = (f32[256,4608]{1,0:T(8,128)S(1)}, bf16[32,16,256]{2,1,0:T(8,128)(2,1)S(1)}, f32[512,48]{1,0:T(8,128)S(1)}) custom-call(s32[576,4096]{1,0:T(8,128)} %get-tuple-element.69.words_ref, bf16[48,4096]{1,0:T(8,128)(2,1)S(1)} %get-tuple-element.73.grad_ref, bf16[4096,48]{1,0:T(8,128)(2,1)S(1)} %get-tuple-element.74.rows_ref, f32[47,512]{1,0:T(8,128)} %bitcast.40, ...), custom_call_target="tpu_custom_call" | custom-call | tf_op jit(solution)/shard_map/scatter_layer/pallas_call | solution.py:756
  115.7 11.2 %middle_layer.1 = (bf16[256,4096]{1,0:T(8,128)(2,1)S(1)}, bf16[4096,256]{1,0:T(8,128)(2,1)S(1)}, f32[256,128]{1,0:T(8,128)S(1)}, bf16[512,256]{1,0:T(8,128)(2,1)S(1)}, bf16[512,384]{1,0:T(8,128)(2,1)S(1)}) custom-call(f32[256,4608]{1,0:T(8,128)S(1)} %get-tuple-element.78.state_ref, f32[256,4096]{1,0:T(8,128)} %get-tuple-element.79.preact_ref, ...), custom_call_target="tpu_custom_call" | custom-call | tf_op jit(solution)/shard_map/middle_layer/pallas_call | solution.py:869
  126.9 19.0 %scatter_layer.3 = (f32[256,4608]{1,0:T(8,128)S(1)}, bf16[32,16,256]{2,1,0:T(8,128)(2,1)S(1)}, bf16[16,384]{1,0:T(8,128)(2,1)S(1)}, f32[2,1,1]{2,1,0:T(1,128)S(1)}) custom-call(s32[576,4096]{1,0:T(8,128)} %get-tuple-element.65.words_ref, bf16[256,4096]{1,0:T(8,128)(2,1)S(1)} %get-tuple-element.84.grad_ref, bf16[4096,256]{1,0:T(8,128)(2,1)S(1)} %get-tuple-element.85.rows_ref, ...), custom_call_target="tpu_custom_call" | custom-call | tf_op jit(solution)/shard_map/scatter_layer/pallas_call | solution.py:756
  145.9 0.0 copy-start.4
  145.9 14.9 %bottom_layer.1 = (bf16[512,128]{1,0:T(8,128)(2,1)S(1)}, bf16[32,16,384]{2,1,0:T(8,128)(2,1)S(1)}) custom-call(f32[256,4608]{1,0:T(8,128)S(1)} %get-tuple-element.88.state_ref, f32[256,4096]{1,0:T(8,128)} %get-tuple-element.89.preact_ref, bf16[32,16,256]{2,1,0:T(8,128)(2,1)S(1)} %get-tuple-element.90.returned_ref, s32[1,512]{1,0:T(1,128)S(1)} %reshape.64.refs_1_.send_ref, ...), custom_call_target="tpu_custom_call" | custom-call | tf_op jit(solution)/shard_map/bottom_layer/pallas_call | solution.py:1000
  160.8 16.6 %share_sums.1 = bf16[32,16,128]{2,1,0:T(8,128)(2,1)S(1)} custom-call(bf16[32,16,128]{2,1,0:T(8,128)(2,1)S(1)} %bitcast.35), custom_call_target="tpu_custom_call" | custom-call | tf_op jit(solution)/shard_map/share_sums/pallas_call | solution.py:1087
  177.4 0.0 copy-done.4
  177.4 0.7 copy.43
  178.1 8.1 %adam.1 = (f32[200,256]{1,0:T(8,128)}, f32[200,256]{1,0:T(8,128)}, f32[200,256]{1,0:T(8,128)}, f32[512,256]{1,0:T(8,128)}, f32[512,256]{1,0:T(8,128)}, /*index=5...) custom-call(bf16[512,128]{1,0:T(8,128)(2,1)S(1)} %bitcast.28, ...), custom_call_target="tpu_custom_call" | custom-call | tf_op jit(solution)/shard_map/adam/pallas_call | solution.py:1201
  186.3 0.5 fusion
Async XLA Ops:
  18.2 1.2 copy-start
  46.2 20.3 %copy-start.1 = (s32[2048]{0:T(1024)S(1)}, s32[2048]{0:T(1024)}, u32[]{:S(2)}) copy-start(s32[2048]{0:T(1024)} %param.28) | copy-start | bytes 24580
  46.2 20.3 %copy-start.2 = (s32[2048]{0:T(1024)S(1)}, s32[2048]{0:T(1024)}, u32[]{:S(2)}) copy-start(s32[2048]{0:T(1024)} %param.27) | copy-start | bytes 24580
  46.2 20.3 %copy-start.3 = (s32[2048]{0:T(1024)S(1)}, s32[2048]{0:T(1024)}, u32[]{:S(2)}) copy-start(s32[2048]{0:T(1024)} %param.29) | copy-start | bytes 24580
  145.9 31.5 %copy-start.4 = (f32[47,47]{1,0:T(8,128)S(1)}, f32[47,47]{1,0:T(8,128)}, u32[]{:S(2)}) copy-start(f32[47,47]{1,0:T(8,128)} %param.42) | copy-start | bytes 26512

commit v2 on v1

--- a/solution.py
+++ b/solution.py
@@ -171,6 +171,137 @@
     )
     copy.wait_send()
     copy.wait_recv()
+
+
+def split_sizes(mesh_sizes):
+    across, along = mesh_sizes
+    high = 4 if across % 4 == 0 else 1
+    return high, across // high, along
+
+
+def split_place(mesh_sizes):
+    _, low, along = split_sizes(mesh_sizes)
+    row, column = lax.axis_index(axes[0]), lax.axis_index(axes[1])
+    top = row // low
+    return top, row - top * low, column, (row - top * low) * along + column
+
+
+def each_high(mesh_sizes, act):
+    high, low, _ = split_sizes(mesh_sizes)
+    top, bottom, column, _ = split_place(mesh_sizes)
+    for ahead in range(1, high):
+        other = top + ahead
+        other = jnp.where(other >= high, other - high, other)
+        act(other, (other * low + bottom, column))
+
+
+def each_plane(mesh_sizes, act):
+    _, low, along = split_sizes(mesh_sizes)
+    top, bottom, column, _ = split_place(mesh_sizes)
+    for down in range(low):
+        for ahead in range(along):
+            if down == 0 and ahead == 0:
+                continue
+            line = bottom + down
+            line = jnp.where(line >= low, line - low, line)
+            place = column + ahead
+            place = jnp.where(place >= along, place - along, place)
+            act(line * along + place, (top * low + line, place))
+
+
+def greet_split(mesh_sizes):
+    barrier = pltpu.get_barrier_semaphore()
+
+    def tell(index, where):
+        pl.semaphore_signal(
+            barrier, inc=1, device_id=where, device_id_type=pl.DeviceIdType.MESH
+        )
+
+    each_high(mesh_sizes, tell)
+    each_plane(mesh_sizes, tell)
+
+
+def split_greeted(mesh_sizes):
+    high, low, along = split_sizes(mesh_sizes)
+    pl.semaphore_wait(pltpu.get_barrier_semaphore(), high - 1 + low * along - 1)
+
+
+def push(src_ref, dst_ref, sems, where):
+    pltpu.make_async_remote_copy(
+        src_ref=src_ref,
+        dst_ref=dst_ref,
+        send_sem=sems[0],
+        recv_sem=sems[1],
+        device_id=where,
+        device_id_type=pl.DeviceIdType.MESH,
+    ).start()
+
+
+def wait_pushed(ref, sems):
+    copy = pltpu.make_async_remote_copy(
+        src_ref=ref,
+        dst_ref=ref,
+        send_sem=sems[0],
+        recv_sem=sems[1],
+        device_id=(lax.axis_index(axes[0]), lax.axis_index(axes[1])),
+        device_id_type=pl.DeviceIdType.MESH,
+    )
+    copy.wait_send()
+    copy.wait_recv()
+
+
+def high_start(mesh_sizes, sent_ref, relay_ref, sems):
+    top = split_place(mesh_sizes)[0]
+    each_high(
+        mesh_sizes, lambda other, where: push(sent_ref.at[other], relay_ref.at[top], sems, where)
+    )
+
+
+def high_wait(mesh_sizes, relay_ref, sems):
+    high = split_sizes(mesh_sizes)[0]
+    if high > 1:
+        wait_pushed(relay_ref.at[pl.ds(0, high - 1)], sems)
+
+
+def plane_wait(mesh_sizes, land_ref, sems):
+    _, low, along = split_sizes(mesh_sizes)
+    wait_pushed(land_ref.at[pl.ds(0, low * along - 1)], sems)
+
+
+def plane_blocks(mesh_sizes, relay_ref, land_ref, sems):
+    me = split_place(mesh_sizes)[3]
+    each_plane(
+        mesh_sizes,
+        lambda other, where: push(relay_ref.at[:, other], land_ref.at[:, me], sems, where),
+    )
+
+
+def plane_blocks_wait(mesh_sizes, land_ref, sems):
+    _, low, along = split_sizes(mesh_sizes)
+    wait_pushed(land_ref.at[:, pl.ds(0, low * along - 1)], sems)
+
+
+NOTES = 120
+
+
+def put_terms(rows, values):
+    lane = lax.broadcasted_iota(jnp.int32, rows.shape, 1)
+    for index, value in enumerate(values):
+        for at in range(3):
+            term = value.astype(jnp.bfloat16).astype(jnp.float32)
+            rows = jnp.where(lane == NOTES + 3 * index + at, term, rows)
+            value = value - term
+    return rows
+
+
+def take_terms(rows):
+    lane = lax.broadcasted_iota(jnp.int32, rows.shape, 1)
+    values = []
+    for index in range(2):
+        first = NOTES + 3 * index
+        mine = (lane >= first) & (lane < first + 3)
+        values.append(jnp.sum(jnp.where(mine, rows, 0.0), axis=1, keepdims=True))
+    return values
 
 
 def semaphores():
@@ -617,25 +748,28 @@
     if flipped:
         weight_in, halo_ref, far_ref, table_ref, far_table = refs[:5]
         state_ref, got_ref, weight_ref = refs[5:8]
-        padded_ref, counts_ref, sums_ref, self_ref, near_ref, land_ref = refs[8:14]
-        send_sem, recv_sem = refs[14:]
+        refs = refs[8:]
     else:
         weight_in, halo_ref, early_ref = refs[:3]
         state_ref, got_ref, early_sum, notes_ref = refs[3:7]
-        padded_ref, counts_ref, sums_ref, self_ref, near_ref, land_ref = refs[7:13]
-        early_land, send_sem, recv_sem, early_send, early_recv = refs[13:]
-        early_moves = (mesh_sizes, early_ref, early_land, early_send, early_recv)
+        refs = refs[7:]
+    padded_ref, counts_ref, sums_ref, self_ref, near_ref, relay_ref, land_ref = refs[:7]
+    if flipped:
+        high_sems, plane_sems = refs[7:9], refs[9:11]
+    else:
+        early_relay, early_part, early_land = refs[7:10]
+        high_sems, plane_sems = refs[10:12], refs[12:14]
+        early_high, early_plane = refs[14:16], refs[16:18]
     step = pl.program_id(0)
     units, nodes = grad_ref.shape
     width = state_ref.shape[0]
     span = words_ref.shape[0]
     part = span * SLOTS
     steps = -(-nodes // part)
-    moves = (mesh_sizes, halo_ref, land_ref, send_sem, recv_sem)
 
     @pl.when(step == 0)
     def _():
-        greet(mesh_sizes)
+        greet_split(mesh_sizes)
         for k in range(steps):
             start = k * part
             stop = min(start + part, nodes)
@@ -653,10 +787,27 @@
         self_ref[...] = weight[:width].astype(jnp.bfloat16)
         near_ref[...] = weight[width:].astype(jnp.bfloat16)
         sums_ref[...] = jnp.zeros_like(sums_ref)
-        all_greeted(mesh_sizes)
-        send_blocks(*moves)
+        split_greeted(mesh_sizes)
+        high_start(mesh_sizes, halo_ref, relay_ref, high_sems)
         if not flipped:
-            send_blocks(*early_moves)
+            plane_blocks(mesh_sizes, early_ref, early_relay, early_plane)
+
+    @pl.when(step == steps // 2)
+    def _():
+        top, _, _, me = split_place(mesh_sizes)
+        high_wait(mesh_sizes, relay_ref, high_sems)
+        relay_ref[top] = halo_ref[top]
+        plane_blocks(mesh_sizes, relay_ref, land_ref, plane_sems)
+        if not flipped:
+            plane_blocks_wait(mesh_sizes, early_relay, early_plane)
+            early_relay[:, me] = early_ref[:, me]
+            total = jnp.sum(early_relay[...].astype(jnp.float32), axis=1)
+            shape = total.shape
+            total = total.reshape(-1, shape[2])
+            last = total[:, -128:]
+            total = jnp.concatenate([total[:, :-128], put_terms(last, take_terms(last))], axis=1)
+            early_part[...] = total.astype(jnp.bfloat16).reshape(shape)
+            high_start(mesh_sizes, early_part, early_land, early_high)
 
     def add(row):
         spread_unit(words_ref, row // SLOTS, counts_ref, row)
@@ -689,22 +840,18 @@
 
     @pl.when(step == steps - 1)
     def _():
-        me = my_index(mesh_sizes)
-        wait_moves(*moves)
-        land_ref[me] = halo_ref[me]
+        me = split_place(mesh_sizes)[3]
+        plane_blocks_wait(mesh_sizes, land_ref, plane_sems)
+        land_ref[:, me] = relay_ref[:, me]
         got_ref[...] = land_ref[...]
         if not flipped:
-            wait_moves(*early_moves)
-            early_land[me] = early_ref[me]
+            top = split_place(mesh_sizes)[0]
+            high_wait(mesh_sizes, early_land, early_high)
+            early_land[top] = early_part[top]
             total = jnp.sum(early_land[...].astype(jnp.float32), axis=0)
             early_sum[...] = total.astype(jnp.bfloat16)
-            lane = lax.broadcasted_iota(jnp.int32, (8, 128), 1)
-            row = lax.broadcasted_iota(jnp.int32, (8, 128), 0)
-            last = jnp.broadcast_to(total[:1, -128:], (8, 128))
-            for index in range(2):
-                mine = (lane >= 120 + 3 * index) & (lane < 123 + 3 * index)
-                note = jnp.sum(jnp.where(mine & (row == 0), last, 0.0))
-                notes_ref[index] = jnp.full((1, 1), note, jnp.float32)
+            for index, value in enumerate(take_terms(total[:, -128:])):
+                notes_ref[index] = value[:1]
 
 
 def scatter_layer(
@@ -718,7 +865,8 @@
     part = total // WORDS
     span = part // SLOTS
     steps = -(-nodes // part)
-    blocks = (parts, halo // parts, width)
+    high = split_sizes(mesh_sizes)[0]
+    blocks = (high, parts // high, halo // parts, width)
     in_specs = [
         pl.BlockSpec((span, nodes), lambda i: (i, 0)),
         whole(grad.shape),
@@ -742,17 +890,22 @@
         operands += [far, table, table]
         out_specs.append(whole((2 * width, units)))
         out_shape.append(jax.ShapeDtypeStruct((2 * width, units), jnp.float32))
-        scratch = semaphores()
+        scratch = semaphores() + semaphores()
     else:
-        early_blocks = (parts, early.shape[0] // parts, early.shape[1])
+        early_blocks = (high, parts // high, early.shape[0] // parts, early.shape[1])
         in_specs.append(whole(early_blocks))
         operands.append(early.reshape(early_blocks))
-        out_specs += [whole(early_blocks[1:]), whole((2, 1, 1))]
+        out_specs += [whole(early_blocks[2:]), whole((2, 1, 1))]
         out_shape += [
-            jax.ShapeDtypeStruct(early_blocks[1:], jnp.bfloat16),
+            jax.ShapeDtypeStruct(early_blocks[2:], jnp.bfloat16),
             jax.ShapeDtypeStruct((2, 1, 1), jnp.float32),
         ]
-        scratch = [pltpu.VMEM(early_blocks, jnp.bfloat16)] + semaphores() + semaphores()
+        scratch = [
+            pltpu.VMEM(early_blocks, jnp.bfloat16),
+            pltpu.VMEM((high,) + early_blocks[2:], jnp.bfloat16),
+            pltpu.VMEM((high,) + early_blocks[2:], jnp.bfloat16),
+        ]
+        scratch += semaphores() * 4
     return pl.pallas_call(
         functools.partial(scatter_kernel, mesh_sizes, fanout, flipped),
         grid=(steps,),
@@ -765,6 +918,7 @@
             pltpu.VMEM((part, units), jnp.bfloat16),
             pltpu.VMEM((width, units), jnp.bfloat16),
             pltpu.VMEM((width, units), jnp.bfloat16),
+            pltpu.VMEM(blocks, jnp.bfloat16),
             pltpu.VMEM(blocks, jnp.bfloat16),
         ]
         + scratch,
@@ -845,13 +999,7 @@
         above = jnp.concatenate(
             [above_ref[...], jnp.zeros((height, 128 - narrow), jnp.float32)], axis=1
         )
-        lane = lax.broadcasted_iota(jnp.int32, above.shape, 1)
-        for index in range(2):
-            value = notes_ref[8 * index : 8 * index + 1, 0:1]
-            for at in range(3):
-                term = value.astype(jnp.bfloat16).astype(jnp.float32)
-                above = jnp.where(lane == 120 + 3 * index + at, term, above)
-                value = value - term
+        above = put_terms(above, [notes_ref[0:1, 0:1], notes_ref[8:9, 0:1]])
         early_ref[:, units:] = above.astype(jnp.bfloat16)
 
 
@@ -932,23 +1080,37 @@
     back_ref,
     sums_ref,
     weight_ref,
+    relay_ref,
     land_ref,
-    send_sem,
-    recv_sem,
+    *sems,
 ):
     step = pl.program_id(0)
     units = state_ref.shape[0]
     halo = send_ref.shape[1]
-    moves = (mesh_sizes, early_ref, land_ref, send_sem, recv_sem)
+    high_sems, plane_sems = sems[:2], sems[2:]
 
     @pl.when(step == 0)
     def _():
-        greet(mesh_sizes)
+        greet_split(mesh_sizes)
         back_ref[...] = returned_ref[...].reshape(halo, units).T
         sums_ref[...] = jnp.zeros_like(sums_ref)
         weight_ref[...] = jnp.zeros_like(weight_ref)
-        all_greeted(mesh_sizes)
-        send_all(*moves)
+        split_greeted(mesh_sizes)
+        top = split_place(mesh_sizes)[0]
+        each_high(
+            mesh_sizes,
+            lambda other, where: push(early_ref, relay_ref.at[top], high_sems, where),
+        )
+
+    @pl.when(step == 3)
+    def _():
+        top, _, _, me = split_place(mesh_sizes)
+        high_wait(mesh_sizes, relay_ref, high_sems)
+        relay_ref[top] = early_ref[...]
+        each_plane(
+            mesh_sizes,
+            lambda other, where: push(relay_ref, land_ref.at[:, me], plane_sems, where),
+        )
 
     grad = active_grad(step, state_ref, preact_ref, back_ref, send_ref)
     sums_ref[...] += jnp.sum(grad.astype(jnp.float32), axis=1, keepdims=True)
@@ -958,7 +1120,7 @@
 
     @pl.when(step == pl.num_programs(0) - 1)
     def _():
-        me = my_index(mesh_sizes)
+        me = split_place(mesh_sizes)[3]
         padded = weight_ref.shape[1]
         row = 0
         for start in range(0, units, 128):
@@ -980,8 +1142,8 @@
         rest = late_ref.shape[0] - row
         pieces.append(jnp.zeros((rest - len(pieces), 128), jnp.float32))
         late_ref[row:, :] = jnp.concatenate(pieces).astype(jnp.bfloat16)
-        wait_moves(*moves)
-        land_ref[me] = early_ref[...]
+        plane_blocks_wait(mesh_sizes, land_ref, plane_sems)
+        land_ref[:, me] = relay_ref[...]
         early_all[...] = land_ref[...]
 
 
@@ -996,7 +1158,8 @@
     rows = units // 128 * (2 * padded + 2) + -(-sums_three.shape[0] // 128)
     rows = -(-rows // 512) * 512
     rows = -(-rows // parts) * parts
-    early_blocks = (parts,) + early.shape
+    high = split_sizes(mesh_sizes)[0]
+    early_blocks = (high, parts // high) + early.shape
     return pl.pallas_call(
         functools.partial(bottom_kernel, mesh_sizes),
         grid=(nodes // BLOCK,),
@@ -1020,8 +1183,10 @@
             pltpu.VMEM((units, halo), jnp.bfloat16),
             pltpu.VMEM((units, 128), jnp.float32),
             pltpu.VMEM((2, padded, units), jnp.float32),
+            pltpu.VMEM((high,) + early.shape, jnp.bfloat16),
             pltpu.VMEM(early_blocks, jnp.bfloat16),
         ]
+        + semaphores()
         + semaphores(),
         compiler_params=params(24, collective),
         name="bottom_layer",
@@ -1063,60 +1228,115 @@
 
 
 def share_kernel(
-    mesh_sizes, late_ref, late_out, late_land, late_sum, late_all, send_sem, recv_sem, last_send, last_recv
+    mesh_sizes,
+    late_ref,
+    early_ref,
+    notes_ref,
+    left_two,
+    right_two,
+    left_three,
+    right_three,
+    first_two,
+    first_three,
+    second_two,
+    second_three,
+    late_out,
+    turned_two,
+    moved_two,
+    turned_three,
+    moved_three,
+    plane_land,
+    part_ref,
+    high_land,
+    whole_ref,
+    *sems,
 ):
-    me = my_index(mesh_sizes)
-    inward = (mesh_sizes, late_ref, late_land, send_sem, recv_sem)
-    outward = (mesh_sizes, late_sum, late_all, last_send, last_recv)
-    greet(mesh_sizes)
-    all_greeted(mesh_sizes)
-    send_blocks(*inward)
-    wait_moves(*inward)
-    late_land[me] = late_ref[me]
-    late_sum[...] = jnp.sum(late_land[...].astype(jnp.float32), axis=0).astype(jnp.bfloat16)
-    send_all(*outward)
-    wait_moves(*outward)
-    late_all[me] = late_sum[...]
-    late_out[...] = late_all[...]
-
-
-def share_sums(late_rows, mesh_sizes, collective):
-    parts = mesh_sizes[0] * mesh_sizes[1]
-    late_shape = (parts, late_rows.shape[0] // parts, 128)
+    inward, across, outward = sems[:2], sems[2:4], sems[4:]
+    top, _, _, me = split_place(mesh_sizes)
+    units = right_two.shape[0]
+    kinds = right_three.shape[0]
+    share = 1.0 / notes_ref[1]
+    greet_split(mesh_sizes)
+    split_greeted(mesh_sizes)
+    each_plane(
+        mesh_sizes,
+        lambda other, where: push(late_ref.at[other], plane_land.at[me], inward, where),
+    )
+
+    grad = early_ref[:, :units]
+    turned = product(product(left_two[...], grad, TRANS_LEFT), right_two[...]) * share
+    turned_two[...] = turned
+
+    plane_wait(mesh_sizes, plane_land, inward)
+    plane_land[me] = late_ref[me]
+    part_ref[...] = jnp.sum(plane_land[...].astype(jnp.float32), axis=0).astype(jnp.bfloat16)
+    each_high(
+        mesh_sizes, lambda other, where: push(part_ref, high_land.at[top], across, where)
+    )
+
+    update = moments(turned, first_two[...], second_two[...])[2]
+    moved_two[...] = product(product(left_two[...], update), right_two[...], TRANS_RIGHT)
+
+    high_wait(mesh_sizes, high_land, across)
+    high_land[top] = part_ref[...]
+    whole_ref[...] = jnp.sum(high_land[...].astype(jnp.float32), axis=0).astype(jnp.bfloat16)
+    each_plane(
+        mesh_sizes, lambda other, where: push(whole_ref, late_out.at[me], outward, where)
+    )
+
+    grad = early_ref[:, units:].astype(jnp.float32).T[:kinds].astype(jnp.bfloat16)
+    turned = product(right_three[...], product(grad, left_three[...])) * share
+    turned_three[...] = turned
+    update = moments(turned, first_three[...], second_three[...])[2]
+    moved = product(update, left_three[...], TRANS_RIGHT)
+    moved_three[...] = product(right_three[...], moved, TRANS_LEFT)
+
+    plane_wait(mesh_sizes, late_out, outward)
+    late_out[me] = whole_ref[...]
+
+
+def share_sums(late_rows, mesh_sizes, collective, early_all, notes, bases, second_state, third_state):
+    high, low, along = split_sizes(mesh_sizes)
+    blocks = (low * along, late_rows.shape[0] // (low * along), 128)
     vmem = pl.BlockSpec(memory_space=pltpu.VMEM)
+    operands = [early_all, notes, *in_hbm(*bases, second_state[0], third_state[0])]
+    operands += in_hbm(second_state[1], third_state[1])
+    two = jax.ShapeDtypeStruct(second_state[0].shape, jnp.float32)
+    three = jax.ShapeDtypeStruct(third_state[0].shape, jnp.float32)
     return pl.pallas_call(
         functools.partial(share_kernel, mesh_sizes),
-        in_specs=[vmem],
-        out_specs=vmem,
-        out_shape=jax.ShapeDtypeStruct(late_shape, jnp.bfloat16),
+        in_specs=[vmem] * (1 + len(operands)),
+        out_specs=[vmem] * 5,
+        out_shape=[jax.ShapeDtypeStruct(blocks, jnp.bfloat16), two, two, three, three],
         scratch_shapes=[
-            pltpu.VMEM(late_shape, jnp.bfloat16),
-            pltpu.VMEM(late_shape[1:], jnp.bfloat16),
-            pltpu.VMEM(late_shape, jnp.bfloat16),
+            pltpu.VMEM(blocks, jnp.bfloat16),
+            pltpu.VMEM(blocks[1:], jnp.bfloat16),
+            pltpu.VMEM((high,) + blocks[1:], jnp.bfloat16),
+            pltpu.VMEM(blocks[1:], jnp.bfloat16),
         ]
+        + semaphores()
         + semaphores()
         + semaphores(),
         compiler_params=pltpu.CompilerParams(
-            vmem_limit_bytes=8 * MIB, collective_id=collective, has_side_effects=True
+            vmem_limit_bytes=32 * MIB, collective_id=collective, has_side_effects=True
         ),
         name="share_sums",
-    )(late_rows.reshape(late_shape))
+    )(late_rows.reshape(blocks), *operands)
 
 
 def adam_kernel(
     padded,
     late_ref,
-    early_ref,
     notes_ref,
+    turned_two,
+    moved_two,
+    turned_three,
+    moved_three,
     weight_one,
     weight_two,
     weight_three,
     left_one,
     right_one,
-    left_two,
-    right_two,
-    left_three,
-    right_three,
     first_one,
     first_two,
     first_three,
@@ -1133,34 +1353,6 @@
     width = weight_one.shape[0] // 2
     kinds = weight_three.shape[0]
 
-    def step(grad, weight, first, second, left, right, rate, out):
-        turned = product(product(left[...], grad, TRANS_LEFT), right[...]) * share
-        new_first, new_second, update = moments(turned, first[...], second[...])
-        out[1][...] = new_first
-        out[2][...] = new_second
-        moved = product(product(left[...], update), right[...], TRANS_RIGHT)
-        out[0][...] = weight[...] - rate * moved
-
-    step(
-        early_ref[:, :units],
-        weight_two,
-        first_two,
-        second_two,
-        left_two,
-        right_two,
-        step_rates[1],
-        outs[3:6],
-    )
-
-    grad = early_ref[:, units:].astype(jnp.float32).T[:kinds].astype(jnp.bfloat16)
-    turned = product(right_three[...], product(grad, left_three[...])) * share
-    new_first, new_second, update = moments(turned, first_three[...], second_three[...])
-    outs[7][...] = new_first
-    outs[8][...] = new_second
-    moved = product(update, left_three[...], TRANS_RIGHT)
-    moved = product(right_three[...], moved, TRANS_LEFT)
-    outs[6][...] = weight_three[...] - step_rates[2] * moved
-
     late_rows = late_ref[...].astype(jnp.float32)
     columns = []
     for start in range(0, units, 128):
@@ -1170,16 +1362,23 @@
                 [late_rows[row : row + width], late_rows[row + padded : row + padded + width]]
             )
         )
-    step(
-        jnp.concatenate(columns, axis=1).astype(jnp.bfloat16),
-        weight_one,
-        first_one,
-        second_one,
-        left_one,
-        right_one,
-        step_rates[0],
-        outs[0:3],
-    )
+    grad = jnp.concatenate(columns, axis=1).astype(jnp.bfloat16)
+    turned = product(product(left_one[...], grad, TRANS_LEFT), right_one[...]) * share
+    new_first, new_second, update = moments(turned, first_one[...], second_one[...])
+    outs[1][...] = new_first
+    outs[2][...] = new_second
+    moved = product(product(left_one[...], update), right_one[...], TRANS_RIGHT)
+    outs[0][...] = weight_one[...] - step_rates[0] * moved
+
+    new_first, new_second, _ = moments(turned_two[...], first_two[...], second_two[...])
+    outs[3][...] = weight_two[...] - step_rates[1] * moved_two[...]
+    outs[4][...] = new_first
+    outs[5][...] = new_second
+    new_first, new_second, _ = moments(turned_three[...], first_three[...], second_three[...])
+    outs[6][...] = weight_three[...] - step_rates[2] * moved_three[...]
+    outs[7][...] = new_first
+    outs[8][...] = new_second
+
     row = units // 128 * 2 * padded
     pieces = []
     while len(pieces) * 128 < 2 * units + kinds:
@@ -1194,18 +1393,18 @@
     outs[11][...] = new_second.reshape(flat)
 
 
-def adam(padded, late_all, early_all, notes, *state):
+def adam(padded, late_all, notes, steps, *state):
     vmem = pl.BlockSpec(memory_space=pltpu.VMEM)
-    order = (0, 9, 12, 1, 10, 13, 2, 11, 14, 15, 16, 17)
+    order = (0, 5, 8, 1, 6, 9, 2, 7, 10, 11, 12, 13)
     outs = [jax.ShapeDtypeStruct(state[at].shape, jnp.float32) for at in order]
     return pl.pallas_call(
         functools.partial(adam_kernel, padded),
-        in_specs=[vmem] * (3 + len(state)),
+        in_specs=[vmem] * (2 + len(steps) + len(state)),
         out_specs=[vmem] * len(outs),
         out_shape=outs,
         compiler_params=pltpu.CompilerParams(vmem_limit_bytes=32 * MIB),
         name="adam",
-    )(late_all, early_all, notes, *in_hbm(*state))
+    )(late_all, notes, *steps, *in_hbm(*state))
 
 
 def on_device(
@@ -1308,27 +1507,33 @@
         mesh_sizes,
         5,
     )
-    late_all = share_sums(late_rows, mesh_sizes, 6)
+    first_three, second_three = first_three.T, second_three.T
+    late_all, *steps = share_sums(
+        late_rows,
+        mesh_sizes,
+        6,
+        early_all.reshape(early.shape),
+        notes,
+        (left_two, right_two, left_three, right_three.T),
+        (first_two, second_two),
+        (first_three, second_three),
+    )
     out = adam(
         mean_one.shape[0],
         late_all.reshape(late_rows.shape),
-        early_all.reshape(early.shape),
         notes,
+        steps,
         weight_one,
         weight_two,
         weight_three,
         left_one,
         right_one,
-        left_two,
-        right_two,
-        left_three,
-        right_three.T,
         first_one,
         first_two,
-        first_three.T,
+        first_three,
         second_one,
         second_two,
-        second_three.T,
+        second_three,
         bias_all,
         bias_first,
         bias_second,

time: 188 us -> 177 us (0.941)
  Pallas kernels: 183 us -> 172 us
    pallas_call x1, Pallas kernels: 8.12 us -> 4.36 us  [adam(): pl.pallas_call(functools.partial(adam_kernel, padded), in_specs=[vmem] *...]
    pallas_call x1, Pallas kernels: 14.9 us -> 12.1 us  [bottom_layer(): pl.pallas_call(functools.partial(bottom_kernel, mesh_sizes), grid=(nodes...]
    pallas_call x2, Pallas kernels: 37.8 us -> 35.2 us  [scatter_layer(): pl.pallas_call(functools.partial(scatter_kernel, mesh_sizes, fanout, flip...]
where the time goes in v2:
time: 177 us; the launch traced here: 176 us
  Pallas kernels  172 us (97%)
  local copies, waits for them, and re-layouts  3.24 us (2%)
    pallas_call x3, Pallas kernels, count_words(): pl.pallas_call(functools.partial(words_kernel, mesh_sizes, kind), grid=(n...  42 us
    pallas_call x2, Pallas kernels, hidden_layer(): pl.pallas_call(functools.partial(hidden_kernel, fanout, bias_start), grid...  36.5 us
    pallas_call x2, Pallas kernels, scatter_layer(): pl.pallas_call(functools.partial(scatter_kernel, mesh_sizes, fanout, flip...  35.2 us
    pallas_call x1, Pallas kernels, last_layer(): pl.pallas_call(functools.partial(last_kernel, fanout, bias_start), grid=(...  15.6 us
    pallas_call x1, Pallas kernels, share_sums(): pl.pallas_call(functools.partial(share_kernel, mesh_sizes), in_specs=[vme...  14.8 us
    pallas_call x1, Pallas kernels, bottom_layer(): pl.pallas_call(functools.partial(bottom_kernel, mesh_sizes), grid=(nodes...  12.1 us
    pallas_call x1, Pallas kernels, middle_layer(): pl.pallas_call(functools.partial(middle_kernel, fanout), grid=(nodes // B...  11.1 us
    pallas_call x1, Pallas kernels, adam(): pl.pallas_call(functools.partial(adam_kernel, padded), in_specs=[vmem] *...  4.36 us

profile of v2, /device:TPU:0, one launch (start us, length us, event | category | flops | bytes accessed | tf_op | source)
XLA Modules:
  0.0 175.6 jit_solution(8950101495106972894)
XLA Ops:
  0.6 0.8 copy.42
  1.4 0.1 reshape.64.refs_1_.send_ref
  1.5 16.7 %count_words.3 = (s32[576,4096]{1,0:T(8,128)}, bf16[32,16,128]{2,1,0:T(8,128)(2,1)S(1)}) custom-call(s32[15,4096]{1,0:T(8,128)} %bitcast.46, bf16[100,4096]{1,0:T(8,128)(2,1)} %bitcast.24, s32[1,512]{1,0:T(1,128)S(1)} %reshape.64.refs_1_.send_ref), custom_call_target="tpu_custom_call" | custom-call | tf_op jit(solution)/shard_map/count_words/pallas_call | solution.py:403
  18.2 0.0 copy-start
  18.2 1.1 copy-done
  19.3 16.3 %hidden_layer.2 = (bf16[256,4096]{1,0:T(8,128)(2,1)S(1)}, f32[256,4096]{1,0:T(8,128)}, bf16[512,256]{1,0:T(8,128)(2,1)S(1)}, bf16[112,4096]{1,0:T(8,128)(2,1)}) custom-call(s32[576,4096]{1,0:T(8,128)} %get-tuple-element.67.words_ref, bf16[100,4096]{1,0:T(8,128)(2,1)S(1)} %bitcast.26, bf16[100,4096]{1,0:T(8,128)(2,1)S(1)} %bitcast.27, ...), custom_call_target="tpu_custom_call" | custom-call | tf_op jit(solution)/shard_map/hidden_layer/pallas_call | solution.py:554
  35.6 10.5 %count_words.4 = (s32[576,4096]{1,0:T(8,128)}, bf16[32,16,256]{2,1,0:T(8,128)(2,1)S(1)}) custom-call(s32[10,4096]{1,0:T(8,128)} %bitcast.47, bf16[32,16,256]{2,1,0:T(8,128)(2,1)S(1)} %bitcast.32), custom_call_target="tpu_custom_call" | custom-call | tf_op jit(solution)/shard_map/count_words/pallas_call | solution.py:403
  46.2 0.0 copy-start.1
  46.2 0.0 copy-start.2
  46.2 0.0 copy-start.3
  46.2 20.2 %hidden_layer.3 = (bf16[256,4096]{1,0:T(8,128)(2,1)S(1)}, f32[256,4096]{1,0:T(8,128)}, bf16[512,256]{1,0:T(8,128)(2,1)S(1)}, bf16[256,4096]{1,0:T(8,128)(2,1)}) custom-call(s32[576,4096]{1,0:T(8,128)} %get-tuple-element.70.words_ref, bf16[256,4096]{1,0:T(8,128)(2,1)S(1)} %get-tuple-element.71.own_ref.own_block, ...), custom_call_target="tpu_custom_call" | custom-call | tf_op jit(solution)/shard_map/hidden_layer/pallas_call | solution.py:554
  66.4 0.0 copy-done.1
  66.4 0.0 copy-done.2
  66.4 0.0 copy-done.3
  66.4 14.8 %count_words.5 = (s32[576,4096]{1,0:T(8,128)}, bf16[32,16,256]{2,1,0:T(8,128)(2,1)S(1)}, f32[48,4096]{1,0:T(8,128)S(1)}) custom-call(s32[5,4096]{1,0:T(8,128)} %bitcast.48, bf16[32,16,256]{2,1,0:T(8,128)(2,1)S(1)} %bitcast.33, s32[1,2048]{1,0:T(1,128)S(1)} %bitcast.36, s32[1,2048]{1,0:T(1,128)S(1)} %bitcast.37, s32[1,2048]{1,0:T(1,128)S(1)} %bitcast.38), custom_call_target="tpu_custom_call" | custom-call | tf_op jit(solution)/shard_map/count_words/pallas_call | solution.py:403
  81.2 15.6 %last_layer.1 = (bf16[48,4096]{1,0:T(8,128)(2,1)S(1)}, bf16[4096,48]{1,0:T(8,128)(2,1)S(1)}, f32[48,128]{1,0:T(8,128)S(1)}, f32[16,128]{1,0:T(8,128)S(1)}, bf16[...) custom-call(s32[576,4096]{1,0:T(8,128)} %get-tuple-element.74.words_ref, ...), custom_call_target="tpu_custom_call" | custom-call | tf_op jit(solution)/shard_map/last_layer/pallas_call | solution.py:702
  96.8 17.2 %scatter_layer.2 = (f32[256,4608]{1,0:T(8,128)S(1)}, bf16[4,8,16,256]{3,2,1,0:T(8,128)(2,1)S(1)}, f32[512,48]{1,0:T(8,128)S(1)}) custom-call(s32[576,4096]{1,0:T(8,128)} %get-tuple-element.74.words_ref, bf16[48,4096]{1,0:T(8,128)(2,1)S(1)} %get-tuple-element.78.grad_ref, bf16[4096,48]{1,0:T(8,128)(2,1)S(1)} %get-tuple-element.79.rows_ref, ...), custom_call_target="tpu_custom_call" | custom-call | tf_op jit(solution)/shard_map/scatter_layer/pallas_call | solution.py:909
  114.0 11.1 %middle_layer.1 = (bf16[256,4096]{1,0:T(8,128)(2,1)S(1)}, bf16[4096,256]{1,0:T(8,128)(2,1)S(1)}, f32[256,128]{1,0:T(8,128)S(1)}, bf16[512,256]{1,0:T(8,128)(2,1)S(1)}, bf16[512,384]{1,0:T(8,128)(2,1)S(1)}) custom-call(f32[256,4608]{1,0:T(8,128)S(1)} %get-tuple-element.83.state_ref, f32[256,4096]{1,0:T(8,128)} %get-tuple-element.84.preact_ref, ...), custom_call_target="tpu_custom_call" | custom-call | tf_op jit(solution)/shard_map/middle_layer/pallas_call | solution.py:1017
  125.2 18.0 %scatter_layer.3 = (f32[256,4608]{1,0:T(8,128)S(1)}, bf16[4,8,16,256]{3,2,1,0:T(8,128)(2,1)S(1)}, bf16[16,384]{1,0:T(8,128)(2,1)S(1)}, f32[2,1,1]{2,1,0:T(1,128)S(1)}) custom-call(s32[576,4096]{1,0:T(8,128)} %get-tuple-element.70.words_ref, bf16[256,4096]{1,0:T(8,128)(2,1)S(1)} %get-tuple-element.89.grad_ref, ...), custom_call_target="tpu_custom_call" | custom-call | tf_op jit(solution)/shard_map/scatter_layer/pallas_call | solution.py:909
  143.1 0.0 copy-start.4
  143.1 12.1 %bottom_layer.1 = (bf16[512,128]{1,0:T(8,128)(2,1)S(1)}, bf16[4,8,16,384]{3,2,1,0:T(8,128)(2,1)S(1)}) custom-call(f32[256,4608]{1,0:T(8,128)S(1)} %get-tuple-element.93.state_ref, f32[256,4096]{1,0:T(8,128)} %get-tuple-element.94.preact_ref, bf16[4,8,16,256]{3,2,1,0:T(8,128)(2,1)S(1)} %get-tuple-element.95.returned_ref, ...), custom_call_target="tpu_custom_call" | custom-call | tf_op jit(solution)/shard_map/bottom_layer/pallas_call | solution.py:1163
  155.3 0.0 copy-done.4
  155.3 0.7 copy.43
  156.0 14.8 %share_sums.1 = (bf16[8,64,128]{2,1,0:T(8,128)(2,1)S(1)}, f32[512,256]{1,0:T(8,128)S(1)}, f32[512,256]{1,0:T(8,128)S(1)}, f32[47,512]{1,0:T(8,128)S(1)}, f32[47,512]{1,0:T(8,128)S(1)}) custom-call(bf16[8,64,128]{2,1,0:T(8,128)(2,1)S(1)} %bitcast.35, bf16[512,384]{1,0:T(8,128)(2,1)S(1)} %bitcast.28, f32[2,1,1]{2,1,0:T(1,128)S(1)} %get-tuple-element.102.notes_ref, ...), custom_call_target="tpu_custom_call" | custom-call | tf_op jit(solution)/shard_map/share_sums/pallas_call | solution.py:1306
  170.7 4.4 %adam.1 = (f32[200,256]{1,0:T(8,128)}, f32[200,256]{1,0:T(8,128)}, f32[200,256]{1,0:T(8,128)}, f32[512,256]{1,0:T(8,128)}, f32[512,256]{1,0:T(8,128)}, /*index=5...) custom-call(bf16[512,128]{1,0:T(8,128)(2,1)S(1)} %bitcast.34, ...), custom_call_target="tpu_custom_call" | custom-call | tf_op jit(solution)/shard_map/adam/pallas_call | solution.py:1400
  175.1 0.5 fusion
Async XLA Ops:
  18.2 1.2 copy-start
  46.2 20.3 %copy-start.1 = (s32[2048]{0:T(1024)S(1)}, s32[2048]{0:T(1024)}, u32[]{:S(2)}) copy-start(s32[2048]{0:T(1024)} %param.28) | copy-start | bytes 24580
  46.2 20.2 %copy-start.2 = (s32[2048]{0:T(1024)S(1)}, s32[2048]{0:T(1024)}, u32[]{:S(2)}) copy-start(s32[2048]{0:T(1024)} %param.27) | copy-start | bytes 24580
  46.2 20.2 %copy-start.3 = (s32[2048]{0:T(1024)S(1)}, s32[2048]{0:T(1024)}, u32[]{:S(2)}) copy-start(s32[2048]{0:T(1024)} %param.29) | copy-start | bytes 24580
  143.1 12.1 %copy-start.4 = (f32[47,47]{1,0:T(8,128)S(1)}, f32[47,47]{1,0:T(8,128)}, u32[]{:S(2)}) copy-start(f32[47,47]{1,0:T(8,128)} %param.42) | copy-start | bytes 26512

commit v3 on v2

--- a/solution.py
+++ b/solution.py
@@ -22,7 +22,8 @@
 SLOTS = 8
 RUN = 48
 UNIT = SLOTS * RUN
-BLOCK = 512
+BLOCK = 1024
+LIST_BLOCK = 512
 MIB = 1024 * 1024
 TRANS_LEFT = (((0,), (0,)), ((), ()))
 TRANS_RIGHT = (((1,), (1,)), ((), ()))
@@ -374,7 +375,7 @@
     fanout, nodes = near.shape
     parts = mesh_sizes[0] * mesh_sizes[1]
     height = (nodes + halo) // SLOTS
-    in_specs = [lanes(fanout, BLOCK)]
+    in_specs = [lanes(fanout, LIST_BLOCK)]
     operands = [near]
     scratch = []
     if sent is None:
@@ -388,7 +389,7 @@
         blocks = (parts, halo // parts, sent.shape[1])
         in_specs.append(whole(blocks))
         operands.append(sent.reshape(blocks))
-    out_specs = [lanes(height, BLOCK), whole(blocks)]
+    out_specs = [lanes(height, LIST_BLOCK), whole(blocks)]
     out_shape = [
         pltpu.HBM((height, nodes), jnp.int32),
         jax.ShapeDtypeStruct(blocks, jnp.bfloat16),
@@ -398,18 +399,18 @@
         classes, slots, labels, mask = seeds
         in_specs += [whole(slots.shape)] * 3
         operands += [slots, labels, mask]
-        out_specs.append(lanes(classes, BLOCK))
+        out_specs.append(lanes(classes, LIST_BLOCK))
         out_shape.append(jax.ShapeDtypeStruct((classes, nodes), jnp.float32))
     return pl.pallas_call(
         functools.partial(words_kernel, mesh_sizes, kind),
-        grid=(nodes // BLOCK,),
+        grid=(nodes // LIST_BLOCK,),
         in_specs=in_specs,
         out_specs=out_specs,
         out_shape=out_shape,
         scratch_shapes=scratch
         + [
-            pltpu.VMEM((16, BLOCK), jnp.int32),
-            pltpu.VMEM((WORDS, 16, BLOCK), jnp.int32),
+            pltpu.VMEM((16, LIST_BLOCK), jnp.int32),
+            pltpu.VMEM((WORDS, 16, LIST_BLOCK), jnp.int32),
             pltpu.VMEM(blocks, jnp.bfloat16),
         ]
         + semaphores(),
@@ -584,7 +585,7 @@
             pltpu.VMEM((units, padded), jnp.bfloat16),
             pltpu.VMEM((units, 128), jnp.float32),
         ],
-        compiler_params=params(28),
+        compiler_params=params(40),
         name="hidden_layer",
     )(*in_hbm(words), own, own, got, *in_hbm(weight, bias), send_row)
 
@@ -738,7 +739,7 @@
             pltpu.VMEM((classes, 128), jnp.float32),
             pltpu.VMEM((far_height, classes), jnp.float32),
         ],
-        compiler_params=params(28),
+        compiler_params=params(40),
         name="last_layer",
     )(*in_hbm(words), own, own, got, *in_hbm(weight, bias), seeds)
 
@@ -751,15 +752,15 @@
         refs = refs[8:]
     else:
         weight_in, halo_ref, early_ref = refs[:3]
-        state_ref, got_ref, early_sum, notes_ref = refs[3:7]
-        refs = refs[7:]
+        state_ref, got_ref, early_sum, loss_ref, count_ref = refs[3:8]
+        refs = refs[8:]
     padded_ref, counts_ref, sums_ref, self_ref, near_ref, relay_ref, land_ref = refs[:7]
     if flipped:
         high_sems, plane_sems = refs[7:9], refs[9:11]
     else:
-        early_relay, early_part, early_land = refs[7:10]
-        high_sems, plane_sems = refs[10:12], refs[12:14]
-        early_high, early_plane = refs[14:16], refs[16:18]
+        early_relay, early_part, early_land, early_own, early_back = refs[7:12]
+        high_sems, plane_sems = refs[12:14], refs[14:16]
+        early_high, early_plane, back_sems = refs[16:18], refs[18:20], refs[20:22]
     step = pl.program_id(0)
     units, nodes = grad_ref.shape
     width = state_ref.shape[0]
@@ -809,6 +810,23 @@
             early_part[...] = total.astype(jnp.bfloat16).reshape(shape)
             high_start(mesh_sizes, early_part, early_land, early_high)
 
+    if not flipped:
+
+        @pl.when(step == steps - 1)
+        def _():
+            top = split_place(mesh_sizes)[0]
+            high_wait(mesh_sizes, early_land, early_high)
+            early_land[top] = early_part[top]
+            total = jnp.sum(early_land[...].astype(jnp.float32), axis=0)
+            early_own[...] = total.astype(jnp.bfloat16)
+            loss, count = take_terms(total[:, -128:])
+            loss_ref[...] = loss[:1]
+            count_ref[...] = count[:1]
+            each_high(
+                mesh_sizes,
+                lambda other, where: push(early_own, early_back.at[top], back_sems, where),
+            )
+
     def add(row):
         spread_unit(words_ref, row // SLOTS, counts_ref, row)
         added = dot(counts_ref[row : row + UNIT, :], rows_ref[...])
@@ -846,12 +864,9 @@
         got_ref[...] = land_ref[...]
         if not flipped:
             top = split_place(mesh_sizes)[0]
-            high_wait(mesh_sizes, early_land, early_high)
-            early_land[top] = early_part[top]
-            total = jnp.sum(early_land[...].astype(jnp.float32), axis=0)
-            early_sum[...] = total.astype(jnp.bfloat16)
-            for index, value in enumerate(take_terms(total[:, -128:])):
-                notes_ref[index] = value[:1]
+            high_wait(mesh_sizes, early_back, back_sems)
+            early_back[top] = early_own[...]
+            early_sum[...] = early_back[...]
 
 
 def scatter_layer(
@@ -895,17 +910,21 @@
         early_blocks = (high, parts // high, early.shape[0] // parts, early.shape[1])
         in_specs.append(whole(early_blocks))
         operands.append(early.reshape(early_blocks))
-        out_specs += [whole(early_blocks[2:]), whole((2, 1, 1))]
+        summed = (high,) + early_blocks[2:]
+        out_specs += [whole(summed), whole((1, 1)), whole((1, 1))]
         out_shape += [
-            jax.ShapeDtypeStruct(early_blocks[2:], jnp.bfloat16),
-            jax.ShapeDtypeStruct((2, 1, 1), jnp.float32),
+            jax.ShapeDtypeStruct(summed, jnp.bfloat16),
+            jax.ShapeDtypeStruct((1, 1), jnp.float32),
+            jax.ShapeDtypeStruct((1, 1), jnp.float32),
         ]
         scratch = [
             pltpu.VMEM(early_blocks, jnp.bfloat16),
-            pltpu.VMEM((high,) + early_blocks[2:], jnp.bfloat16),
-            pltpu.VMEM((high,) + early_blocks[2:], jnp.bfloat16),
+            pltpu.VMEM(summed, jnp.bfloat16),
+            pltpu.VMEM(summed, jnp.bfloat16),
+            pltpu.VMEM(summed[1:], jnp.bfloat16),
+            pltpu.VMEM(summed, jnp.bfloat16),
         ]
-        scratch += semaphores() * 4
+        scratch += semaphores() * 5
     return pl.pallas_call(
         functools.partial(scatter_kernel, mesh_sizes, fanout, flipped),
         grid=(steps,),
@@ -1049,7 +1068,7 @@
             pltpu.VMEM((far_height, units), jnp.float32),
             pltpu.VMEM((2 * width, units), jnp.float32),
         ],
-        compiler_params=params(26),
+        compiler_params=params(30),
         name="middle_layer",
     )(
         state_grad,
@@ -1064,6 +1083,31 @@
     )
 
 
+def in_two(value):
+    high = value.astype(jnp.bfloat16)
+    return high, (value - high.astype(jnp.float32)).astype(jnp.bfloat16)
+
+
+def product(left, right, dims=(((1,), (0,)), ((), ()))):
+    if left.dtype == jnp.bfloat16:
+        high, low = in_two(right)
+        return dot(left, high, dims) + dot(left, low, dims)
+    high, low = in_two(left)
+    if right.dtype == jnp.bfloat16:
+        return dot(high, right, dims) + dot(low, right, dims)
+    right_high, right_low = in_two(right)
+    return dot(high, right_high, dims) + (
+        dot(high, right_low, dims) + dot(low, right_high, dims)
+    )
+
+
+def moments(turned, first, second):
+    first = beta_one * first + (1.0 - beta_one) * turned
+    second = beta_two * second + (1.0 - beta_two) * turned * turned
+    update = first / (1.0 - beta_one**STEP) / (jnp.sqrt(second / (1.0 - beta_two**STEP)) + epsilon)
+    return first, second, update
+
+
 def bottom_kernel(
     mesh_sizes,
     state_ref,
@@ -1075,41 +1119,33 @@
     sums_two,
     sums_three,
     early_ref,
-    late_ref,
-    early_all,
-    back_ref,
-    sums_ref,
-    weight_ref,
-    relay_ref,
-    land_ref,
-    *sems,
+    count_ref,
+    *refs,
 ):
+    refs = list(refs)
+    kept, refs = refs[:10], refs[10:]
+    late_out, *new, back_ref, sums_ref, weight_ref, late_ref = refs[:11]
+    land_ref, plane_land, part_ref, high_land, whole_ref, last_land = refs[11:17]
+    fetched, refs = refs[17:27], refs[27:]
+    plane_sems, inward, across, outward = refs[:2], refs[2:4], refs[4:6], refs[6:8]
+    fetch_sem = refs[8]
     step = pl.program_id(0)
     units = state_ref.shape[0]
     halo = send_ref.shape[1]
-    high_sems, plane_sems = sems[:2], sems[2:]
+    top, _, _, me = split_place(mesh_sizes)
 
     @pl.when(step == 0)
     def _():
         greet_split(mesh_sizes)
+        for index, (source, target) in enumerate(zip(kept, fetched)):
+            pltpu.make_async_copy(source, target, fetch_sem.at[index]).start()
         back_ref[...] = returned_ref[...].reshape(halo, units).T
         sums_ref[...] = jnp.zeros_like(sums_ref)
         weight_ref[...] = jnp.zeros_like(weight_ref)
         split_greeted(mesh_sizes)
-        top = split_place(mesh_sizes)[0]
-        each_high(
-            mesh_sizes,
-            lambda other, where: push(early_ref, relay_ref.at[top], high_sems, where),
-        )
-
-    @pl.when(step == 3)
-    def _():
-        top, _, _, me = split_place(mesh_sizes)
-        high_wait(mesh_sizes, relay_ref, high_sems)
-        relay_ref[top] = early_ref[...]
         each_plane(
             mesh_sizes,
-            lambda other, where: push(relay_ref, land_ref.at[:, me], plane_sems, where),
+            lambda other, where: push(early_ref, land_ref.at[:, me], plane_sems, where),
         )
 
     grad = active_grad(step, state_ref, preact_ref, back_ref, send_ref)
@@ -1120,7 +1156,6 @@
 
     @pl.when(step == pl.num_programs(0) - 1)
     def _():
-        me = split_place(mesh_sizes)[3]
         padded = weight_ref.shape[1]
         row = 0
         for start in range(0, units, 128):
@@ -1133,8 +1168,7 @@
         for sums in (sums_ref, sums_two, sums_three):
             flat = sums[...].T[:1]
             for start in range(0, flat.shape[1], 128):
-                piece = flat[:, start : start + 128]
-                pieces.append(piece)
+                pieces.append(flat[:, start : start + 128])
         narrow = pieces[-1].shape[1]
         pieces[-1] = jnp.concatenate(
             [pieces[-1], jnp.zeros((1, 128 - narrow), jnp.float32)], axis=1
@@ -1142,24 +1176,89 @@
         rest = late_ref.shape[0] - row
         pieces.append(jnp.zeros((rest - len(pieces), 128), jnp.float32))
         late_ref[row:, :] = jnp.concatenate(pieces).astype(jnp.bfloat16)
+
+        tall = part_ref.shape[0]
+
+        def rows_of(place):
+            return late_ref.at[pl.ds(pl.multiple_of(place * tall, tall), tall)]
+
+        each_plane(
+            mesh_sizes,
+            lambda other, where: push(rows_of(other), plane_land.at[me], inward, where),
+        )
+        for index, (source, target) in enumerate(zip(kept, fetched)):
+            pltpu.make_async_copy(source, target, fetch_sem.at[index]).wait()
+        left_two, right_two, left_three, right_three = fetched[:4]
+        weight_two, first_two, second_two = fetched[4:7]
+        weight_three, first_three, second_three = fetched[7:]
+        share = 1.0 / count_ref[...]
         plane_blocks_wait(mesh_sizes, land_ref, plane_sems)
-        land_ref[:, me] = relay_ref[...]
-        early_all[...] = land_ref[...]
+        land_ref[:, me] = early_ref[...]
+        early = land_ref[...].reshape(-1, land_ref.shape[3])
+        grad = early[:, :units]
+        turned = product(product(left_two[...], grad, TRANS_LEFT), right_two[...]) * share
+        new_first, new_second, update = moments(turned, first_two[...], second_two[...])
+        new[1][...] = new_first
+        new[2][...] = new_second
+
+        plane_wait(mesh_sizes, plane_land, inward)
+        plane_land[me] = late_ref[pl.ds(pl.multiple_of(me * tall, tall), tall), :]
+        part_ref[...] = jnp.sum(plane_land[...].astype(jnp.float32), axis=0).astype(jnp.bfloat16)
+        each_high(
+            mesh_sizes, lambda other, where: push(part_ref, high_land.at[top], across, where)
+        )
+
+        moved = product(product(left_two[...], update), right_two[...], TRANS_RIGHT)
+        new[0][...] = weight_two[...] - step_rates[1] * moved
+
+        high_wait(mesh_sizes, high_land, across)
+        high_land[top] = part_ref[...]
+        whole_ref[...] = jnp.sum(high_land[...].astype(jnp.float32), axis=0).astype(jnp.bfloat16)
+        each_plane(
+            mesh_sizes, lambda other, where: push(whole_ref, last_land.at[me], outward, where)
+        )
+
+        kinds = right_three.shape[0]
+        grad = early[:, units:].astype(jnp.float32).T[:kinds].astype(jnp.bfloat16)
+        turned = product(right_three[...], product(grad, left_three[...]), TRANS_LEFT) * share
+        new_first, new_second, update = moments(turned, first_three[...], second_three[...])
+        new[4][...] = new_first
+        new[5][...] = new_second
+        moved = product(right_three[...], product(update, left_three[...], TRANS_RIGHT))
+        new[3][...] = weight_three[...] - step_rates[2] * moved
+
+        plane_wait(mesh_sizes, last_land, outward)
+        last_land[me] = whole_ref[...]
+        late_out[...] = last_land[...]
 
 
 def bottom_layer(
-    state_grad, preact, returned, send_row, own, mean, sums_two, sums_three, early, mesh_sizes, collective
+    state_grad,
+    preact,
+    returned,
+    send_row,
+    own,
+    mean,
+    sums_two,
+    sums_three,
+    early,
+    count,
+    kept,
+    mesh_sizes,
+    collective,
 ):
     units, nodes = preact.shape
     width = own.shape[0]
     padded = mean.shape[0]
     halo = send_row.shape[1]
-    parts = mesh_sizes[0] * mesh_sizes[1]
     rows = units // 128 * (2 * padded + 2) + -(-sums_three.shape[0] // 128)
     rows = -(-rows // 512) * 512
-    rows = -(-rows // parts) * parts
-    high = split_sizes(mesh_sizes)[0]
-    early_blocks = (high, parts // high) + early.shape
+    high, low, along = split_sizes(mesh_sizes)
+    plane = low * along
+    early_blocks = (high, plane) + early.shape[1:]
+    late_blocks = (plane, rows // plane, 128)
+    hbm = pl.BlockSpec(memory_space=pl.ANY)
+    new = [jax.ShapeDtypeStruct(array.shape, jnp.float32) for array in kept[4:]]
     return pl.pallas_call(
         functools.partial(bottom_kernel, mesh_sizes),
         grid=(nodes // BLOCK,),
@@ -1173,22 +1272,27 @@
             whole(sums_two.shape),
             whole(sums_three.shape),
             whole(early.shape),
-        ],
-        out_specs=[whole((rows, 128)), whole(early_blocks)],
-        out_shape=[
-            jax.ShapeDtypeStruct((rows, 128), jnp.bfloat16),
-            jax.ShapeDtypeStruct(early_blocks, jnp.bfloat16),
-        ],
+            whole(count.shape),
+        ]
+        + [hbm] * len(kept),
+        out_specs=[whole(late_blocks)] + [whole(array.shape) for array in new],
+        out_shape=[jax.ShapeDtypeStruct(late_blocks, jnp.bfloat16)] + new,
         scratch_shapes=[
             pltpu.VMEM((units, halo), jnp.bfloat16),
             pltpu.VMEM((units, 128), jnp.float32),
             pltpu.VMEM((2, padded, units), jnp.float32),
-            pltpu.VMEM((high,) + early.shape, jnp.bfloat16),
+            pltpu.VMEM((rows, 128), jnp.bfloat16),
             pltpu.VMEM(early_blocks, jnp.bfloat16),
+            pltpu.VMEM(late_blocks, jnp.bfloat16),
+            pltpu.VMEM(late_blocks[1:], jnp.bfloat16),
+            pltpu.VMEM((high,) + late_blocks[1:], jnp.bfloat16),
+            pltpu.VMEM(late_blocks[1:], jnp.bfloat16),
+            pltpu.VMEM(late_blocks, jnp.bfloat16),
         ]
-        + semaphores()
-        + semaphores(),
-        compiler_params=params(24, collective),
+        + [pltpu.VMEM(array.shape, array.dtype) for array in kept]
+        + semaphores() * 4
+        + [pltpu.SemaphoreType.DMA((len(kept),))],
+        compiler_params=params(34, collective),
         name="bottom_layer",
     )(
         state_grad,
@@ -1199,159 +1303,32 @@
         sums_two,
         sums_three,
         early,
-    )
-
-
-def in_two(value):
-    high = value.astype(jnp.bfloat16)
-    return high, (value - high.astype(jnp.float32)).astype(jnp.bfloat16)
-
-
-def product(left, right, dims=(((1,), (0,)), ((), ()))):
-    if left.dtype == jnp.bfloat16:
-        high, low = in_two(right)
-        return dot(left, high, dims) + dot(left, low, dims)
-    high, low = in_two(left)
-    if right.dtype == jnp.bfloat16:
-        return dot(high, right, dims) + dot(low, right, dims)
-    right_high, right_low = in_two(right)
-    return dot(high, right_high, dims) + (
-        dot(high, right_low, dims) + dot(low, right_high, dims)
-    )
-
-
-def moments(turned, first, second):
-    first = beta_one * first + (1.0 - beta_one) * turned
-    second = beta_two * second + (1.0 - beta_two) * turned * turned
-    update = first / (1.0 - beta_one**STEP) / (jnp.sqrt(second / (1.0 - beta_two**STEP)) + epsilon)
-    return first, second, update
-
-
-def share_kernel(
-    mesh_sizes,
-    late_ref,
-    early_ref,
-    notes_ref,
-    left_two,
-    right_two,
-    left_three,
-    right_three,
-    first_two,
-    first_three,
-    second_two,
-    second_three,
-    late_out,
-    turned_two,
-    moved_two,
-    turned_three,
-    moved_three,
-    plane_land,
-    part_ref,
-    high_land,
-    whole_ref,
-    *sems,
-):
-    inward, across, outward = sems[:2], sems[2:4], sems[4:]
-    top, _, _, me = split_place(mesh_sizes)
-    units = right_two.shape[0]
-    kinds = right_three.shape[0]
-    share = 1.0 / notes_ref[1]
-    greet_split(mesh_sizes)
-    split_greeted(mesh_sizes)
-    each_plane(
-        mesh_sizes,
-        lambda other, where: push(late_ref.at[other], plane_land.at[me], inward, where),
-    )
-
-    grad = early_ref[:, :units]
-    turned = product(product(left_two[...], grad, TRANS_LEFT), right_two[...]) * share
-    turned_two[...] = turned
-
-    plane_wait(mesh_sizes, plane_land, inward)
-    plane_land[me] = late_ref[me]
-    part_ref[...] = jnp.sum(plane_land[...].astype(jnp.float32), axis=0).astype(jnp.bfloat16)
-    each_high(
-        mesh_sizes, lambda other, where: push(part_ref, high_land.at[top], across, where)
-    )
-
-    update = moments(turned, first_two[...], second_two[...])[2]
-    moved_two[...] = product(product(left_two[...], update), right_two[...], TRANS_RIGHT)
-
-    high_wait(mesh_sizes, high_land, across)
-    high_land[top] = part_ref[...]
-    whole_ref[...] = jnp.sum(high_land[...].astype(jnp.float32), axis=0).astype(jnp.bfloat16)
-    each_plane(
-        mesh_sizes, lambda other, where: push(whole_ref, late_out.at[me], outward, where)
-    )
-
-    grad = early_ref[:, units:].astype(jnp.float32).T[:kinds].astype(jnp.bfloat16)
-    turned = product(right_three[...], product(grad, left_three[...])) * share
-    turned_three[...] = turned
-    update = moments(turned, first_three[...], second_three[...])[2]
-    moved = product(update, left_three[...], TRANS_RIGHT)
-    moved_three[...] = product(right_three[...], moved, TRANS_LEFT)
-
-    plane_wait(mesh_sizes, late_out, outward)
-    late_out[me] = whole_ref[...]
-
-
-def share_sums(late_rows, mesh_sizes, collective, early_all, notes, bases, second_state, third_state):
-    high, low, along = split_sizes(mesh_sizes)
-    blocks = (low * along, late_rows.shape[0] // (low * along), 128)
-    vmem = pl.BlockSpec(memory_space=pltpu.VMEM)
-    operands = [early_all, notes, *in_hbm(*bases, second_state[0], third_state[0])]
-    operands += in_hbm(second_state[1], third_state[1])
-    two = jax.ShapeDtypeStruct(second_state[0].shape, jnp.float32)
-    three = jax.ShapeDtypeStruct(third_state[0].shape, jnp.float32)
-    return pl.pallas_call(
-        functools.partial(share_kernel, mesh_sizes),
-        in_specs=[vmem] * (1 + len(operands)),
-        out_specs=[vmem] * 5,
-        out_shape=[jax.ShapeDtypeStruct(blocks, jnp.bfloat16), two, two, three, three],
-        scratch_shapes=[
-            pltpu.VMEM(blocks, jnp.bfloat16),
-            pltpu.VMEM(blocks[1:], jnp.bfloat16),
-            pltpu.VMEM((high,) + blocks[1:], jnp.bfloat16),
-            pltpu.VMEM(blocks[1:], jnp.bfloat16),
-        ]
-        + semaphores()
-        + semaphores()
-        + semaphores(),
-        compiler_params=pltpu.CompilerParams(
-            vmem_limit_bytes=32 * MIB, collective_id=collective, has_side_effects=True
-        ),
-        name="share_sums",
-    )(late_rows.reshape(blocks), *operands)
+        count,
+        *in_hbm(*kept),
+    )
 
 
 def adam_kernel(
     padded,
     late_ref,
-    notes_ref,
-    turned_two,
-    moved_two,
-    turned_three,
-    moved_three,
+    count_ref,
     weight_one,
-    weight_two,
-    weight_three,
     left_one,
     right_one,
     first_one,
-    first_two,
-    first_three,
     second_one,
-    second_two,
-    second_three,
     bias_ref,
     bias_first,
     bias_second,
-    *outs,
+    *refs,
 ):
-    share = 1.0 / notes_ref[1]
-    units = weight_two.shape[1]
+    ready, refs = refs[:6], refs[6:]
+    outs, sem = refs[:12], refs[12]
+    for index in range(6):
+        pltpu.make_async_copy(ready[index], outs[3 + index], sem.at[index]).start()
+    share = 1.0 / count_ref[...]
+    units = weight_one.shape[1]
     width = weight_one.shape[0] // 2
-    kinds = weight_three.shape[0]
 
     late_rows = late_ref[...].astype(jnp.float32)
     columns = []
@@ -1370,41 +1347,37 @@
     moved = product(product(left_one[...], update), right_one[...], TRANS_RIGHT)
     outs[0][...] = weight_one[...] - step_rates[0] * moved
 
-    new_first, new_second, _ = moments(turned_two[...], first_two[...], second_two[...])
-    outs[3][...] = weight_two[...] - step_rates[1] * moved_two[...]
-    outs[4][...] = new_first
-    outs[5][...] = new_second
-    new_first, new_second, _ = moments(turned_three[...], first_three[...], second_three[...])
-    outs[6][...] = weight_three[...] - step_rates[2] * moved_three[...]
-    outs[7][...] = new_first
-    outs[8][...] = new_second
-
     row = units // 128 * 2 * padded
+    size = bias_ref.shape[0]
     pieces = []
-    while len(pieces) * 128 < 2 * units + kinds:
+    while len(pieces) * 128 < size:
         pieces.append(late_rows[row : row + 1])
         row += 1
-    grad = jnp.concatenate(pieces, axis=1)[:, : 2 * units + kinds] * share
+    grad = jnp.concatenate(pieces, axis=1)[:, :size] * share
     flat = bias_ref.shape
     bias, first, second = (ref[...].reshape(grad.shape) for ref in (bias_ref, bias_first, bias_second))
     new_first, new_second, update = moments(grad, first, second)
     outs[9][...] = (bias - bias_rate * (update + weight_decay * bias)).reshape(flat)
     outs[10][...] = new_first.reshape(flat)
     outs[11][...] = new_second.reshape(flat)
-
-
-def adam(padded, late_all, notes, steps, *state):
+    for index in range(6):
+        pltpu.make_async_copy(ready[index], outs[3 + index], sem.at[index]).wait()
+
+
+def adam(padded, late_all, count, state, ready):
     vmem = pl.BlockSpec(memory_space=pltpu.VMEM)
-    order = (0, 5, 8, 1, 6, 9, 2, 7, 10, 11, 12, 13)
-    outs = [jax.ShapeDtypeStruct(state[at].shape, jnp.float32) for at in order]
+    hbm = pl.BlockSpec(memory_space=pl.ANY)
+    one, bias = state[0], state[5]
+    shapes = [one.shape] * 3 + [array.shape for array in ready] + [bias.shape] * 3
     return pl.pallas_call(
         functools.partial(adam_kernel, padded),
-        in_specs=[vmem] * (2 + len(steps) + len(state)),
-        out_specs=[vmem] * len(outs),
-        out_shape=outs,
-        compiler_params=pltpu.CompilerParams(vmem_limit_bytes=32 * MIB),
+        in_specs=[vmem] * (2 + len(state)) + [hbm] * len(ready),
+        out_specs=[vmem] * 3 + [hbm] * 6 + [vmem] * 3,
+        out_shape=[jax.ShapeDtypeStruct(shape, jnp.float32) for shape in shapes],
+        scratch_shapes=[pltpu.SemaphoreType.DMA((6,))],
+        compiler_params=pltpu.CompilerParams(vmem_limit_bytes=24 * MIB),
         name="adam",
-    )(late_all, notes, *steps, *in_hbm(*state))
+    )(late_all, count, *in_hbm(*state), *ready)
 
 
 def on_device(
@@ -1454,6 +1427,7 @@
     words_one, got = count_words(
         neighbors_one.T, mesh_sizes, 0, halo, feats=feats, send_row=send_row
     )
+    feats = in_hbm(feats)[0]
     state_one, preact_one, sent, mean_one = hidden_layer(
         words_one, feats, got, weight_one, bias_all, 0, send_row, fans[0]
     )
@@ -1491,10 +1465,10 @@
         notes,
         fans[1],
     )
-    state_grad, returned, early_sum, notes = scatter_layer(
+    state_grad, returned, early_sum, loss, count = scatter_layer(
         words_two, grad_two, rows_two, weight_two, halo_grad, mesh_sizes, 4, fans[1], early=early
     )
-    late_rows, early_all = bottom_layer(
+    late_all, *ready = bottom_layer(
         state_grad,
         preact_one,
         returned,
@@ -1504,42 +1478,40 @@
         sums_two,
         sums_three,
         early_sum,
+        count,
+        (
+            left_two,
+            right_two,
+            left_three,
+            right_three,
+            weight_two,
+            first_two,
+            second_two,
+            weight_three,
+            first_three.T,
+            second_three.T,
+        ),
         mesh_sizes,
         5,
     )
-    first_three, second_three = first_three.T, second_three.T
-    late_all, *steps = share_sums(
-        late_rows,
-        mesh_sizes,
-        6,
-        early_all.reshape(early.shape),
-        notes,
-        (left_two, right_two, left_three, right_three.T),
-        (first_two, second_two),
-        (first_three, second_three),
-    )
     out = adam(
         mean_one.shape[0],
-        late_all.reshape(late_rows.shape),
-        notes,
-        steps,
-        weight_one,
-        weight_two,
-        weight_three,
-        left_one,
-        right_one,
-        first_one,
-        first_two,
-        first_three,
-        second_one,
-        second_two,
-        second_three,
-        bias_all,
-        bias_first,
-        bias_second,
+        late_all.reshape(-1, 128),
+        count,
+        (
+            weight_one,
+            left_one,
+            right_one,
+            first_one,
+            second_one,
+            bias_all,
+            bias_first,
+            bias_second,
+        ),
+        ready,
     )
     third = [value.T for value in out[6:9]]
-    return (*out[:6], *third, *out[9:12], notes[0, 0, 0], notes[1, 0, 0])
+    return (*out[:6], *third, *out[9:12], loss.reshape(()), count.reshape(()))
 
 
 def solution(mesh):

time: 177 us -> 171 us (0.966)
  Pallas kernels: 172 us -> 165 us
  between operations: 0.78 us -> 4.25 us
  local copies, waits for them, and re-layouts: 3.24 us -> 0.87 us
    pallas_call x1 -> x0, Pallas kernels: 14.8 us -> none  [share_sums(): pl.pallas_call(functools.partial(share_kernel, mesh_sizes), in_specs=[vme...]
    pallas_call x1, Pallas kernels: 12.1 us -> 20.9 us  [bottom_layer(): pl.pallas_call(functools.partial(bottom_kernel, mesh_sizes), grid=(nodes...]
    pallas_call x2, Pallas kernels: 35.2 us -> 37.3 us  [scatter_layer(): pl.pallas_call(functools.partial(scatter_kernel, mesh_sizes, fanout, flip...]
    unnamed x12 -> x7, local copies, waits for them, and re-layouts: 2.64 us -> 0.79 us
where the time goes in v3:
time: 171 us; the launch traced here: 170 us
  Pallas kernels  165 us (96%)
  between operations  4.25 us (2%)
    pallas_call x3, Pallas kernels, count_words(): pl.pallas_call(functools.partial(words_kernel, mesh_sizes, kind), grid=(n...  42.1 us
    pallas_call x2, Pallas kernels, scatter_layer(): pl.pallas_call(functools.partial(scatter_kernel, mesh_sizes, fanout, flip...  37.3 us
    pallas_call x2, Pallas kernels, hidden_layer(): pl.pallas_call(functools.partial(hidden_kernel, fanout, bias_start), grid...  35.5 us
    pallas_call x1, Pallas kernels, bottom_layer(): pl.pallas_call(functools.partial(bottom_kernel, mesh_sizes), grid=(nodes...  20.9 us
    pallas_call x1, Pallas kernels, last_layer(): pl.pallas_call(functools.partial(last_kernel, fanout, bias_start), grid=(...  14.8 us
    pallas_call x1, Pallas kernels, middle_layer(): pl.pallas_call(functools.partial(middle_kernel, fanout), grid=(nodes // B...  10.1 us
    pallas_call x1, Pallas kernels, adam(): pl.pallas_call(functools.partial(adam_kernel, padded), in_specs=[vmem] *...  4.12 us

profile of v3, /device:TPU:0, one launch (start us, length us, event | category | flops | bytes accessed | tf_op | source)
XLA Modules:
  0.0 170.0 jit_solution(5538093241276943852)
XLA Ops:
  0.6 0.8 copy.41
  1.4 0.1 reshape.64.refs_1_.send_ref
  1.5 16.7 %count_words.3 = (s32[576,4096]{1,0:T(8,128)}, bf16[32,16,128]{2,1,0:T(8,128)(2,1)S(1)}) custom-call(s32[15,4096]{1,0:T(8,128)} %bitcast.37, bf16[100,4096]{1,0:T(8,128)(2,1)} %bitcast.30, s32[1,512]{1,0:T(1,128)S(1)} %reshape.64.refs_1_.send_ref), custom_call_target="tpu_custom_call" | custom-call | tf_op jit(solution)/shard_map/count_words/pallas_call | solution.py:404
  18.2 15.9 %hidden_layer.2 = (bf16[256,4096]{1,0:T(8,128)(2,1)S(1)}, f32[256,4096]{1,0:T(8,128)}, bf16[512,256]{1,0:T(8,128)(2,1)S(1)}, bf16[112,4096]{1,0:T(8,128)(2,1)}) custom-call(s32[576,4096]{1,0:T(8,128)} %get-tuple-element.68.words_ref, bf16[100,4096]{1,0:T(8,128)(2,1)} %bitcast.31, bf16[100,4096]{1,0:T(8,128)(2,1)} %bitcast.32, ...), custom_call_target="tpu_custom_call" | custom-call | tf_op jit(solution)/shard_map/hidden_layer/pallas_call | solution.py:555
  34.1 10.5 %count_words.4 = (s32[576,4096]{1,0:T(8,128)}, bf16[32,16,256]{2,1,0:T(8,128)(2,1)S(1)}) custom-call(s32[10,4096]{1,0:T(8,128)} %bitcast.38, bf16[32,16,256]{2,1,0:T(8,128)(2,1)S(1)} %bitcast.24), custom_call_target="tpu_custom_call" | custom-call | tf_op jit(solution)/shard_map/count_words/pallas_call | solution.py:404
  44.6 0.0 copy-start
  44.6 0.0 copy-start.1
  44.6 0.0 copy-start.2
  44.6 19.6 %hidden_layer.3 = (bf16[256,4096]{1,0:T(8,128)(2,1)S(1)}, f32[256,4096]{1,0:T(8,128)}, bf16[512,256]{1,0:T(8,128)(2,1)S(1)}, bf16[256,4096]{1,0:T(8,128)(2,1)}) custom-call(s32[576,4096]{1,0:T(8,128)} %get-tuple-element.71.words_ref, bf16[256,4096]{1,0:T(8,128)(2,1)S(1)} %get-tuple-element.72.own_ref.own_block, ...), custom_call_target="tpu_custom_call" | custom-call | tf_op jit(solution)/shard_map/hidden_layer/pallas_call | solution.py:555
  64.2 0.0 copy-done
  64.2 0.0 copy-done.1
  64.2 0.0 copy-done.2
  64.2 15.0 %count_words.5 = (s32[576,4096]{1,0:T(8,128)}, bf16[32,16,256]{2,1,0:T(8,128)(2,1)S(1)}, f32[48,4096]{1,0:T(8,128)S(1)}) custom-call(s32[5,4096]{1,0:T(8,128)} %bitcast.39, bf16[32,16,256]{2,1,0:T(8,128)(2,1)S(1)} %bitcast.25, s32[1,2048]{1,0:T(1,128)S(1)} %bitcast.27, s32[1,2048]{1,0:T(1,128)S(1)} %bitcast.28, s32[1,2048]{1,0:T(1,128)S(1)} %bitcast.29), custom_call_target="tpu_custom_call" | custom-call | tf_op jit(solution)/shard_map/count_words/pallas_call | solution.py:404
  79.2 14.8 %last_layer.1 = (bf16[48,4096]{1,0:T(8,128)(2,1)S(1)}, bf16[4096,48]{1,0:T(8,128)(2,1)S(1)}, f32[48,128]{1,0:T(8,128)S(1)}, f32[16,128]{1,0:T(8,128)S(1)}, bf16[...) custom-call(s32[576,4096]{1,0:T(8,128)} %get-tuple-element.75.words_ref, ...), custom_call_target="tpu_custom_call" | custom-call | tf_op jit(solution)/shard_map/last_layer/pallas_call | solution.py:703
  94.0 17.0 %scatter_layer.2 = (f32[256,4608]{1,0:T(8,128)S(1)}, bf16[4,8,16,256]{3,2,1,0:T(8,128)(2,1)S(1)}, f32[512,48]{1,0:T(8,128)S(1)}) custom-call(s32[576,4096]{1,0:T(8,128)} %get-tuple-element.75.words_ref, bf16[48,4096]{1,0:T(8,128)(2,1)S(1)} %get-tuple-element.79.grad_ref, bf16[4096,48]{1,0:T(8,128)(2,1)S(1)} %get-tuple-element.80.rows_ref, ...), custom_call_target="tpu_custom_call" | custom-call | tf_op jit(solution)/shard_map/scatter_layer/pallas_call | solution.py:928
  111.1 10.1 %middle_layer.1 = (bf16[256,4096]{1,0:T(8,128)(2,1)S(1)}, bf16[4096,256]{1,0:T(8,128)(2,1)S(1)}, f32[256,128]{1,0:T(8,128)S(1)}, bf16[512,256]{1,0:T(8,128)(2,1)S(1)}, bf16[512,384]{1,0:T(8,128)(2,1)S(1)}) custom-call(f32[256,4608]{1,0:T(8,128)S(1)} %get-tuple-element.84.state_ref, f32[256,4096]{1,0:T(8,128)} %get-tuple-element.85.preact_ref, ...), custom_call_target="tpu_custom_call" | custom-call | tf_op jit(solution)/shard_map/middle_layer/pallas_call | solution.py:1036
  121.2 20.3 %scatter_layer.3 = (f32[256,4608]{1,0:T(8,128)S(1)}, bf16[4,8,16,256]{3,2,1,0:T(8,128)(2,1)S(1)}, bf16[4,16,384]{2,1,0:T(8,128)(2,1)S(1)}, f32[1,1]{1,0:T(1,128)}, f32[1,1]{1,0:T(1,128)}) custom-call(s32[576,4096]{1,0:T(8,128)} %get-tuple-element.71.words_ref, bf16[256,4096]{1,0:T(8,128)(2,1)S(1)} %get-tuple-element.90.grad_ref, ...), custom_call_target="tpu_custom_call" | custom-call | tf_op jit(solution)/shard_map/scatter_layer/pallas_call | solution.py:928
  141.5 20.9 %bottom_layer.1 = (bf16[8,64,128]{2,1,0:T(8,128)(2,1)S(1)}, f32[512,256]{1,0:T(8,128)S(1)}, f32[512,256]{1,0:T(8,128)S(1)}, f32[512,256]{1,0:T(8,128)S(1)}, f32[...) custom-call(f32[256,4608]{1,0:T(8,128)S(1)} %get-tuple-element.94.state_ref, ...), custom_call_target="tpu_custom_call" | custom-call | tf_op jit(solution)/shard_map/bottom_layer/pallas_call | solution.py:1262
  162.4 4.1 %adam.1 = (f32[200,256]{1,0:T(8,128)}, f32[200,256]{1,0:T(8,128)}, f32[200,256]{1,0:T(8,128)}, f32[512,256]{1,0:T(8,128)}, f32[512,256]{1,0:T(8,128)}, /*index=5...) custom-call(bf16[512,128]{1,0:T(8,128)(2,1)S(1)} %bitcast.26, ...), custom_call_target="tpu_custom_call" | custom-call | tf_op jit(solution)/shard_map/adam/pallas_call | solution.py:1372
Async XLA Ops:
  44.6 19.6 %copy-start = (s32[2048]{0:T(1024)S(1)}, s32[2048]{0:T(1024)}, u32[]{:S(2)}) copy-start(s32[2048]{0:T(1024)} %param.28) | copy-start | bytes 24580
  44.6 19.6 %copy-start.1 = (s32[2048]{0:T(1024)S(1)}, s32[2048]{0:T(1024)}, u32[]{:S(2)}) copy-start(s32[2048]{0:T(1024)} %param.27) | copy-start | bytes 24580
  44.6 19.6 %copy-start.2 = (s32[2048]{0:T(1024)S(1)}, s32[2048]{0:T(1024)}, u32[]{:S(2)}) copy-start(s32[2048]{0:T(1024)} %param.29) | copy-start | bytes 24580

commit v4 on v3

--- a/solution.py
+++ b/solution.py
@@ -309,6 +309,21 @@
     return [pltpu.SemaphoreType.DMA, pltpu.SemaphoreType.DMA]
 
 
+def one_row(rows):
+    per, parts = rows.shape
+    column = lax.broadcasted_iota(jnp.int32, (parts, parts * per), 1)
+    owner = lax.broadcasted_iota(jnp.int32, (parts, parts * per), 0)
+    rest = column - owner * per
+    mine = jnp.where((rest >= 0) & (rest < per), 1.0, 0.0).astype(jnp.bfloat16)
+    high = (rows >> 7).astype(jnp.float32).astype(jnp.bfloat16)
+    low = (rows & 127).astype(jnp.float32).astype(jnp.bfloat16)
+    wide = dot(high, mine) * 128.0 + dot(low, mine)
+    column = lax.broadcasted_iota(jnp.int32, wide.shape, 1)
+    at = lax.broadcasted_iota(jnp.int32, wide.shape, 0)
+    picked = jnp.where(column - floor_over(column, per) * per == at, wide, 0.0)
+    return jnp.sum(picked, axis=0, keepdims=True).astype(jnp.int32)
+
+
 def chosen_nodes(send_row, start, count):
     node = lax.broadcasted_iota(jnp.int32, (count, send_row.shape[1]), 0) + start
     return jnp.where(node == send_row, 1.0, 0.0).astype(jnp.bfloat16)
@@ -317,8 +332,8 @@
 def words_kernel(mesh_sizes, kind, near_ref, *refs):
     refs = list(refs)
     if kind == "features":
-        feats_ref, send_ref, out_ref, got_ref, sent_ref = refs[:5]
-        refs = refs[5:]
+        feats_ref, send_ref, out_ref, got_ref, row_ref, sent_ref = refs[:6]
+        refs = refs[6:]
     elif kind == "seeds":
         sent_ref, slots_ref, labels_ref, mask_ref, out_ref, got_ref, seeds_ref = refs[:7]
         refs = refs[7:]
@@ -339,10 +354,11 @@
         @pl.when(step == 0)
         def _():
             width, nodes = feats_ref.shape
-            halo = send_ref.shape[1]
+            halo = row_ref.shape[1]
+            row_ref[...] = one_row(send_ref[...])
             total = jnp.zeros((width, halo), jnp.float32)
             for start in range(0, nodes, block):
-                chosen = chosen_nodes(send_ref[...], start, block)
+                chosen = chosen_nodes(row_ref[...], start, block)
                 total = total + dot(feats_ref[:, start : start + block], chosen)
             padded = sent_ref.shape[2]
             total = jnp.concatenate([total, jnp.zeros((padded - width, halo), jnp.float32)])
@@ -371,7 +387,17 @@
         got_ref[...] = land_ref[...]
 
 
-def count_words(near, mesh_sizes, collective, halo, sent=None, feats=None, send_row=None, seeds=None):
+def words_space(table, near):
+    return pltpu.VMEM if near and table <= 5120 else pltpu.HBM
+
+
+def place_words(words, near):
+    return pltpu.with_memory_space_constraint(words, words_space(words.shape[0] * SLOTS, near))
+
+
+def count_words(
+    near, mesh_sizes, collective, halo, sent=None, feats=None, send_rows=None, seeds=None
+):
     fanout, nodes = near.shape
     parts = mesh_sizes[0] * mesh_sizes[1]
     height = (nodes + halo) // SLOTS
@@ -381,8 +407,8 @@
     if sent is None:
         kind = "features"
         blocks = (parts, halo // parts, -(-feats.shape[0] // 128) * 128)
-        in_specs += [whole(feats.shape), whole(send_row.shape)]
-        operands += [*in_hbm(feats), send_row]
+        in_specs += [whole(feats.shape), whole(send_rows.shape)]
+        operands += in_hbm(feats, send_rows)
         scratch.append(pltpu.VMEM(blocks, jnp.bfloat16))
     else:
         kind = "plain"
@@ -391,9 +417,14 @@
         operands.append(sent.reshape(blocks))
     out_specs = [lanes(height, LIST_BLOCK), whole(blocks)]
     out_shape = [
-        pltpu.HBM((height, nodes), jnp.int32),
+        words_space(nodes + halo, sent is None)(
+            (height, nodes), jnp.int32
+        ),
         jax.ShapeDtypeStruct(blocks, jnp.bfloat16),
     ]
+    if sent is None:
+        out_specs.append(whole((1, halo)))
+        out_shape.append(jax.ShapeDtypeStruct((1, halo), jnp.int32))
     if seeds is not None:
         kind = "seeds"
         classes, slots, labels, mask = seeds
@@ -525,6 +556,8 @@
     def finish():
         mean = mean_ref[...]
         extra_ref[...] = mean
+        if padded > width:
+            extra_ref[width : width + 1, :] = jnp.ones((1, block), jnp.bfloat16)
         preact = dot(self_ref[...], own_block[...]) + dot(near_ref[...], mean) + bias_col[:, :1]
         preact_ref[...] = preact
         active = preact * jax.nn.sigmoid(preact)
@@ -550,7 +583,7 @@
     halo = send_row.shape[1]
     table = nodes + halo
     units = weight.shape[1]
-    padded = -(-width // 16) * 16
+    padded = width if width == units else (width // 16 + 1) * 16
     steps = nodes // BLOCK
     return pl.pallas_call(
         functools.partial(hidden_kernel, fanout, bias_start),
@@ -587,11 +620,15 @@
         ],
         compiler_params=params(40),
         name="hidden_layer",
-    )(*in_hbm(words), own, own, got, *in_hbm(weight, bias), send_row)
+    )(place_words(words, width != units), own, own, got, *in_hbm(weight, bias), send_row)
 
 
 def far_start(nodes):
     return nodes // UNIT * UNIT
+
+
+def column_sums(rows):
+    return dot(jnp.ones((16, rows.shape[0]), jnp.bfloat16), rows)
 
 
 def unscaled(sums, fanout):
@@ -673,11 +710,11 @@
         grad = (powers / total * uses - seeds).astype(jnp.bfloat16)
         grad_ref[...] = grad
         loss = uses * normer - jnp.sum(seeds * logits, axis=0, keepdims=True)
-        sums_ref[...] += jnp.sum(grad.astype(jnp.float32), axis=1, keepdims=True)
         notes_ref[:8, :] += jnp.sum(loss)
         notes_ref[8:, :] += jnp.sum(uses)
         rows = grad.T
         rows_ref[...] = rows
+        sums_ref[...] += column_sums(rows)
         far_sums[...] += dot(counts_ref[first:, :], rows)
 
     @pl.when(step < last)
@@ -715,7 +752,7 @@
         out_specs=[
             late(classes, BLOCK),
             pl.BlockSpec((BLOCK, classes), lambda i: (jnp.maximum(i - 1, 0), 0)),
-            whole((classes, 128)),
+            whole((16, classes)),
             whole((16, 128)),
             whole((width, table)),
             whole((halo, classes)),
@@ -724,7 +761,7 @@
         out_shape=[
             jax.ShapeDtypeStruct((classes, nodes), jnp.bfloat16),
             jax.ShapeDtypeStruct((nodes, classes), jnp.bfloat16),
-            jax.ShapeDtypeStruct((classes, 128), jnp.float32),
+            jax.ShapeDtypeStruct((16, classes), jnp.float32),
             jax.ShapeDtypeStruct((16, 128), jnp.float32),
             jax.ShapeDtypeStruct((width, table), jnp.bfloat16),
             jax.ShapeDtypeStruct((halo, classes), jnp.bfloat16),
@@ -1000,9 +1037,9 @@
         spread_unit(words_ref, (row - base) // SLOTS, counts_ref, row - first)
     grad = active_grad(step, state_ref, preact_ref, back_ref, send_ref)
     grad_ref[...] = grad
-    sums_ref[...] += jnp.sum(grad.astype(jnp.float32), axis=1, keepdims=True)
     rows = grad.T
     rows_ref[...] = rows
+    sums_ref[...] += column_sums(rows)
     far_sums[...] += dot(counts_ref[...], rows)
     width = own_block.shape[0]
     total_ref[:width, :] += dot(own_block[...], rows)
@@ -1051,14 +1088,14 @@
         out_specs=[
             lanes(units, BLOCK),
             pl.BlockSpec((BLOCK, units), lambda i: (i, 0)),
-            whole((units, 128)),
+            whole((16, units)),
             whole((halo, units)),
             whole((2 * width, wide)),
         ],
         out_shape=[
             jax.ShapeDtypeStruct((units, nodes), jnp.bfloat16),
             jax.ShapeDtypeStruct((nodes, units), jnp.bfloat16),
-            jax.ShapeDtypeStruct((units, 128), jnp.float32),
+            jax.ShapeDtypeStruct((16, units), jnp.float32),
             jax.ShapeDtypeStruct((halo, units), jnp.bfloat16),
             jax.ShapeDtypeStruct((2 * width, wide), jnp.bfloat16),
         ],
@@ -1124,9 +1161,9 @@
 ):
     refs = list(refs)
     kept, refs = refs[:10], refs[10:]
-    late_out, *new, back_ref, sums_ref, weight_ref, late_ref = refs[:11]
-    land_ref, plane_land, part_ref, high_land, whole_ref, last_land = refs[11:17]
-    fetched, refs = refs[17:27], refs[27:]
+    late_out, *new, back_ref, weight_ref, late_ref = refs[:10]
+    land_ref, plane_land, part_ref, high_land, whole_ref, last_land = refs[10:16]
+    fetched, refs = refs[16:26], refs[26:]
     plane_sems, inward, across, outward = refs[:2], refs[2:4], refs[4:6], refs[6:8]
     fetch_sem = refs[8]
     step = pl.program_id(0)
@@ -1140,8 +1177,19 @@
         for index, (source, target) in enumerate(zip(kept, fetched)):
             pltpu.make_async_copy(source, target, fetch_sem.at[index]).start()
         back_ref[...] = returned_ref[...].reshape(halo, units).T
-        sums_ref[...] = jnp.zeros_like(sums_ref)
         weight_ref[...] = jnp.zeros_like(weight_ref)
+        pieces = []
+        for sums in (sums_two, sums_three):
+            for start in range(0, sums.shape[1], 128):
+                pieces.append(sums[:1, start : start + 128])
+        narrow = pieces[-1].shape[1]
+        pieces[-1] = jnp.concatenate(
+            [pieces[-1], jnp.zeros((1, 128 - narrow), jnp.float32)], axis=1
+        )
+        row = units // 128 * 2 * weight_ref.shape[1]
+        rest = late_ref.shape[0] - row
+        pieces.append(jnp.zeros((rest - len(pieces), 128), jnp.float32))
+        late_ref[row:, :] = jnp.concatenate(pieces).astype(jnp.bfloat16)
         split_greeted(mesh_sizes)
         each_plane(
             mesh_sizes,
@@ -1149,7 +1197,6 @@
         )
 
     grad = active_grad(step, state_ref, preact_ref, back_ref, send_ref)
-    sums_ref[...] += jnp.sum(grad.astype(jnp.float32), axis=1, keepdims=True)
     width = own_block.shape[0]
     weight_ref[0, :width, :] += dot(own_block[...], grad, TRANS_RIGHT)
     weight_ref[1] += dot(mean_block[...], grad, TRANS_RIGHT)
@@ -1164,19 +1211,6 @@
                     jnp.bfloat16
                 )
                 row += padded
-        pieces = []
-        for sums in (sums_ref, sums_two, sums_three):
-            flat = sums[...].T[:1]
-            for start in range(0, flat.shape[1], 128):
-                pieces.append(flat[:, start : start + 128])
-        narrow = pieces[-1].shape[1]
-        pieces[-1] = jnp.concatenate(
-            [pieces[-1], jnp.zeros((1, 128 - narrow), jnp.float32)], axis=1
-        )
-        rest = late_ref.shape[0] - row
-        pieces.append(jnp.zeros((rest - len(pieces), 128), jnp.float32))
-        late_ref[row:, :] = jnp.concatenate(pieces).astype(jnp.bfloat16)
-
         tall = part_ref.shape[0]
 
         def rows_of(place):
@@ -1251,7 +1285,7 @@
     width = own.shape[0]
     padded = mean.shape[0]
     halo = send_row.shape[1]
-    rows = units // 128 * (2 * padded + 2) + -(-sums_three.shape[0] // 128)
+    rows = units // 128 * (2 * padded + 1) + -(-sums_three.shape[1] // 128)
     rows = -(-rows // 512) * 512
     high, low, along = split_sizes(mesh_sizes)
     plane = low * along
@@ -1279,7 +1313,6 @@
         out_shape=[jax.ShapeDtypeStruct(late_blocks, jnp.bfloat16)] + new,
         scratch_shapes=[
             pltpu.VMEM((units, halo), jnp.bfloat16),
-            pltpu.VMEM((units, 128), jnp.float32),
             pltpu.VMEM((2, padded, units), jnp.float32),
             pltpu.VMEM((rows, 128), jnp.bfloat16),
             pltpu.VMEM(early_blocks, jnp.bfloat16),
@@ -1347,9 +1380,12 @@
     moved = product(product(left_one[...], update), right_one[...], TRANS_RIGHT)
     outs[0][...] = weight_one[...] - step_rates[0] * moved
 
-    row = units // 128 * 2 * padded
     size = bias_ref.shape[0]
     pieces = []
+    for start in range(0, units, 128):
+        row = start // 128 * 2 * padded + padded + width
+        pieces.append(late_rows[row : row + 1])
+    row = units // 128 * 2 * padded
     while len(pieces) * 128 < size:
         pieces.append(late_rows[row : row + 1])
         row += 1
@@ -1414,7 +1450,6 @@
     halo = send_rows.size
     fans = (neighbors_one.shape[1], neighbors_two.shape[1], neighbors_three.shape[1])
     feats = features.T
-    send_row = send_rows.reshape(1, halo)
     weight_three = weight_three.T
     padded_classes = -(-classes // 16) * 16
     seed_slots = (
@@ -1424,8 +1459,8 @@
         seed_mask.reshape(1, -1),
     )
 
-    words_one, got = count_words(
-        neighbors_one.T, mesh_sizes, 0, halo, feats=feats, send_row=send_row
+    words_one, got, send_row = count_words(
+        neighbors_one.T, mesh_sizes, 0, halo, feats=feats, send_rows=send_rows.T
     )
     feats = in_hbm(feats)[0]
     state_one, preact_one, sent, mean_one = hidden_layer(

time: 171 us -> 169 us (0.988)
  no operation moved by 1% of the time
where the time goes in v4:
time: 169 us
  Pallas kernels  164 us (97%)
  between operations  4.25 us (3%)
    pallas_call x3, Pallas kernels, count_words(): pl.pallas_call(functools.partial(words_kernel, mesh_sizes, kind), grid=(n...  41.9 us
    pallas_call x2, Pallas kernels, scatter_layer(): pl.pallas_call(functools.partial(scatter_kernel, mesh_sizes, fanout, flip...  37.3 us
    pallas_call x2, Pallas kernels, hidden_layer(): pl.pallas_call(functools.partial(hidden_kernel, fanout, bias_start), grid...  35.4 us
    pallas_call x1, Pallas kernels, bottom_layer(): pl.pallas_call(functools.partial(bottom_kernel, mesh_sizes), grid=(nodes...  20.5 us
    pallas_call x1, Pallas kernels, last_layer(): pl.pallas_call(functools.partial(last_kernel, fanout, bias_start), grid=(...  15.1 us
    pallas_call x1, Pallas kernels, middle_layer(): pl.pallas_call(functools.partial(middle_kernel, fanout), grid=(nodes // B...  10.2 us
    pallas_call x1, Pallas kernels, adam(): pl.pallas_call(functools.partial(adam_kernel, padded), in_specs=[vmem] *...  4.12 us

profile of v4, /device:TPU:0, one launch (start us, length us, event | category | flops | bytes accessed | tf_op | source)
XLA Modules:
  0.0 168.7 jit_solution(246243744979503099)
XLA Ops:
  0.6 16.2 %count_words.3 = (s32[576,4096]{1,0:T(8,128)S(1)}, bf16[32,16,128]{2,1,0:T(8,128)(2,1)S(1)}, s32[1,512]{1,0:T(1,128)S(1)}) custom-call(s32[15,4096]{1,0:T(8,128)} %bitcast.38, bf16[100,4096]{1,0:T(8,128)(2,1)} %bitcast.31, s32[16,32]{1,0:T(8,128)} %bitcast.43), custom_call_target="tpu_custom_call" | custom-call | tf_op jit(solution)/shard_map/count_words/pallas_call | solution.py:435
  16.9 15.9 %hidden_layer.2 = (bf16[256,4096]{1,0:T(8,128)(2,1)S(1)}, f32[256,4096]{1,0:T(8,128)}, bf16[512,256]{1,0:T(8,128)(2,1)S(1)}, bf16[112,4096]{1,0:T(8,128)(2,1)}) custom-call(s32[576,4096]{1,0:T(8,128)S(1)} %get-tuple-element.69.words_ref, bf16[100,4096]{1,0:T(8,128)(2,1)} %bitcast.32, bf16[100,4096]{1,0:T(8,128)(2,1)} %bitcast.33, ...), custom_call_target="tpu_custom_call" | custom-call | tf_op jit(solution)/shard_map/hidden_layer/pallas_call | solution.py:588
  32.7 10.7 %count_words.4 = (s32[576,4096]{1,0:T(8,128)}, bf16[32,16,256]{2,1,0:T(8,128)(2,1)S(1)}) custom-call(s32[10,4096]{1,0:T(8,128)} %bitcast.39, bf16[32,16,256]{2,1,0:T(8,128)(2,1)S(1)} %bitcast.25), custom_call_target="tpu_custom_call" | custom-call | tf_op jit(solution)/shard_map/count_words/pallas_call | solution.py:435
  43.4 0.0 copy-start
  43.4 0.0 copy-start.1
  43.5 0.0 copy-start.2
  43.5 19.6 %hidden_layer.3 = (bf16[256,4096]{1,0:T(8,128)(2,1)S(1)}, f32[256,4096]{1,0:T(8,128)}, bf16[512,256]{1,0:T(8,128)(2,1)S(1)}, bf16[256,4096]{1,0:T(8,128)(2,1)}) custom-call(s32[576,4096]{1,0:T(8,128)} %get-tuple-element.73.words_ref, bf16[256,4096]{1,0:T(8,128)(2,1)S(1)} %get-tuple-element.74.own_ref.own_block, ...), custom_call_target="tpu_custom_call" | custom-call | tf_op jit(solution)/shard_map/hidden_layer/pallas_call | solution.py:588
  63.0 0.0 copy-done
  63.0 0.0 copy-done.1
  63.0 0.0 copy-done.2
  63.0 14.9 %count_words.5 = (s32[576,4096]{1,0:T(8,128)}, bf16[32,16,256]{2,1,0:T(8,128)(2,1)S(1)}, f32[48,4096]{1,0:T(8,128)S(1)}) custom-call(s32[5,4096]{1,0:T(8,128)} %bitcast.40, bf16[32,16,256]{2,1,0:T(8,128)(2,1)S(1)} %bitcast.26, s32[1,2048]{1,0:T(1,128)S(1)} %bitcast.28, s32[1,2048]{1,0:T(1,128)S(1)} %bitcast.29, s32[1,2048]{1,0:T(1,128)S(1)} %bitcast.30), custom_call_target="tpu_custom_call" | custom-call | tf_op jit(solution)/shard_map/count_words/pallas_call | solution.py:435
  78.0 15.1 %last_layer.1 = (bf16[48,4096]{1,0:T(8,128)(2,1)S(1)}, bf16[4096,48]{1,0:T(8,128)(2,1)S(1)}, f32[16,48]{1,0:T(8,128)S(1)}, f32[16,128]{1,0:T(8,128)S(1)}, bf16[2...) custom-call(s32[576,4096]{1,0:T(8,128)} %get-tuple-element.77.words_ref, ...), custom_call_target="tpu_custom_call" | custom-call | tf_op jit(solution)/shard_map/last_layer/pallas_call | solution.py:740
  93.1 16.9 %scatter_layer.2 = (f32[256,4608]{1,0:T(8,128)S(1)}, bf16[4,8,16,256]{3,2,1,0:T(8,128)(2,1)S(1)}, f32[512,48]{1,0:T(8,128)S(1)}) custom-call(s32[576,4096]{1,0:T(8,128)} %get-tuple-element.77.words_ref, bf16[48,4096]{1,0:T(8,128)(2,1)S(1)} %get-tuple-element.81.grad_ref, bf16[4096,48]{1,0:T(8,128)(2,1)S(1)} %get-tuple-element.82.rows_ref, ...), custom_call_target="tpu_custom_call" | custom-call | tf_op jit(solution)/shard_map/scatter_layer/pallas_call | solution.py:965
  110.0 10.2 %middle_layer.1 = (bf16[256,4096]{1,0:T(8,128)(2,1)S(1)}, bf16[4096,256]{1,0:T(8,128)(2,1)S(1)}, f32[16,256]{1,0:T(8,128)S(1)}, bf16[512,256]{1,0:T(8,128)(2,1)S(1)}, bf16[512,384]{1,0:T(8,128)(2,1)S(1)}) custom-call(f32[256,4608]{1,0:T(8,128)S(1)} %get-tuple-element.86.state_ref, f32[256,4096]{1,0:T(8,128)} %get-tuple-element.87.preact_ref, ...), custom_call_target="tpu_custom_call" | custom-call | tf_op jit(solution)/shard_map/middle_layer/pallas_call | solution.py:1073
  120.2 20.4 %scatter_layer.3 = (f32[256,4608]{1,0:T(8,128)S(1)}, bf16[4,8,16,256]{3,2,1,0:T(8,128)(2,1)S(1)}, bf16[4,16,384]{2,1,0:T(8,128)(2,1)S(1)}, f32[1,1]{1,0:T(1,128)}, f32[1,1]{1,0:T(1,128)}) custom-call(s32[576,4096]{1,0:T(8,128)} %get-tuple-element.73.words_ref, bf16[256,4096]{1,0:T(8,128)(2,1)S(1)} %get-tuple-element.92.grad_ref, ...), custom_call_target="tpu_custom_call" | custom-call | tf_op jit(solution)/shard_map/scatter_layer/pallas_call | solution.py:965
  140.6 20.5 %bottom_layer.1 = (bf16[8,64,128]{2,1,0:T(8,128)(2,1)S(1)}, f32[512,256]{1,0:T(8,128)S(1)}, f32[512,256]{1,0:T(8,128)S(1)}, f32[512,256]{1,0:T(8,128)S(1)}, f32[...) custom-call(f32[256,4608]{1,0:T(8,128)S(1)} %get-tuple-element.96.state_ref, ...), custom_call_target="tpu_custom_call" | custom-call | tf_op jit(solution)/shard_map/bottom_layer/pallas_call | solution.py:1296
  161.0 4.1 %adam.1 = (f32[200,256]{1,0:T(8,128)}, f32[200,256]{1,0:T(8,128)}, f32[200,256]{1,0:T(8,128)}, f32[512,256]{1,0:T(8,128)}, f32[512,256]{1,0:T(8,128)}, /*index=5...) custom-call(bf16[512,128]{1,0:T(8,128)(2,1)S(1)} %bitcast.27, ...), custom_call_target="tpu_custom_call" | custom-call | tf_op jit(solution)/shard_map/adam/pallas_call | solution.py:1408
Async XLA Ops:
  43.4 19.6 %copy-start = (s32[2048]{0:T(1024)S(1)}, s32[2048]{0:T(1024)}, u32[]{:S(2)}) copy-start(s32[2048]{0:T(1024)} %param.28) | copy-start | bytes 24580
  43.4 19.6 %copy-start.1 = (s32[2048]{0:T(1024)S(1)}, s32[2048]{0:T(1024)}, u32[]{:S(2)}) copy-start(s32[2048]{0:T(1024)} %param.27) | copy-start | bytes 24580
  43.5 19.6 %copy-start.2 = (s32[2048]{0:T(1024)S(1)}, s32[2048]{0:T(1024)}, u32[]{:S(2)}) copy-start(s32[2048]{0:T(1024)} %param.29) | copy-start | bytes 24580

commit v5 on v4

--- a/solution.py
+++ b/solution.py
@@ -110,7 +110,8 @@
     for ahead in range(1, along):
         place = wrapped(column + ahead, along)
         act(row * along + place, (row, place))
-    lax.fori_loop(1, across, line, 0)
+    for down in range(1, across):
+        line(down, 0)
 
 
 def greet(mesh_sizes):
@@ -325,8 +326,14 @@
 
 
 def chosen_nodes(send_row, start, count):
-    node = lax.broadcasted_iota(jnp.int32, (count, send_row.shape[1]), 0) + start
-    return jnp.where(node == send_row, 1.0, 0.0).astype(jnp.bfloat16)
+    node = (lax.broadcasted_iota(jnp.int32, (count, 128), 0) + start).astype(jnp.int16)
+    one = jnp.ones((count, 128), jnp.bfloat16)
+    pieces = []
+    for tile in range(0, send_row.shape[1], 128):
+        wanted = jnp.broadcast_to(send_row[:, tile : tile + 128], (16, 128)).astype(jnp.int16)
+        wanted = jnp.concatenate([wanted] * (count // 16))
+        pieces.append(jnp.where(node == wanted, one, jnp.zeros_like(one)))
+    return jnp.concatenate(pieces, axis=1)
 
 
 def words_kernel(mesh_sizes, kind, near_ref, *refs):

time: 169 us -> 169 us (level)
  no operation moved by 1% of the time
where the time goes in v5:
time: 169 us; the launch traced here: 168 us
  Pallas kernels  164 us (97%)
  between operations  4.25 us (3%)
    pallas_call x3, Pallas kernels, count_words(): pl.pallas_call(functools.partial(words_kernel, mesh_sizes, kind), grid=(n...  41.6 us
    pallas_call x2, Pallas kernels, scatter_layer(): pl.pallas_call(functools.partial(scatter_kernel, mesh_sizes, fanout, flip...  37.3 us
    pallas_call x2, Pallas kernels, hidden_layer(): pl.pallas_call(functools.partial(hidden_kernel, fanout, bias_start), grid...  35.4 us
    pallas_call x1, Pallas kernels, bottom_layer(): pl.pallas_call(functools.partial(bottom_kernel, mesh_sizes), grid=(nodes...  20.6 us
    pallas_call x1, Pallas kernels, last_layer(): pl.pallas_call(functools.partial(last_kernel, fanout, bias_start), grid=(...  15.1 us
    pallas_call x1, Pallas kernels, middle_layer(): pl.pallas_call(functools.partial(middle_kernel, fanout), grid=(nodes // B...  10.1 us
    pallas_call x1, Pallas kernels, adam(): pl.pallas_call(functools.partial(adam_kernel, padded), in_specs=[vmem] *...  4.12 us

profile of v5, /device:TPU:0, one launch (start us, length us, event | category | flops | bytes accessed | tf_op | source)
XLA Modules:
  0.0 168.4 jit_solution(12298707582688220008)
XLA Ops:
  0.6 16.2 %count_words.3 = (s32[576,4096]{1,0:T(8,128)S(1)}, bf16[32,16,128]{2,1,0:T(8,128)(2,1)S(1)}, s32[1,512]{1,0:T(1,128)S(1)}) custom-call(s32[15,4096]{1,0:T(8,128)} %bitcast.38, bf16[100,4096]{1,0:T(8,128)(2,1)} %bitcast.31, s32[16,32]{1,0:T(8,128)} %bitcast.43), custom_call_target="tpu_custom_call" | custom-call | tf_op jit(solution)/shard_map/count_words/pallas_call | solution.py:442
  16.9 15.7 %hidden_layer.2 = (bf16[256,4096]{1,0:T(8,128)(2,1)S(1)}, f32[256,4096]{1,0:T(8,128)}, bf16[512,256]{1,0:T(8,128)(2,1)S(1)}, bf16[112,4096]{1,0:T(8,128)(2,1)}) custom-call(s32[576,4096]{1,0:T(8,128)S(1)} %get-tuple-element.69.words_ref, bf16[100,4096]{1,0:T(8,128)(2,1)} %bitcast.32, bf16[100,4096]{1,0:T(8,128)(2,1)} %bitcast.33, ...), custom_call_target="tpu_custom_call" | custom-call | tf_op jit(solution)/shard_map/hidden_layer/pallas_call | solution.py:595
  32.5 10.6 %count_words.4 = (s32[576,4096]{1,0:T(8,128)}, bf16[32,16,256]{2,1,0:T(8,128)(2,1)S(1)}) custom-call(s32[10,4096]{1,0:T(8,128)} %bitcast.39, bf16[32,16,256]{2,1,0:T(8,128)(2,1)S(1)} %bitcast.25), custom_call_target="tpu_custom_call" | custom-call | tf_op jit(solution)/shard_map/count_words/pallas_call | solution.py:442
  43.1 0.0 copy-start
  43.1 0.0 copy-start.1
  43.2 0.0 copy-start.2
  43.2 19.7 %hidden_layer.3 = (bf16[256,4096]{1,0:T(8,128)(2,1)S(1)}, f32[256,4096]{1,0:T(8,128)}, bf16[512,256]{1,0:T(8,128)(2,1)S(1)}, bf16[256,4096]{1,0:T(8,128)(2,1)}) custom-call(s32[576,4096]{1,0:T(8,128)} %get-tuple-element.73.words_ref, bf16[256,4096]{1,0:T(8,128)(2,1)S(1)} %get-tuple-element.74.own_ref.own_block, ...), custom_call_target="tpu_custom_call" | custom-call | tf_op jit(solution)/shard_map/hidden_layer/pallas_call | solution.py:595
  62.9 0.0 copy-done
  62.9 0.0 copy-done.1
  62.9 0.0 copy-done.2
  62.9 14.8 %count_words.5 = (s32[576,4096]{1,0:T(8,128)}, bf16[32,16,256]{2,1,0:T(8,128)(2,1)S(1)}, f32[48,4096]{1,0:T(8,128)S(1)}) custom-call(s32[5,4096]{1,0:T(8,128)} %bitcast.40, bf16[32,16,256]{2,1,0:T(8,128)(2,1)S(1)} %bitcast.26, s32[1,2048]{1,0:T(1,128)S(1)} %bitcast.28, s32[1,2048]{1,0:T(1,128)S(1)} %bitcast.29, s32[1,2048]{1,0:T(1,128)S(1)} %bitcast.30), custom_call_target="tpu_custom_call" | custom-call | tf_op jit(solution)/shard_map/count_words/pallas_call | solution.py:442
  77.7 15.1 %last_layer.1 = (bf16[48,4096]{1,0:T(8,128)(2,1)S(1)}, bf16[4096,48]{1,0:T(8,128)(2,1)S(1)}, f32[16,48]{1,0:T(8,128)S(1)}, f32[16,128]{1,0:T(8,128)S(1)}, bf16[2...) custom-call(s32[576,4096]{1,0:T(8,128)} %get-tuple-element.77.words_ref, ...), custom_call_target="tpu_custom_call" | custom-call | tf_op jit(solution)/shard_map/last_layer/pallas_call | solution.py:747
  92.7 17.1 %scatter_layer.2 = (f32[256,4608]{1,0:T(8,128)S(1)}, bf16[4,8,16,256]{3,2,1,0:T(8,128)(2,1)S(1)}, f32[512,48]{1,0:T(8,128)S(1)}) custom-call(s32[576,4096]{1,0:T(8,128)} %get-tuple-element.77.words_ref, bf16[48,4096]{1,0:T(8,128)(2,1)S(1)} %get-tuple-element.81.grad_ref, bf16[4096,48]{1,0:T(8,128)(2,1)S(1)} %get-tuple-element.82.rows_ref, ...), custom_call_target="tpu_custom_call" | custom-call | tf_op jit(solution)/shard_map/scatter_layer/pallas_call | solution.py:972
  109.9 10.1 %middle_layer.1 = (bf16[256,4096]{1,0:T(8,128)(2,1)S(1)}, bf16[4096,256]{1,0:T(8,128)(2,1)S(1)}, f32[16,256]{1,0:T(8,128)S(1)}, bf16[512,256]{1,0:T(8,128)(2,1)S(1)}, bf16[512,384]{1,0:T(8,128)(2,1)S(1)}) custom-call(f32[256,4608]{1,0:T(8,128)S(1)} %get-tuple-element.86.state_ref, f32[256,4096]{1,0:T(8,128)} %get-tuple-element.87.preact_ref, ...), custom_call_target="tpu_custom_call" | custom-call | tf_op jit(solution)/shard_map/middle_layer/pallas_call | solution.py:1080
  120.0 20.2 %scatter_layer.3 = (f32[256,4608]{1,0:T(8,128)S(1)}, bf16[4,8,16,256]{3,2,1,0:T(8,128)(2,1)S(1)}, bf16[4,16,384]{2,1,0:T(8,128)(2,1)S(1)}, f32[1,1]{1,0:T(1,128)}, f32[1,1]{1,0:T(1,128)}) custom-call(s32[576,4096]{1,0:T(8,128)} %get-tuple-element.73.words_ref, bf16[256,4096]{1,0:T(8,128)(2,1)S(1)} %get-tuple-element.92.grad_ref, ...), custom_call_target="tpu_custom_call" | custom-call | tf_op jit(solution)/shard_map/scatter_layer/pallas_call | solution.py:972
  140.2 20.6 %bottom_layer.1 = (bf16[8,64,128]{2,1,0:T(8,128)(2,1)S(1)}, f32[512,256]{1,0:T(8,128)S(1)}, f32[512,256]{1,0:T(8,128)S(1)}, f32[512,256]{1,0:T(8,128)S(1)}, f32[...) custom-call(f32[256,4608]{1,0:T(8,128)S(1)} %get-tuple-element.96.state_ref, ...), custom_call_target="tpu_custom_call" | custom-call | tf_op jit(solution)/shard_map/bottom_layer/pallas_call | solution.py:1303
  160.8 4.1 %adam.1 = (f32[200,256]{1,0:T(8,128)}, f32[200,256]{1,0:T(8,128)}, f32[200,256]{1,0:T(8,128)}, f32[512,256]{1,0:T(8,128)}, f32[512,256]{1,0:T(8,128)}, /*index=5...) custom-call(bf16[512,128]{1,0:T(8,128)(2,1)S(1)} %bitcast.27, ...), custom_call_target="tpu_custom_call" | custom-call | tf_op jit(solution)/shard_map/adam/pallas_call | solution.py:1415
Async XLA Ops:
  43.1 19.7 %copy-start = (s32[2048]{0:T(1024)S(1)}, s32[2048]{0:T(1024)}, u32[]{:S(2)}) copy-start(s32[2048]{0:T(1024)} %param.28) | copy-start | bytes 24580
  43.1 19.7 %copy-start.1 = (s32[2048]{0:T(1024)S(1)}, s32[2048]{0:T(1024)}, u32[]{:S(2)}) copy-start(s32[2048]{0:T(1024)} %param.27) | copy-start | bytes 24580
  43.2 19.7 %copy-start.2 = (s32[2048]{0:T(1024)S(1)}, s32[2048]{0:T(1024)}, u32[]{:S(2)}) copy-start(s32[2048]{0:T(1024)} %param.29) | copy-start | bytes 24580

commit v6 on v5

--- a/solution.py
+++ b/solution.py
@@ -577,7 +577,7 @@
     def _():
         finish()
         total = gather_product(table_ref, words_ref, counts_ref)
-        mean_ref[...] = (total / fanout).astype(jnp.bfloat16)
+        mean_ref[...] = (total * (1.0 / fanout)).astype(jnp.bfloat16)
 
     @pl.when(step == last)
     def _():
@@ -706,7 +706,7 @@
         far_sums[...] = jnp.zeros_like(far_sums)
 
     def finish():
-        near_part = (both_ref[:classes, :] + both_ref[classes:, :]) / fanout
+        near_part = (both_ref[:classes, :] + both_ref[classes:, :]) * (1.0 / fanout)
         logits = dot(self_ref[...], own_block[...]) + near_part + bias_col[:, :1]
         top = jnp.max(logits, axis=0, keepdims=True)
         powers = jnp.exp(logits - top)
@@ -714,7 +714,7 @@
         normer = jnp.log(total) + top
         seeds = seeds_ref[...]
         uses = jnp.sum(seeds, axis=0, keepdims=True)
-        grad = (powers / total * uses - seeds).astype(jnp.bfloat16)
+        grad = (powers * (uses / total) - seeds).astype(jnp.bfloat16)
         grad_ref[...] = grad
         loss = uses * normer - jnp.sum(seeds * logits, axis=0, keepdims=True)
         notes_ref[:8, :] += jnp.sum(loss)
@@ -1000,7 +1000,7 @@
     norm = lax.rsqrt(jnp.sum(active * active, axis=0, keepdims=True) + 1e-06)
     along = jnp.sum(active * upper, axis=0, keepdims=True)
     inner = norm * upper - active * (norm * norm * norm * along)
-    return (inner * (gate * (1.0 + preact * (1.0 - gate)))).astype(jnp.bfloat16)
+    return (inner * (gate + active * (1.0 - gate))).astype(jnp.bfloat16)
 
 
 def middle_kernel(

time: 169 us -> 169 us (level)
  no operation moved by 1% of the time
where the time goes in v6:
time: 169 us; the launch traced here: 168 us
  Pallas kernels  164 us (97%)
  between operations  4.25 us (3%)
    pallas_call x3, Pallas kernels, count_words(): pl.pallas_call(functools.partial(words_kernel, mesh_sizes, kind), grid=(n...  41.6 us
    pallas_call x2, Pallas kernels, scatter_layer(): pl.pallas_call(functools.partial(scatter_kernel, mesh_sizes, fanout, flip...  37.3 us
    pallas_call x2, Pallas kernels, hidden_layer(): pl.pallas_call(functools.partial(hidden_kernel, fanout, bias_start), grid...  35.4 us
    pallas_call x1, Pallas kernels, bottom_layer(): pl.pallas_call(functools.partial(bottom_kernel, mesh_sizes), grid=(nodes...  20.6 us
    pallas_call x1, Pallas kernels, last_layer(): pl.pallas_call(functools.partial(last_kernel, fanout, bias_start), grid=(...  15.1 us
    pallas_call x1, Pallas kernels, middle_layer(): pl.pallas_call(functools.partial(middle_kernel, fanout), grid=(nodes // B...  9.96 us
    pallas_call x1, Pallas kernels, adam(): pl.pallas_call(functools.partial(adam_kernel, padded), in_specs=[vmem] *...  4.12 us

profile of v6, /device:TPU:0, one launch (start us, length us, event | category | flops | bytes accessed | tf_op | source)
XLA Modules:
  0.0 168.3 jit_solution(13658709071201330389)
XLA Ops:
  0.6 16.2 %count_words.3 = (s32[576,4096]{1,0:T(8,128)S(1)}, bf16[32,16,128]{2,1,0:T(8,128)(2,1)S(1)}, s32[1,512]{1,0:T(1,128)S(1)}) custom-call(s32[15,4096]{1,0:T(8,128)} %bitcast.38, bf16[100,4096]{1,0:T(8,128)(2,1)} %bitcast.31, s32[16,32]{1,0:T(8,128)} %bitcast.43), custom_call_target="tpu_custom_call" | custom-call | tf_op jit(solution)/shard_map/count_words/pallas_call | solution.py:442
  16.9 15.7 %hidden_layer.2 = (bf16[256,4096]{1,0:T(8,128)(2,1)S(1)}, f32[256,4096]{1,0:T(8,128)}, bf16[512,256]{1,0:T(8,128)(2,1)S(1)}, bf16[112,4096]{1,0:T(8,128)(2,1)}) custom-call(s32[576,4096]{1,0:T(8,128)S(1)} %get-tuple-element.69.words_ref, bf16[100,4096]{1,0:T(8,128)(2,1)} %bitcast.32, bf16[100,4096]{1,0:T(8,128)(2,1)} %bitcast.33, ...), custom_call_target="tpu_custom_call" | custom-call | tf_op jit(solution)/shard_map/hidden_layer/pallas_call | solution.py:595
  32.5 10.6 %count_words.4 = (s32[576,4096]{1,0:T(8,128)}, bf16[32,16,256]{2,1,0:T(8,128)(2,1)S(1)}) custom-call(s32[10,4096]{1,0:T(8,128)} %bitcast.39, bf16[32,16,256]{2,1,0:T(8,128)(2,1)S(1)} %bitcast.25), custom_call_target="tpu_custom_call" | custom-call | tf_op jit(solution)/shard_map/count_words/pallas_call | solution.py:442
  43.1 0.0 copy-start
  43.1 0.0 copy-start.1
  43.2 0.0 copy-start.2
  43.2 19.7 %hidden_layer.3 = (bf16[256,4096]{1,0:T(8,128)(2,1)S(1)}, f32[256,4096]{1,0:T(8,128)}, bf16[512,256]{1,0:T(8,128)(2,1)S(1)}, bf16[256,4096]{1,0:T(8,128)(2,1)}) custom-call(s32[576,4096]{1,0:T(8,128)} %get-tuple-element.73.words_ref, bf16[256,4096]{1,0:T(8,128)(2,1)S(1)} %get-tuple-element.74.own_ref.own_block, ...), custom_call_target="tpu_custom_call" | custom-call | tf_op jit(solution)/shard_map/hidden_layer/pallas_call | solution.py:595
  62.9 0.0 copy-done
  62.9 0.0 copy-done.1
  62.9 0.0 copy-done.2
  62.9 14.8 %count_words.5 = (s32[576,4096]{1,0:T(8,128)}, bf16[32,16,256]{2,1,0:T(8,128)(2,1)S(1)}, f32[48,4096]{1,0:T(8,128)S(1)}) custom-call(s32[5,4096]{1,0:T(8,128)} %bitcast.40, bf16[32,16,256]{2,1,0:T(8,128)(2,1)S(1)} %bitcast.26, s32[1,2048]{1,0:T(1,128)S(1)} %bitcast.28, s32[1,2048]{1,0:T(1,128)S(1)} %bitcast.29, s32[1,2048]{1,0:T(1,128)S(1)} %bitcast.30), custom_call_target="tpu_custom_call" | custom-call | tf_op jit(solution)/shard_map/count_words/pallas_call | solution.py:442
  77.7 15.1 %last_layer.1 = (bf16[48,4096]{1,0:T(8,128)(2,1)S(1)}, bf16[4096,48]{1,0:T(8,128)(2,1)S(1)}, f32[16,48]{1,0:T(8,128)S(1)}, f32[16,128]{1,0:T(8,128)S(1)}, bf16[2...) custom-call(s32[576,4096]{1,0:T(8,128)} %get-tuple-element.77.words_ref, ...), custom_call_target="tpu_custom_call" | custom-call | tf_op jit(solution)/shard_map/last_layer/pallas_call | solution.py:747
  92.8 17.1 %scatter_layer.2 = (f32[256,4608]{1,0:T(8,128)S(1)}, bf16[4,8,16,256]{3,2,1,0:T(8,128)(2,1)S(1)}, f32[512,48]{1,0:T(8,128)S(1)}) custom-call(s32[576,4096]{1,0:T(8,128)} %get-tuple-element.77.words_ref, bf16[48,4096]{1,0:T(8,128)(2,1)S(1)} %get-tuple-element.81.grad_ref, bf16[4096,48]{1,0:T(8,128)(2,1)S(1)} %get-tuple-element.82.rows_ref, ...), custom_call_target="tpu_custom_call" | custom-call | tf_op jit(solution)/shard_map/scatter_layer/pallas_call | solution.py:972
  109.9 10.0 %middle_layer.1 = (bf16[256,4096]{1,0:T(8,128)(2,1)S(1)}, bf16[4096,256]{1,0:T(8,128)(2,1)S(1)}, f32[16,256]{1,0:T(8,128)S(1)}, bf16[512,256]{1,0:T(8,128)(2,1)S(1)}, bf16[512,384]{1,0:T(8,128)(2,1)S(1)}) custom-call(f32[256,4608]{1,0:T(8,128)S(1)} %get-tuple-element.86.state_ref, f32[256,4096]{1,0:T(8,128)} %get-tuple-element.87.preact_ref, ...), custom_call_target="tpu_custom_call" | custom-call | tf_op jit(solution)/shard_map/middle_layer/pallas_call | solution.py:1080
  119.9 20.2 %scatter_layer.3 = (f32[256,4608]{1,0:T(8,128)S(1)}, bf16[4,8,16,256]{3,2,1,0:T(8,128)(2,1)S(1)}, bf16[4,16,384]{2,1,0:T(8,128)(2,1)S(1)}, f32[1,1]{1,0:T(1,128)}, f32[1,1]{1,0:T(1,128)}) custom-call(s32[576,4096]{1,0:T(8,128)} %get-tuple-element.73.words_ref, bf16[256,4096]{1,0:T(8,128)(2,1)S(1)} %get-tuple-element.92.grad_ref, ...), custom_call_target="tpu_custom_call" | custom-call | tf_op jit(solution)/shard_map/scatter_layer/pallas_call | solution.py:972
  140.0 20.6 %bottom_layer.1 = (bf16[8,64,128]{2,1,0:T(8,128)(2,1)S(1)}, f32[512,256]{1,0:T(8,128)S(1)}, f32[512,256]{1,0:T(8,128)S(1)}, f32[512,256]{1,0:T(8,128)S(1)}, f32[...) custom-call(f32[256,4608]{1,0:T(8,128)S(1)} %get-tuple-element.96.state_ref, ...), custom_call_target="tpu_custom_call" | custom-call | tf_op jit(solution)/shard_map/bottom_layer/pallas_call | solution.py:1303
  160.7 4.1 %adam.1 = (f32[200,256]{1,0:T(8,128)}, f32[200,256]{1,0:T(8,128)}, f32[200,256]{1,0:T(8,128)}, f32[512,256]{1,0:T(8,128)}, f32[512,256]{1,0:T(8,128)}, /*index=5...) custom-call(bf16[512,128]{1,0:T(8,128)(2,1)S(1)} %bitcast.27, ...), custom_call_target="tpu_custom_call" | custom-call | tf_op jit(solution)/shard_map/adam/pallas_call | solution.py:1415
Async XLA Ops:
  43.1 19.7 %copy-start = (s32[2048]{0:T(1024)S(1)}, s32[2048]{0:T(1024)}, u32[]{:S(2)}) copy-start(s32[2048]{0:T(1024)} %param.28) | copy-start | bytes 24580
  43.1 19.7 %copy-start.1 = (s32[2048]{0:T(1024)S(1)}, s32[2048]{0:T(1024)}, u32[]{:S(2)}) copy-start(s32[2048]{0:T(1024)} %param.27) | copy-start | bytes 24580
  43.2 19.7 %copy-start.2 = (s32[2048]{0:T(1024)S(1)}, s32[2048]{0:T(1024)}, u32[]{:S(2)}) copy-start(s32[2048]{0:T(1024)} %param.29) | copy-start | bytes 24580
